TPU v7x, 128 devices: a whole 4x4x4 slice. The times are simulated.
128 devices in a mesh: wide: 64 (over x, y_lo, z, core), narrow: 2 (over y_hi).
Axes of the slice: x: 4, y: 4 (y_hi: 2, y_lo: 2; y = y_hi * 2 + y_lo), z: 4, core: 2. Of those that a mesh axis runs over, the one named last changes fastest.
Arguments:
- tokens: bfloat16 [32768, 1024], P(('wide', 'narrow')), may hold values from -6 to 6
- seg_ids: int32 [32768], P(('wide', 'narrow')), may hold values from 0 to 681, never falling along the last dimension, each value on 1 to 256 neighbouring positions
- buckets: int32 [256], replicated, may hold values from 0 to 31, as said below
- cotangent: bfloat16 [32768, 1024], P(('wide', 'narrow')), may hold values from -6 to 6
- ln1_gain: bfloat16 [2, 1024], P(None, 'wide'), may hold values from 0.5 to 1.5
- ln1_bias: bfloat16 [2, 1024], P(None, 'wide'), may hold values from -2 to 2
- w_query: bfloat16 [2, 1024, 1024], P(None, 'wide'), may hold values from -0.1875 to 0.1875
- w_key: bfloat16 [2, 1024, 1024], P(None, 'wide'), may hold values from -0.1875 to 0.1875
- w_value: bfloat16 [2, 1024, 1024], P(None, 'wide'), may hold values from -0.1875 to 0.1875
- w_out: bfloat16 [2, 1024, 1024], P(None, 'wide'), may hold values from -0.75 to 0.75
- rel_table: bfloat16 [2, 512], P(None, 'wide'), may hold values from -4 to 4
- ln2_gain: bfloat16 [2, 1024], P(None, 'wide'), may hold values from 0.5 to 1.5
- ln2_bias: bfloat16 [2, 1024], P(None, 'wide'), may hold values from -2 to 2
- w_up: bfloat16 [2, 1024, 4096], P(None, 'wide'), may hold values from -0.1875 to 0.1875
- w_down: bfloat16 [2, 4096, 1024], P(None, 'wide'), may hold values from -0.09375 to 0.09375
Outputs:
- acts: bfloat16 [2, 32768, 1024], P(None, ('wide', 'narrow'))
- grad_input: float32 [32768, 1024], P(('wide', 'narrow'))
- grad_ln1_gain: float32 [2, 1024], P(None, 'wide')
- grad_ln1_bias: float32 [2, 1024], P(None, 'wide')
- grad_query: float32 [2, 1024, 1024], P(None, 'wide')
- grad_key: float32 [2, 1024, 1024], P(None, 'wide')
- grad_value: float32 [2, 1024, 1024], P(None, 'wide')
- grad_out: float32 [2, 1024, 1024], P(None, 'wide')
- grad_table: float32 [2, 512], P(None, 'wide')
- grad_ln2_gain: float32 [2, 1024], P(None, 'wide')
- grad_ln2_bias: float32 [2, 1024], P(None, 'wide')
- grad_up: float32 [2, 1024, 4096], P(None, 'wide')
- grad_down: float32 [2, 4096, 1024], P(None, 'wide')
Inputs may be any that keep to these rules, and one draw needn't show every extreme that they name: `seg_ids`: never falling along the tokens. `buckets`: equal to the distance below 16, never falling, reaching 31 at the largest distance.
All inputs are finite; a program needn't handle non-finite values.
Results may differ from a plain program's by a relative error of at most 0.02.
Values may be sent and summed in bfloat16 or wider, within the bound.
A program may use at most 256 MiB of HBM per device.

v0:
```python
import jax
import jax.numpy as jnp
from jax import lax
from jax.sharding import PartitionSpec as P

HEADS = 16
HEAD = 64
BUCKETS = 32


epsilon = 1e-05
gelu_coef = 0.7978845608028654


def normalize(stream, gain, shift):
    center = jnp.mean(stream, -1, keepdims=True)
    centered = stream - center
    spread = jnp.mean(centered * centered, -1, keepdims=True)
    inverse = lax.rsqrt(spread + epsilon)
    normed = centered * inverse
    return (normed, inverse, normed * gain.astype(jnp.float32) + shift.astype(jnp.float32))


def norm_back(grad_hidden, normed, inverse, gain):
    scaled = grad_hidden * gain.astype(jnp.float32)
    return inverse * (
        scaled
        - jnp.mean(scaled, -1, keepdims=True)
        - normed * jnp.mean(scaled * normed, -1, keepdims=True)
    )


def smooth_gelu(inputs):
    return (
        0.5 * inputs * (1.0 + jnp.tanh(gelu_coef * (inputs + 0.044715 * inputs * inputs * inputs)))
    )


def gelu_slope(inputs):
    tangent = jnp.tanh(gelu_coef * (inputs + 0.044715 * inputs * inputs * inputs))
    return 0.5 * (1.0 + tangent) + 0.5 * inputs * (1.0 - tangent * tangent) * gelu_coef * (
        1.0 + 3.0 * 0.044715 * inputs * inputs
    )


def reduce_grads(grads):
    shares = (
        lax.psum_scatter(grads[0], "wide", scatter_dimension=0, tiled=True),
        lax.psum_scatter(grads[1], "wide", scatter_dimension=0, tiled=True),
        lax.psum_scatter(grads[2], "wide", scatter_dimension=0, tiled=True),
        lax.psum_scatter(grads[3], "wide", scatter_dimension=0, tiled=True),
        lax.psum_scatter(grads[4], "wide", scatter_dimension=0, tiled=True),
        lax.psum_scatter(grads[5], "wide", scatter_dimension=0, tiled=True),
        lax.psum_scatter(grads[6], "wide", scatter_dimension=0, tiled=True),
        lax.psum_scatter(grads[7], "wide", scatter_dimension=0, tiled=True),
        lax.psum_scatter(grads[8], "wide", scatter_dimension=0, tiled=True),
        lax.psum_scatter(grads[9], "wide", scatter_dimension=0, tiled=True),
        lax.psum_scatter(grads[10], "wide", scatter_dimension=0, tiled=True),
    )
    return (
        lax.psum(shares[0].astype(jnp.bfloat16), "narrow").astype(jnp.float32),
        lax.psum(shares[1].astype(jnp.bfloat16), "narrow").astype(jnp.float32),
        lax.psum(shares[2].astype(jnp.bfloat16), "narrow").astype(jnp.float32),
        lax.psum(shares[3].astype(jnp.bfloat16), "narrow").astype(jnp.float32),
        lax.psum(shares[4].astype(jnp.bfloat16), "narrow").astype(jnp.float32),
        lax.psum(shares[5].astype(jnp.bfloat16), "narrow").astype(jnp.float32),
        lax.psum(shares[6].astype(jnp.bfloat16), "narrow").astype(jnp.float32),
        lax.psum(shares[7].astype(jnp.bfloat16), "narrow").astype(jnp.float32),
        lax.psum(shares[8].astype(jnp.bfloat16), "narrow").astype(jnp.float32),
        lax.psum(shares[9].astype(jnp.bfloat16), "narrow").astype(jnp.float32),
        lax.psum(shares[10].astype(jnp.bfloat16), "narrow").astype(jnp.float32),
    )


def on_device(
    tokens,
    seg_ids,
    buckets,
    cotangent,
    ln1_gain,
    ln1_bias,
    w_query,
    w_key,
    w_value,
    w_out,
    rel_table,
    ln2_gain,
    ln2_bias,
    w_up,
    w_down,
):
    length = tokens.shape[0]
    model_width = tokens.shape[1]
    score_scale = HEAD ** (-0.5)
    positions = jnp.arange(length, dtype=jnp.int32)
    distance = jnp.maximum(positions[:, None] - positions[None, :], 0)
    onehot = (
        buckets[distance][:, :, None] == jnp.arange(BUCKETS, dtype=jnp.int32)[None, None, :]
    ).astype(jnp.bfloat16)
    allowed = (positions[:, None] >= positions[None, :]) & (seg_ids[:, None] == seg_ids[None, :])

    def masked_scores(queries, key_rows, rel_bias):
        raw_scores = (
            jnp.einsum("ihe,jhe->hij", queries, key_rows, preferred_element_type=jnp.float32)
            * score_scale
            + rel_bias
        )
        return jnp.where(allowed[None], raw_scores, -1e30)

    def layer_backward(grad_result, saved_layer, layer_weights):
        (
            gain_one,
            shift_one,
            query_w,
            key_w,
            value_w,
            out_w,
            table,
            gain_two,
            shift_two,
            up_w,
            down_w,
        ) = layer_weights
        (
            normed_one,
            inverse_one,
            input_one,
            queries,
            key_rows,
            values,
            rel_bias,
            log_total,
            mixed,
            normed_two,
            inverse_two,
            input_two,
            upward,
            activated,
        ) = saved_layer
        down_in = grad_result.astype(jnp.bfloat16)
        grad_down = jnp.einsum("lf,ld->fd", activated, down_in, preferred_element_type=jnp.float32)
        grad_active = jnp.einsum("ld,fd->lf", down_in, down_w, preferred_element_type=jnp.float32)
        grad_upward = (grad_active * gelu_slope(upward)).astype(jnp.bfloat16)
        grad_up = jnp.einsum(
            "ld,lf->df", input_two, grad_upward, preferred_element_type=jnp.float32
        )
        grad_hidden_two = jnp.einsum(
            "lf,df->ld", grad_upward, up_w, preferred_element_type=jnp.float32
        )
        grad_gain_two = jnp.sum(grad_hidden_two * normed_two, 0)
        grad_shift_two = jnp.sum(grad_hidden_two, 0)
        grad_middle = grad_result + norm_back(grad_hidden_two, normed_two, inverse_two, gain_two)
        branch_in = grad_middle.astype(jnp.bfloat16)
        grad_out_w = jnp.einsum("ld,le->de", mixed, branch_in, preferred_element_type=jnp.float32)
        grad_mixed = jnp.einsum("le,de->ld", branch_in, out_w, preferred_element_type=jnp.float32)
        grad_mixed = grad_mixed.astype(jnp.bfloat16).reshape(length, HEADS, HEAD)
        scores = masked_scores(queries, key_rows, rel_bias)
        prob_rows = jnp.exp(scores - log_total)
        grad_probs = jnp.einsum(
            "ihe,jhe->hij", grad_mixed, values, preferred_element_type=jnp.float32
        )
        grad_values = jnp.einsum(
            "hij,ihe->jhe",
            prob_rows.astype(jnp.bfloat16),
            grad_mixed,
            preferred_element_type=jnp.float32,
        )
        grad_values = grad_values.astype(jnp.bfloat16).reshape(length, model_width)
        grad_scores = (
            prob_rows * (grad_probs - jnp.sum(prob_rows * grad_probs, -1, keepdims=True))
        ).astype(jnp.bfloat16)
        grad_queries = (
            (
                jnp.einsum(
                    "hij,jhe->ihe", grad_scores, key_rows, preferred_element_type=jnp.float32
                )
                * score_scale
            )
            .astype(jnp.bfloat16)
            .reshape(length, model_width)
        )
        grad_keys = (
            (
                jnp.einsum("hij,ihe->jhe", grad_scores, queries, preferred_element_type=jnp.float32)
                * score_scale
            )
            .astype(jnp.bfloat16)
            .reshape(length, model_width)
        )
        grad_bias_table = jnp.einsum(
            "hij,ijb->bh", grad_scores, onehot, preferred_element_type=jnp.float32
        ).reshape(BUCKETS * HEADS)
        grad_query_w = jnp.einsum(
            "ld,le->de", input_one, grad_queries, preferred_element_type=jnp.float32
        )
        grad_key_w = jnp.einsum(
            "ld,le->de", input_one, grad_keys, preferred_element_type=jnp.float32
        )
        grad_value_w = jnp.einsum(
            "ld,le->de", input_one, grad_values, preferred_element_type=jnp.float32
        )
        grad_hidden_one = jnp.einsum(
            "le,de->ld", grad_queries, query_w, preferred_element_type=jnp.float32
        )
        grad_hidden_one = grad_hidden_one + jnp.einsum(
            "le,de->ld", grad_keys, key_w, preferred_element_type=jnp.float32
        )
        grad_hidden_one = grad_hidden_one + jnp.einsum(
            "le,de->ld", grad_values, value_w, preferred_element_type=jnp.float32
        )
        grad_gain_one = jnp.sum(grad_hidden_one * normed_one, 0)
        grad_shift_one = jnp.sum(grad_hidden_one, 0)
        grad_stream = grad_middle + norm_back(grad_hidden_one, normed_one, inverse_one, gain_one)
        grads = (
            grad_gain_one,
            grad_shift_one,
            grad_query_w,
            grad_key_w,
            grad_value_w,
            grad_out_w,
            grad_bias_table,
            grad_gain_two,
            grad_shift_two,
            grad_up,
            grad_down,
        )
        return (grad_stream, grads)

    stream = tokens.astype(jnp.float32)
    saved_all = []
    fetched_all = []
    layer_acts = []
    for layer_at in range(2):
        layer_weights = (
            lax.all_gather(ln1_gain[layer_at], "wide", axis=0, tiled=True),
            lax.all_gather(ln1_bias[layer_at], "wide", axis=0, tiled=True),
            lax.all_gather(w_query[layer_at], "wide", axis=0, tiled=True),
            lax.all_gather(w_key[layer_at], "wide", axis=0, tiled=True),
            lax.all_gather(w_value[layer_at], "wide", axis=0, tiled=True),
            lax.all_gather(w_out[layer_at], "wide", axis=0, tiled=True),
            lax.all_gather(rel_table[layer_at], "wide", axis=0, tiled=True),
            lax.all_gather(ln2_gain[layer_at], "wide", axis=0, tiled=True),
            lax.all_gather(ln2_bias[layer_at], "wide", axis=0, tiled=True),
            lax.all_gather(w_up[layer_at], "wide", axis=0, tiled=True),
            lax.all_gather(w_down[layer_at], "wide", axis=0, tiled=True),
        )
        (
            layer_gain_one,
            layer_shift_one,
            layer_query_w,
            layer_key_w,
            layer_value_w,
            layer_out_w,
            layer_table,
            layer_gain_two,
            layer_shift_two,
            layer_up_w,
            layer_down_w,
        ) = layer_weights
        layer_normed_one, layer_inverse_one, hidden_one = normalize(
            stream, layer_gain_one, layer_shift_one
        )
        layer_input_one = hidden_one.astype(jnp.bfloat16)
        layer_queries = (
            jnp.dot(layer_input_one, layer_query_w, preferred_element_type=jnp.float32)
            .astype(jnp.bfloat16)
            .reshape(length, HEADS, HEAD)
        )
        layer_key_rows = (
            jnp.dot(layer_input_one, layer_key_w, preferred_element_type=jnp.float32)
            .astype(jnp.bfloat16)
            .reshape(length, HEADS, HEAD)
        )
        layer_values = (
            jnp.dot(layer_input_one, layer_value_w, preferred_element_type=jnp.float32)
            .astype(jnp.bfloat16)
            .reshape(length, HEADS, HEAD)
        )
        layer_rel_bias = jnp.einsum(
            "ijb,bh->hij",
            onehot,
            layer_table.reshape(BUCKETS, HEADS),
            preferred_element_type=jnp.float32,
        )
        layer_scores = masked_scores(layer_queries, layer_key_rows, layer_rel_bias)
        row_peak = jnp.max(layer_scores, -1, keepdims=True)
        exp_terms = jnp.exp(layer_scores - row_peak)
        totals = jnp.sum(exp_terms, -1, keepdims=True)
        layer_prob_rows = exp_terms / totals
        layer_log_total = row_peak + jnp.log(totals)
        layer_mixed = jnp.einsum(
            "hij,jhe->ihe",
            layer_prob_rows.astype(jnp.bfloat16),
            layer_values,
            preferred_element_type=jnp.float32,
        )
        layer_mixed = layer_mixed.reshape(length, model_width).astype(jnp.bfloat16)
        middle = stream + jnp.dot(layer_mixed, layer_out_w, preferred_element_type=jnp.float32)
        layer_normed_two, layer_inverse_two, hidden_two = normalize(
            middle, layer_gain_two, layer_shift_two
        )
        layer_input_two = hidden_two.astype(jnp.bfloat16)
        layer_upward = jnp.dot(layer_input_two, layer_up_w, preferred_element_type=jnp.float32)
        layer_activated = smooth_gelu(layer_upward).astype(jnp.bfloat16)
        result = middle + jnp.dot(layer_activated, layer_down_w, preferred_element_type=jnp.float32)
        layer_saved_layer = (
            layer_normed_one,
            layer_inverse_one,
            layer_input_one,
            layer_queries,
            layer_key_rows,
            layer_values,
            layer_rel_bias,
            layer_log_total,
            layer_mixed,
            layer_normed_two,
            layer_inverse_two,
            layer_input_two,
            layer_upward,
            layer_activated,
        )
        stream = result
        saved_layer = layer_saved_layer
        saved_all.append(saved_layer)
        fetched_all.append(layer_weights)
        layer_acts.append(stream.astype(jnp.bfloat16))
    grad_stream = cotangent.astype(jnp.float32)
    reduced = [None, None]
    for layer_at in (1, 0):
        layer_weights = (
            lax.all_gather(ln1_gain[layer_at], "wide", axis=0, tiled=True),
            lax.all_gather(ln1_bias[layer_at], "wide", axis=0, tiled=True),
            lax.all_gather(w_query[layer_at], "wide", axis=0, tiled=True),
            lax.all_gather(w_key[layer_at], "wide", axis=0, tiled=True),
            lax.all_gather(w_value[layer_at], "wide", axis=0, tiled=True),
            lax.all_gather(w_out[layer_at], "wide", axis=0, tiled=True),
            lax.all_gather(rel_table[layer_at], "wide", axis=0, tiled=True),
            lax.all_gather(ln2_gain[layer_at], "wide", axis=0, tiled=True),
            lax.all_gather(ln2_bias[layer_at], "wide", axis=0, tiled=True),
            lax.all_gather(w_up[layer_at], "wide", axis=0, tiled=True),
            lax.all_gather(w_down[layer_at], "wide", axis=0, tiled=True),
        )
        grad_stream, grads = layer_backward(grad_stream, saved_all[layer_at], layer_weights)
        reduced[layer_at] = reduce_grads(grads)
    stacked = tuple((jnp.stack([reduced[0][index], reduced[1][index]]) for index in range(11)))
    return (jnp.stack(layer_acts), grad_stream) + stacked


def solution(mesh):
    placed = (
        P(("wide", "narrow"), None),
        P(("wide", "narrow")),
        P(),
        P(("wide", "narrow"), None),
        P(None, "wide"),
        P(None, "wide"),
        P(None, "wide", None),
        P(None, "wide", None),
        P(None, "wide", None),
        P(None, "wide", None),
        P(None, "wide"),
        P(None, "wide"),
        P(None, "wide"),
        P(None, "wide", None),
        P(None, "wide", None),
    )
    return jax.shard_map(
        on_device,
        mesh=mesh,
        in_specs=placed,
        out_specs=(
            P(None, ("wide", "narrow"), None),
            P(("wide", "narrow"), None),
            P(None, "wide"),
            P(None, "wide"),
            P(None, "wide", None),
            P(None, "wide", None),
            P(None, "wide", None),
            P(None, "wide", None),
            P(None, "wide"),
            P(None, "wide"),
            P(None, "wide"),
            P(None, "wide", None),
            P(None, "wide", None),
        ),
        check_vma=False,
    )
```

profile of v0, /device:TPU:0, one launch (start us, length us, event | category | flops | bytes accessed | tf_op | source)
XLA Modules:
  0.0 4954.2 jit_solution(9190431298836450080)
XLA Ops:
  29.3 281.9 %all-reduce.21 = (bf16[1024]{0:T(1024)(128)(2,1)S(1)}, bf16[1024]{0:T(1024)(128)(2,1)S(1)}, bf16[512]{0:T(512)(128)(2,1)S(1)}, bf16[1024]{0:T(1024)(128)(2,1)S(1...) all-reduce(bf16[1024]{0:T(1024)(128)(2,1)S(1)} %dynamic-update-slic, ...), channel_id=3, replica_groups=mesh['wide'=64,'narrow'=2] {'wide'}, use_global_device_ids=true, to_apply=%add.1 | all-reduce | flops 9216 | bytes 36864
  311.6 408.0 %gather_fusion = s32[65536]{0:T(1024)S(1)} fusion(s32[256]{0:T(256)S(1)} %copy-done, s32[65536]{0:T(1024)S(1)} %broadcast_clamp_fusion), kind=kCustom, calls=%fused_computation | custom fusion | bytes 786432 | tf_op jit(solution)/shard_map/gather | solution.py:98
  719.7 3.6 fusion.18
  723.3 5.3 copy.90
  728.6 3.5 fusion.19
  732.1 5.5 copy.84
  746.5 3.4 fusion.212
  755.7 8.0 fusion.14
  763.7 7.5 fusion.214
  774.5 87.5 %all-gather.49.cloned.1.call-done = bf16[1,1024,1024]{2,1,0:T(8,128)(2,1)} async-done(((bf16[1,16,1024]{2,1,0:T(8,128)(2,1)}), bf16[1,1024,1024]{2,1,0:T(8,128)(2,1)}) %all-gather.49.cloned.1.call-update) | async-done | bytes 2097168 | tf_op jit(solution)/shard_map/all_gather | solution.py:237
  864.8 101.9 %all-gather.47.cloned.1.call-done = bf16[1,1024,1024]{2,1,0:T(8,128)(2,1)} async-done(((bf16[1,16,1024]{2,1,0:T(8,128)(2,1)}), bf16[1,1024,1024]{2,1,0:T(8,128)(2,1)}) %all-gather.47.cloned.1.call-update) | async-done | bytes 2097168 | tf_op jit(solution)/shard_map/all_gather | solution.py:239
  969.2 3.4 fusion.215
  975.6 95.0 %all-gather.53.cloned.1.call-done = bf16[1,1024,1024]{2,1,0:T(8,128)(2,1)} async-done(((bf16[1,16,1024]{2,1,0:T(8,128)(2,1)}), bf16[1,1024,1024]{2,1,0:T(8,128)(2,1)}) %all-gather.53.cloned.1.call-update) | async-done | bytes 2097168 | tf_op jit(solution)/shard_map/all_gather | solution.py:240
  1073.3 110.3 %all-gather.55.cloned.1.call-done = bf16[1,1024,4096]{2,1,0:T(8,128)(2,1)} async-done(((bf16[1,16,4096]{2,1,0:T(8,128)(2,1)}), bf16[1,1024,4096]{2,1,0:T(8,128)(2,1)}) %all-gather.55.cloned.1.call-update) | async-done | bytes 8388624 | tf_op jit(solution)/shard_map/all_gather | solution.py:244
  1183.6 7.9 fusion.6
  1191.5 104.3 %all-gather.57.cloned.1.call-done = bf16[1,4096,1024]{2,1,0:T(8,128)(2,1)} async-done(((bf16[1,64,1024]{2,1,0:T(8,128)(2,1)}), bf16[1,4096,1024]{2,1,0:T(8,128)(2,1)}) %all-gather.57.cloned.1.call-update) | async-done | bytes 8388624 | tf_op jit(solution)/shard_map/all_gather | solution.py:245
  1295.8 11.5 fusion.26
  1313.3 3.2 fusion.143
  1317.8 3.5 multiply_reduce_fusion.1
  1329.8 7.9 fusion.29
  1344.7 3.5 fusion.131
  1349.5 3.0 fusion.119
  1356.3 3.6 multiply_reduce_fusion
  1363.6 2.9 fusion.200
  1370.0 3.0 fusion.198
  1373.0 3.7 fusion.219
  1376.8 3.8 fusion.217
  1380.7 3.9 fusion.218
  1385.9 3.1 copy.102
  1389.0 4.6 copy.100
  1405.0 277.5 %all-reduce.20 = (bf16[1024]{0:T(1024)(128)(2,1)S(1)}, bf16[1024]{0:T(1024)(128)(2,1)S(1)}, bf16[1024]{0:T(1024)(128)(2,1)S(1)}, bf16[1024]{0:T(1024)(128)(2,1)S...) all-reduce(f32[1024]{0:T(1024)S(1)} %get-tuple-element.17, ...), channel_id=25, replica_groups=mesh['wide'=64,'narrow'=2] {'wide'}, use_global_device_ids=true, to_apply=%region_26.27.clone | all-reduce | flops 9216 | bytes 55296
  1690.0 201.7 %reduce-scatter.25.cloned.1.call-done = f32[16,1024]{1,0:T(8,128)} async-done(((f32[1024,1024]{1,0:T(8,128)}), f32[16,1024]{1,0:T(8,128)}) %reduce-scatter.25.cloned.1.call-update) | async-done | bytes 65552 | tf_op jit(solution)/shard_map/reduce_scatter | solution.py:53
  1893.1 287.4 %reduce-scatter.21.cloned.1.call-done = f32[16,1024]{1,0:T(8,128)} async-done(((f32[1024,1024]{1,0:T(8,128)}), f32[16,1024]{1,0:T(8,128)}) %reduce-scatter.21.cloned.1.call-update) | async-done | bytes 65552 | tf_op jit(solution)/shard_map/reduce_scatter | solution.py:52
  2182.0 287.5 %reduce-scatter.13.cloned.1.call-done = f32[16,1024]{1,0:T(8,128)} async-done(((f32[1024,1024]{1,0:T(8,128)}), f32[16,1024]{1,0:T(8,128)}) %reduce-scatter.13.cloned.1.call-update) | async-done | bytes 65552 | tf_op jit(solution)/shard_map/reduce_scatter | solution.py:50
  2471.0 287.4 %reduce-scatter.17.cloned.1.call-done = f32[16,1024]{1,0:T(8,128)} async-done(((f32[1024,1024]{1,0:T(8,128)}), f32[16,1024]{1,0:T(8,128)}) %reduce-scatter.17.cloned.1.call-update) | async-done | bytes 65552 | tf_op jit(solution)/shard_map/reduce_scatter | solution.py:51
  2759.8 287.5 %reduce-scatter.23.cloned.1.call-done = f32[16,1024]{1,0:T(8,128)} async-done(((f32[1024,1024]{1,0:T(8,128)}), f32[16,1024]{1,0:T(8,128)}) %reduce-scatter.23.cloned.1.call-update) | async-done | bytes 65552 | tf_op jit(solution)/shard_map/reduce_scatter | solution.py:52
  3048.8 287.5 %reduce-scatter.15.cloned.1.call-done = f32[16,1024]{1,0:T(8,128)} async-done(((f32[1024,1024]{1,0:T(8,128)}), f32[16,1024]{1,0:T(8,128)}) %reduce-scatter.15.cloned.1.call-update) | async-done | bytes 65552 | tf_op jit(solution)/shard_map/reduce_scatter | solution.py:50
  3337.7 287.5 %reduce-scatter.19.cloned.1.call-done = f32[16,1024]{1,0:T(8,128)} async-done(((f32[1024,1024]{1,0:T(8,128)}), f32[16,1024]{1,0:T(8,128)}) %reduce-scatter.19.cloned.1.call-update) | async-done | bytes 65552 | tf_op jit(solution)/shard_map/reduce_scatter | solution.py:51
  3627.1 10.8 fusion.174
  3638.9 10.8 fusion.195
  3651.0 9.9 fusion.193
  3662.1 9.9 fusion.194
  3672.4 7.5 fusion.158
  3687.3 287.9 %reduce-scatter.33.cloned.1.call-done = f32[64,1024]{1,0:T(8,128)} async-done(((f32[4096,1024]{1,0:T(8,128)}), f32[64,1024]{1,0:T(8,128)}) %reduce-scatter.33.cloned.1.call-update) | async-done | bytes 262160 | tf_op jit(solution)/shard_map/reduce_scatter | solution.py:58
  3976.8 309.1 %reduce-scatter.35.cloned.1.call-done = f32[64,1024]{1,0:T(8,128)} async-done(((f32[4096,1024]{1,0:T(8,128)}), f32[64,1024]{1,0:T(8,128)}) %reduce-scatter.35.cloned.1.call-update) | async-done | bytes 262160 | tf_op jit(solution)/shard_map/reduce_scatter | solution.py:58
  4287.5 308.9 %reduce-scatter.29.cloned.1.call-done = f32[16,4096]{1,0:T(8,128)} async-done(((f32[1024,4096]{1,0:T(8,128)}), f32[16,4096]{1,0:T(8,128)}) %reduce-scatter.29.cloned.1.call-update) | async-done | bytes 262160 | tf_op jit(solution)/shard_map/reduce_scatter | solution.py:57
  4598.0 309.1 %reduce-scatter.31.cloned.1.call-done = f32[16,4096]{1,0:T(8,128)} async-done(((f32[1024,4096]{1,0:T(8,128)}), f32[16,4096]{1,0:T(8,128)}) %reduce-scatter.31.cloned.1.call-update) | async-done | bytes 262160 | tf_op jit(solution)/shard_map/reduce_scatter | solution.py:57
  4915.7 27.9 all-reduce.29.cloned.1.call-done
  (366 shorter events, 141.9 us)
Async XLA Ops:
  7.2 304.4 %copy-start = (s32[256]{0:T(256)S(1)}, s32[256]{0:T(256)}, u32[]{:S(2)}) copy-start(s32[256]{0:T(256)} %param.17) | copy-start | bytes 3076
  7.2 731.1 %all-gather.35.cloned.1.call-start = ((), (), s32[]{:S(2)}) async-start(), calls=%async_computation.24 | async-start | bytes 2129920 | tf_op jit(solution)/shard_map/all_gather | solution.py:239
  8.7 732.2 %all-gather.39.cloned.1.call-start = ((), (), s32[]{:S(2)}) async-start(), calls=%async_computation.26 | async-start | bytes 2129920 | tf_op jit(solution)/shard_map/all_gather | solution.py:238
  10.1 733.5 %all-gather.37.cloned.1.call-start = ((), (), s32[]{:S(2)}) async-start(), calls=%async_computation.25 | async-start | bytes 2129920 | tf_op jit(solution)/shard_map/all_gather | solution.py:237
  11.6 741.1 %all-gather.41.cloned.1.call-start = ((), (), s32[]{:S(2)}) async-start(), calls=%async_computation.27 | async-start | bytes 2129920 | tf_op jit(solution)/shard_map/all_gather | solution.py:240
  13.1 742.6 %all-gather.43.cloned.1.call-start = ((), (), s32[]{:S(2)}) async-start(), calls=%async_computation.28 | async-start | bytes 8519680 | tf_op jit(solution)/shard_map/all_gather | solution.py:244
  14.9 748.8 %all-gather.45.cloned.1.call-start = ((), (), s32[]{:S(2)}) async-start(), calls=%async_computation.29 | async-start | bytes 8519680 | tf_op jit(solution)/shard_map/all_gather | solution.py:245
  16.6 755.2 %all-gather.51.cloned.1.call-start = ((), (), s32[]{:S(2)}) async-start(), calls=%async_computation.32 | async-start | bytes 2129920 | tf_op jit(solution)/shard_map/all_gather | solution.py:238
  17.4 844.6 %all-gather.49.cloned.1.call-start = ((), (), s32[]{:S(2)}) async-start(), calls=%async_computation.31 | async-start | bytes 2129920 | tf_op jit(solution)/shard_map/all_gather | solution.py:237
  18.1 948.5 %all-gather.47.cloned.1.call-start = ((), (), s32[]{:S(2)}) async-start(), calls=%async_computation.30 | async-start | bytes 2129920 | tf_op jit(solution)/shard_map/all_gather | solution.py:239
  18.9 1051.7 %all-gather.53.cloned.1.call-start = ((), (), s32[]{:S(2)}) async-start(), calls=%async_computation.33 | async-start | bytes 2129920 | tf_op jit(solution)/shard_map/all_gather | solution.py:240
  19.4 1164.1 %all-gather.55.cloned.1.call-start = ((), (), s32[]{:S(2)}) async-start(), calls=%async_computation.34 | async-start | bytes 8519680 | tf_op jit(solution)/shard_map/all_gather | solution.py:244
  20.2 1275.6 %all-gather.57.cloned.1.call-start = ((), (), s32[]{:S(2)}) async-start(), calls=%async_computation.35 | async-start | bytes 8519680 | tf_op jit(solution)/shard_map/all_gather | solution.py:245
  20.8 1667.7 %reduce-scatter.27.cloned.1.call-start = ((), (), s32[]{:S(2)}) async-start(), calls=%async_computation.19 | async-start | bytes 4259840 | tf_op jit(solution)/shard_map/reduce_scatter | solution.py:53
  737.8 665.1 %copy-start.60 = (f32[256]{0:T(256)}, f32[256]{0:T(256)S(1)}, u32[]{:S(2)}) copy-start(f32[256]{0:T(256)S(1)} %broadcast_multiply_fusion.11) | copy-start | bytes 3076
  740.9 9.6 copy-start.46
  752.7 10.9 copy-start.53
  771.2 93.1 %copy-start.66 = (f32[256]{0:T(256)}, f32[256]{0:T(256)S(1)}, u32[]{:S(2)}) copy-start(f32[256]{0:T(256)S(1)} %broadcast_multiply_fusion.9) | copy-start | bytes 3076
  771.5 92.8 %copy-start.70 = (f32[256]{0:T(256)}, f32[256]{0:T(256)S(1)}, u32[]{:S(2)}) copy-start(f32[256]{0:T(256)S(1)} %add_rsqrt_fusion.1) | copy-start | bytes 3076
  771.8 194.9 %copy-start.20 = (bf16[256,1024]{1,0:T(8,128)(2,1)}, bf16[256,1024]{1,0:T(8,128)(2,1)S(1)}, u32[]{:S(2)}) copy-start(bf16[256,1024]{1,0:T(8,128)(2,1)S(1)} %add_convert_fusion.1) | copy-start | bytes 1572868
  774.5 194.7 %copy-start.35 = (bf16[256,1024]{0,1:T(8,128)(2,1)}, bf16[256,1024]{0,1:T(8,128)(2,1)S(1)}, u32[]{:S(2)}) copy-start(bf16[256,1024]{0,1:T(8,128)(2,1)S(1)} %copy.88) | copy-start | bytes 1572868
  864.8 107.8 %copy-start.37 = (bf16[256,1024]{0,1:T(8,128)(2,1)}, bf16[256,1024]{0,1:T(8,128)(2,1)S(1)}, u32[]{:S(2)}) copy-start(bf16[256,1024]{0,1:T(8,128)(2,1)S(1)} %copy.87) | copy-start | bytes 1572868
  975.5 97.7 %copy-start.55 = (bf16[16,64,256]{2,1,0:T(8,128)(2,1)}, bf16[16,64,256]{2,1,0:T(8,128)(2,1)S(1)}, u32[]{:S(2)}) copy-start(bf16[16,64,256]{2,1,0:T(8,128)(2,1)S(1)} %fusion.150) | copy-start | bytes 1572868
  1073.0 237.1 %copy-start.9 = (f32[256,1024]{1,0:T(8,128)}, f32[256,1024]{1,0:T(8,128)S(1)}, u32[]{:S(2)}) copy-start(f32[256,1024]{1,0:T(8,128)S(1)} %get-tuple-element.106) | copy-start | bytes 3145732
  1073.3 222.5 %copy-start.40 = (bf16[256,1024]{1,0:T(8,128)(2,1)S(1)}, bf16[256,1024]{1,0:T(8,128)(2,1)}, u32[]{:S(2)}) copy-start(bf16[256,1024]{1,0:T(8,128)(2,1)} %param.18) | copy-start | bytes 1572868
  1295.8 11.5 copy-start.73
  1313.3 578.4 %reduce-scatter.25.cloned.1.call-start = ((), (), s32[]{:S(2)}) async-start(), calls=%async_computation.18 | async-start | bytes 4259840 | tf_op jit(solution)/shard_map/reduce_scatter | solution.py:53
  1328.5 9.2 slice-start
  1329.7 10.8 copy-start.18
  1344.6 835.9 %reduce-scatter.21.cloned.1.call-start = ((), (), s32[]{:S(2)}) async-start(), calls=%async_computation.16 | async-start | bytes 4259840 | tf_op jit(solution)/shard_map/reduce_scatter | solution.py:52
  1344.7 8.6 copy-start.8
  1344.7 8.6 copy-start.65
  1356.2 1113.3 %reduce-scatter.13.cloned.1.call-start = ((), (), s32[]{:S(2)}) async-start(), calls=%async_computation.12 | async-start | bytes 4259840 | tf_op jit(solution)/shard_map/reduce_scatter | solution.py:50
  1366.5 1391.8 %reduce-scatter.17.cloned.1.call-start = ((), (), s32[]{:S(2)}) async-start(), calls=%async_computation.14 | async-start | bytes 4259840 | tf_op jit(solution)/shard_map/reduce_scatter | solution.py:51
  1372.9 1674.4 %reduce-scatter.23.cloned.1.call-start = ((), (), s32[]{:S(2)}) async-start(), calls=%async_computation.17 | async-start | bytes 4259840 | tf_op jit(solution)/shard_map/reduce_scatter | solution.py:52
  1376.8 1959.5 %reduce-scatter.15.cloned.1.call-start = ((), (), s32[]{:S(2)}) async-start(), calls=%async_computation.13 | async-start | bytes 4259840 | tf_op jit(solution)/shard_map/reduce_scatter | solution.py:50
  1380.6 2244.6 %reduce-scatter.19.cloned.1.call-start = ((), (), s32[]{:S(2)}) async-start(), calls=%async_computation.15 | async-start | bytes 4259840 | tf_op jit(solution)/shard_map/reduce_scatter | solution.py:51
  1384.6 2297.8 %all-reduce.27.cloned.1.call-start = ((), (), s32[]{:S(2)}) async-start(), calls=%async_computation.36 | async-start | bytes 534528 | tf_op jit(solution)/shard_map/psum | solution.py:61
  1402.9 2224.1 %copy-start.19 = (f32[256,1024]{1,0:T(8,128)S(1)}, f32[256,1024]{1,0:T(8,128)}, u32[]{:S(2)}) copy-start(f32[256,1024]{1,0:T(8,128)} %copy-done.18) | copy-start | bytes 3145732
  3626.8 348.4 %reduce-scatter.33.cloned.1.call-start = ((), (), s32[]{:S(2)}) async-start(), calls=%async_computation.22 | async-start | bytes 17039360 | tf_op jit(solution)/shard_map/reduce_scatter | solution.py:58
  3637.9 648.0 %reduce-scatter.35.cloned.1.call-start = ((), (), s32[]{:S(2)}) async-start(), calls=%async_computation.23 | async-start | bytes 17039360 | tf_op jit(solution)/shard_map/reduce_scatter | solution.py:58
  3649.7 946.7 %reduce-scatter.29.cloned.1.call-start = ((), (), s32[]{:S(2)}) async-start(), calls=%async_computation.20 | async-start | bytes 17039360 | tf_op jit(solution)/shard_map/reduce_scatter | solution.py:57
  3660.9 1246.2 %reduce-scatter.31.cloned.1.call-start = ((), (), s32[]{:S(2)}) async-start(), calls=%async_computation.21 | async-start | bytes 17039360 | tf_op jit(solution)/shard_map/reduce_scatter | solution.py:57
  3672.0 9.0 copy-start.15
  3672.0 9.0 copy-start.61
  3672.0 1271.6 %all-reduce.29.cloned.1.call-start = ((), (), s32[]{:S(2)}) async-start(), calls=%async_computation.37 | async-start | bytes 1048576 | tf_op jit(solution)/shard_map/psum | solution.py:70
  3672.4 8.6 copy-start.59
  3679.9 1267.3 %copy-start.1 = (s32[256]{0:T(256)S(1)}, s32[256]{0:T(256)}, u32[]{:S(2)}) copy-start(s32[256]{0:T(256)} %param.17) | copy-start | bytes 3076
  (55 other events, 190.2 us)
Sparse Core Ops, SparseCore 0:
  10.3 105.8 all-gather.34
  117.9 102.2 all-gather.38
  222.5 102.2 all-gather.36
  326.4 102.2 all-gather.40
  430.9 110.6 all-gather.42
  543.7 109.8 all-gather.44
  655.3 101.9 all-gather.50
  759.7 102.2 all-gather.48
  864.3 102.3 all-gather.46
  968.2 102.3 all-gather.52
  1072.9 110.6 all-gather.54
  1185.7 110.0 all-gather.56
  1313.4 289.2 reduce-scatter.26
  1605.0 286.5 reduce-scatter.24
  1893.9 286.5 reduce-scatter.20
  2182.9 286.5 reduce-scatter.12
  2471.7 286.5 reduce-scatter.16
  2760.7 286.5 reduce-scatter.22
  3049.7 286.5 reduce-scatter.14
  3338.6 286.5 reduce-scatter.18
  3630.1 30.8 all-reduce.26
  3663.6 311.5 reduce-scatter.32
  3977.7 308.1 reduce-scatter.34
  4288.3 308.1 reduce-scatter.28
  4598.9 308.1 reduce-scatter.30
  4910.4 33.2 all-reduce.28
where the time goes:
time: 4960 us; the launch traced here: 4950 us
  waiting for transfers between devices  3670 us (74%)
  blocking collectives  559 us (11%)
  local copies, waits for them, and re-layouts  466 us (9%)
  matrix products  193 us (4%)
    reduce_scatter x2, waiting for transfers between devices, reduce_grads(): lax.psum_scatter(grads[9], 'wide', scatter_dimension=0, tiled=True)  618 us
    reduce_scatter x2, waiting for transfers between devices, reduce_grads(): lax.psum_scatter(grads[10], 'wide', scatter_dimension=0, tiled=True)  597 us
    reduce_scatter x2, waiting for transfers between devices, reduce_grads(): lax.psum_scatter(grads[2], 'wide', scatter_dimension=0, tiled=True)  575 us
    reduce_scatter x2, waiting for transfers between devices, reduce_grads(): lax.psum_scatter(grads[4], 'wide', scatter_dimension=0, tiled=True)  575 us
    reduce_scatter x2, waiting for transfers between devices, reduce_grads(): lax.psum_scatter(grads[3], 'wide', scatter_dimension=0, tiled=True)  575 us
    unnamed x2, blocking collectives  559 us
    gather x2, local copies, waits for them, and re-layouts, on_device(): buckets[distance][:, :, None]  408 us
    reduce_scatter x2, waiting for transfers between devices, reduce_grads(): lax.psum_scatter(grads[5], 'wide', scatter_dimension=0, tiled=True)  202 us
  transfers between devices with their start and end apart: 26, of which 17 were waited for; matrix products, arithmetic and copies ran while one was open for 13% of the time, Pallas kernels for 0%

commit v1 on v0

--- a/solution.py
+++ b/solution.py
@@ -1,12 +1,15 @@
+import functools
+
 import jax
 import jax.numpy as jnp
 from jax import lax
+from jax.experimental import pallas as pl
+from jax.experimental.pallas import tpu as pltpu
 from jax.sharding import PartitionSpec as P
 
 HEADS = 16
 HEAD = 64
 BUCKETS = 32
-
 
 epsilon = 1e-05
 gelu_coef = 0.7978845608028654
@@ -43,33 +46,437 @@
     )
 
 
-def reduce_grads(grads):
-    shares = (
-        lax.psum_scatter(grads[0], "wide", scatter_dimension=0, tiled=True),
-        lax.psum_scatter(grads[1], "wide", scatter_dimension=0, tiled=True),
-        lax.psum_scatter(grads[2], "wide", scatter_dimension=0, tiled=True),
-        lax.psum_scatter(grads[3], "wide", scatter_dimension=0, tiled=True),
-        lax.psum_scatter(grads[4], "wide", scatter_dimension=0, tiled=True),
-        lax.psum_scatter(grads[5], "wide", scatter_dimension=0, tiled=True),
-        lax.psum_scatter(grads[6], "wide", scatter_dimension=0, tiled=True),
-        lax.psum_scatter(grads[7], "wide", scatter_dimension=0, tiled=True),
-        lax.psum_scatter(grads[8], "wide", scatter_dimension=0, tiled=True),
-        lax.psum_scatter(grads[9], "wide", scatter_dimension=0, tiled=True),
-        lax.psum_scatter(grads[10], "wide", scatter_dimension=0, tiled=True),
+MESH = pl.DeviceIdType.MESH
+TILE = 128
+BF = jnp.bfloat16
+F32 = jnp.float32
+ORDERS = (("y", "x", "z"), ("z", "y", "x"), ("x", "z", "y"))
+CHAINS = (
+    ((0, 0, 10, 0), (0, 10, 10, 1), (0, 20, 12, 2), (3, 0, 2, 0)),
+    ((1, 0, 10, 0), (1, 10, 10, 1), (1, 20, 12, 2)),
+    ((2, 0, 3, 0), (2, 3, 3, 1), (2, 6, 2, 2)),
+)
+
+
+def place():
+    wide, narrow = lax.axis_index("wide"), lax.axis_index("narrow")
+    return {
+        "x": wide // 16,
+        "y": narrow * 2 + (wide // 8) % 2,
+        "z": (wide // 2) % 4,
+        "c": wide % 2,
+    }
+
+
+def device(at):
+    return (((at["x"] * 2 + at["y"] % 2) * 4 + at["z"]) * 2 + at["c"], at["y"] // 2)
+
+
+def moved(at, axis, by):
+    new = dict(at)
+    new[axis] = (at[axis] + by) % (2 if axis == "c" else 4)
+    return new
+
+
+def pick(ref, chain, sel, lead=()):
+    array, tile, tiles, _ = chain
+    y = sel["y"]
+    columns = pl.ds(tile * TILE, tiles * TILE)
+    rows = pl.ds(0, 64 if array == 2 else 16)
+    if y is None:
+        low = pl.ds(0, 2)
+    elif isinstance(y, tuple):
+        low = pl.ds(y[0], 1)
+    else:
+        low = y % 2
+        if array == 2:
+            rows = pl.ds(pl.multiple_of((y // 2) * 32, 32), 32)
+        else:
+            half = tiles // 2 * TILE
+            columns = pl.ds(pl.multiple_of(tile * TILE + (y // 2) * half, TILE), half)
+
+    def one(v):
+        return pl.ds(0, 4) if v is None else v
+
+    index = lead + (one(sel["x"]), low, one(sel["z"]))
+    if "c" in sel:
+        index = index + (sel["c"],)
+    return ref.at[index + (rows, columns)]
+
+
+def half_of(axis, part):
+    return (part,) if axis == "y" else pl.ds(2 * part, 2)
+
+
+def greet(at, peers):
+    barrier = pltpu.get_barrier_semaphore()
+    for axis, by in peers:
+        pl.semaphore_signal(barrier, inc=1, device_id=device(moved(at, axis, by)), device_id_type=MESH)
+    pl.semaphore_wait(barrier, len(peers))
+
+
+PEERS = tuple((a, b) for a in "xyz" for b in (1, 3, 2)) + (("c", 1),)
+
+
+class Gather:
+    def __init__(self, at, ref, chain, send, recv):
+        self.at, self.ref, self.chain, self.send, self.recv = at, ref, chain, send, recv
+        self.axes = ORDERS[chain[3]]
+        self.count = 0
+        self.sent = []
+
+    def place_own(self, mine, sem):
+        array, tile, tiles, _ = self.chain
+        side = self.at["y"] // 2
+        if array == 2:
+            where = (pl.ds(pl.multiple_of(side * 32, 32), 32), pl.ds(tile * TILE, tiles * TILE))
+        else:
+            wide = tiles // 2 * TILE
+            where = (slice(None), pl.ds(pl.multiple_of(tile * TILE + side * wide, TILE), wide))
+        self.own = pltpu.make_async_copy(mine.at[where], pick(self.ref, self.chain, self.sel(())), sem)
+        self.own.start()
+
+    def copy(self, sel, axis, by):
+        slot = self.count
+        self.count += 1
+        block = pick(self.ref, self.chain, sel)
+        made = pltpu.make_async_remote_copy(
+            src_ref=block,
+            dst_ref=block,
+            send_sem=self.send.at[slot],
+            recv_sem=self.recv.at[slot],
+            device_id=device(moved(self.at, axis, by)),
+            device_id_type=MESH,
+        )
+        made.start()
+        self.sent.append(made)
+        return made
+
+    def sel(self, done, axis=None, by=0, half=None):
+        at = {k: self.at[k] for k in "xyzc"}
+        for d in done:
+            at[d] = None
+        if half is not None:
+            at[done[0]] = half_of(done[0], half)
+        if axis is not None:
+            at[axis] = (self.at[axis] + by) % 4
+        return at
+
+    def step(self, k):
+        a1, a2, a3 = self.axes
+        if k == 0:
+            self.own.wait()
+            own = self.sel(())
+            self.first = [self.copy(own, a1, by) for by in (1, 3, 2)]
+        elif k in (1, 3):
+            done, axis = ((a1,), a2) if k == 1 else ((a1, a2), a3)
+            for c in self.first:
+                c.wait_recv()
+            own = self.sel(done)
+            self.pair = [self.copy(own, axis, 1), self.copy(own, axis, 3)]
+            if k == 3:
+                self.across = [self.copy(own, "c", 1)]
+        elif k in (2, 4):
+            done, axis = ((a1,), a2) if k == 2 else ((a1, a2), a3)
+            self.pair[0].wait_recv()
+            forward = self.copy(self.sel(done, axis, 3, 0), axis, 1)
+            self.pair[1].wait_recv()
+            self.first = [forward, self.copy(self.sel(done, axis, 1, 1), axis, 3)]
+            if k == 4:
+                for by in (3, 1):
+                    self.across.append(self.copy(self.sel(done, axis, by), "c", 1))
+        elif k == 5:
+            for c in self.first:
+                c.wait_recv()
+            self.across.append(self.copy(self.sel((a1, a2), a3, 2), "c", 1))
+        elif k == 6:
+            for c in self.across:
+                c.wait_recv()
+            for c in self.sent:
+                c.wait_send()
+
+
+N_GATHER = 15
+
+
+def gather_kernel(n_layers, att, up, down, small, *rest):
+    outs, (send, recv, local) = rest[:-3], rest[-3:]
+    at = place()
+    greet(at, PEERS)
+    mine = (att, up, down, small)
+    groups = []
+    index = 0
+    for layer in range(n_layers):
+        for group in CHAINS:
+            chains = []
+            for chain in group:
+                if chain[0] == 3:
+                    if layer > 0:
+                        continue
+                    ref = outs[3 * n_layers]
+                else:
+                    ref = outs[3 * layer + chain[0]]
+                made = Gather(at, ref, chain, send.at[index], recv.at[index])
+                made.place_own(mine[chain[0]] if chain[0] == 3 else mine[chain[0]].at[layer], local.at[index])
+                chains.append(made)
+                index += 1
+            groups.append(chains)
+    for slot in range(7 + len(groups) - 1):
+        for g, chains in reversed(list(enumerate(groups))):
+            k = slot - g
+            if 0 <= k < 7:
+                for chain in chains:
+                    chain.step(k)
+
+
+def gather(att, up, down, small):
+    n_layers = att.shape[0]
+    n_chains = n_layers * 9 + 1
+    shapes = []
+    for _ in range(n_layers):
+        shapes += [(4, 2, 4, 2, 16, 4096), (4, 2, 4, 2, 16, 4096), (4, 2, 4, 2, 64, 1024)]
+    shapes.append((4, 2, 4, 2, 16, 256))
+    return pl.pallas_call(
+        functools.partial(gather_kernel, n_layers),
+        out_shape=[jax.ShapeDtypeStruct(s, BF) for s in shapes],
+        in_specs=[pl.BlockSpec(memory_space=pltpu.VMEM)] * 4,
+        out_specs=[pl.BlockSpec(memory_space=pl.ANY)] * len(shapes),
+        scratch_shapes=[
+            pltpu.SemaphoreType.DMA((n_chains, N_GATHER)),
+            pltpu.SemaphoreType.DMA((n_chains, N_GATHER)),
+            pltpu.SemaphoreType.DMA((n_chains,)),
+        ],
+        compiler_params=pltpu.CompilerParams(collective_id=0, has_side_effects=True),
+        name="gather_weights",
+    )(att, up, down, small)
+
+
+N_SCATTER = 12
+PART_SHAPES = ((4, 2, 4, 16, 4096), (4, 2, 4, 16, 4096), (4, 2, 4, 64, 1024), (4, 2, 4, 16, 256))
+OUT_SHAPES = ((16, 4096), (16, 4096), (64, 1024), (16, 256))
+SCATTER_ORDER = (CHAINS[2], CHAINS[1], CHAINS[0])
+
+
+def landing_shapes(chain):
+    array, _, tiles, order = chain
+    a1, a2, a3 = ORDERS[order]
+    rows, cols = (64, tiles * TILE) if array == 2 else (16, tiles * TILE)
+    unit = (rows // 2, cols) if array == 2 else (rows, cols // 2)
+
+    def block(full, half=None):
+        dims = []
+        for axis in "xyz":
+            if axis in full:
+                size = 2 if axis == "y" else 4
+                dims.append(size // 2 if axis == half else size)
+        return tuple(dims) + ((rows, cols) if "y" in full else unit)
+
+    return (
+        (2,) + block((a1, a2), a1),
+        (2,) + block((a1, a2)),
+        (2,) + block((a1,), a1),
+        (2,) + block((a1,)),
+        (3,) + unit,
+        unit,
     )
-    return (
-        lax.psum(shares[0].astype(jnp.bfloat16), "narrow").astype(jnp.float32),
-        lax.psum(shares[1].astype(jnp.bfloat16), "narrow").astype(jnp.float32),
-        lax.psum(shares[2].astype(jnp.bfloat16), "narrow").astype(jnp.float32),
-        lax.psum(shares[3].astype(jnp.bfloat16), "narrow").astype(jnp.float32),
-        lax.psum(shares[4].astype(jnp.bfloat16), "narrow").astype(jnp.float32),
-        lax.psum(shares[5].astype(jnp.bfloat16), "narrow").astype(jnp.float32),
-        lax.psum(shares[6].astype(jnp.bfloat16), "narrow").astype(jnp.float32),
-        lax.psum(shares[7].astype(jnp.bfloat16), "narrow").astype(jnp.float32),
-        lax.psum(shares[8].astype(jnp.bfloat16), "narrow").astype(jnp.float32),
-        lax.psum(shares[9].astype(jnp.bfloat16), "narrow").astype(jnp.float32),
-        lax.psum(shares[10].astype(jnp.bfloat16), "narrow").astype(jnp.float32),
+
+
+class Scatter:
+    def __init__(self, at, part, out, landing, chain, send, recv):
+        self.at, self.part, self.out, self.chain = at, part, out, chain
+        self.landing, self.send, self.recv = landing, send, recv
+        self.axes = ORDERS[chain[3]]
+        self.count = 0
+        self.sent = []
+
+    def copy(self, src, dst, axis, by):
+        slot = self.count
+        self.count += 1
+        made = pltpu.make_async_remote_copy(
+            src_ref=src,
+            dst_ref=dst,
+            send_sem=self.send.at[slot],
+            recv_sem=self.recv.at[slot],
+            device_id=device(moved(self.at, axis, by)),
+            device_id_type=MESH,
+        )
+        made.start()
+        self.sent.append(made)
+        return made
+
+    def sel(self, done, axis=None, by=0, half=None):
+        at = {k: self.at[k] for k in "xyz"}
+        for d in done:
+            at[d] = None
+        if half is not None:
+            at[done[0]] = half_of(done[0], half)
+        if axis is not None:
+            at[axis] = (self.at[axis] + by) % 4
+        return pick(self.part, self.chain, at)
+
+    def step(self, k):
+        a1, a2, a3 = self.axes
+        if k in (1, 3):
+            done, axis = ((a1, a2), a3) if k == 1 else ((a1,), a2)
+            land, blocks = self.landing[k - 1], self.landing[k]
+            self.blocks = []
+            for i, by in ((0, 1), (1, 3)):
+                self.halves[i].wait_recv()
+                add_to(self.sel(done, axis, by, i), (land.at[i],))
+                self.blocks.append(self.copy(self.sel(done, axis, by), blocks.at[i], axis, by))
+        if k in (2, 4):
+            done = (a1, a2) if k == 2 else (a1,)
+            blocks = self.landing[k - 1]
+            for c in self.blocks:
+                c.wait_recv()
+            add_to(self.sel(done), (blocks.at[0], blocks.at[1]))
+        if k in (0, 2):
+            done, axis = ((a1, a2), a3) if k == 0 else ((a1,), a2)
+            land = self.landing[0 if k == 0 else 2]
+            self.halves = [
+                self.copy(self.sel(done, axis, 2, 0), land.at[0], axis, 1),
+                self.copy(self.sel(done, axis, 2, 1), land.at[1], axis, 3),
+            ]
+        if k == 4:
+            land = self.landing[4]
+            self.units = [self.copy(self.sel((), a1, by), land.at[i], a1, by) for i, by in enumerate((1, 3, 2))]
+        if k == 5:
+            land = self.landing[4]
+            for c in self.units:
+                c.wait_recv()
+            add_to(self.sel(()), (land.at[0], land.at[1], land.at[2]))
+            self.last = self.copy(self.sel(()), self.landing[5], "y", 2)
+        if k == 6:
+            self.last.wait_recv()
+            array, tile, tiles, _ = self.chain
+            high = self.at["y"] // 2
+            for side, ref in ((high, self.sel(())), (1 - high, self.landing[5])):
+                if array == 2:
+                    where = (pl.ds(pl.multiple_of(side * 32, 32), 32), pl.ds(tile * TILE, tiles * TILE))
+                else:
+                    wide = tiles // 2 * TILE
+                    where = (slice(None), pl.ds(pl.multiple_of(tile * TILE + side * wide, TILE), wide))
+                self.out[where] = ref[...].astype(F32)
+            for c in self.sent:
+                c.wait_send()
+
+
+def add_to(ref, terms):
+    lead = ref.shape[:-2]
+    if not lead:
+        total = ref[...]
+        for t in terms:
+            total = total + t[...]
+        ref[...] = total
+        return
+    n = 1
+    for d in lead:
+        n *= d
+
+    def body(i, _):
+        index = []
+        rest = i
+        for d in reversed(lead):
+            index.append(rest % d)
+            rest = rest // d
+        index = tuple(reversed(index))
+        total = ref[index]
+        for t in terms:
+            total = total + t[index]
+        ref[index] = total
+        return 0
+
+    lax.fori_loop(0, n, body, 0)
+
+
+def scatter_kernel(gqkv, go, gup, gdown, gsmall, *rest):
+    outs, rest = rest[:4], rest[4:]
+    parts, lands, rest = rest[:4], rest[4:8], rest[8:]
+    landings, (send, recv, local, across_s, across_r) = rest[:-5], rest[-5:]
+    at = place()
+    c = at["c"]
+    greet(at, PEERS)
+    partner = device(moved(at, "c", 1))
+
+    def half(ref, core):
+        return ref.at[:, :, :, core]
+
+    loads = {}
+    for array, src, cols in (
+        (2, gdown, None),
+        (1, gup, None),
+        (0, gqkv, (0, 3072)),
+        (0, go, (3072, 1024)),
+        (3, gsmall, None),
+    ):
+        i = len(loads)
+        window = (lambda r: r) if cols is None else (lambda r, w=cols: r.at[:, :, :, :, pl.ds(w[0], w[1])])
+        own = pltpu.make_async_copy(half(src, c), window(parts[array]), local.at[i])
+        other = pltpu.make_async_remote_copy(
+            src_ref=half(src, 1 - c),
+            dst_ref=window(lands[array]),
+            send_sem=across_s.at[i],
+            recv_sem=across_r.at[i],
+            device_id=partner,
+            device_id_type=MESH,
+        )
+        own.start()
+        other.start()
+        loads[i] = (own, other)
+    needs = {2: (0,), 1: (1,), 0: (2, 3), 3: (4,)}
+    groups = []
+    index = 0
+    for group in SCATTER_ORDER:
+        chains = []
+        for chain in group:
+            land = landings[6 * index : 6 * index + 6]
+            chains.append(Scatter(at, parts[chain[0]], outs[chain[0]], land, chain, send.at[index], recv.at[index]))
+            index += 1
+        groups.append(chains)
+
+    def enter(chains):
+        for array in sorted({chain.chain[0] for chain in chains}):
+            for i in needs[array]:
+                loads[i][0].wait()
+                loads[i][1].wait_recv()
+            add_to(parts[array], (lands[array],))
+
+    for slot in range(8 + len(groups) - 1):
+        for g, chains in enumerate(groups):
+            k = slot - g
+            if k == 0:
+                enter(chains)
+            elif 0 < k < 8:
+                for chain in chains:
+                    chain.step(k - 1)
+    for i in loads:
+        loads[i][1].wait_send()
+
+
+def scatter(gqkv, go, gup, gdown, gsmall):
+    lead = (4, 2, 4, 2)
+    args = (
+        gqkv.reshape(lead + (16, 3072)),
+        go.reshape(lead + (16, 1024)),
+        gup.reshape(lead + (16, 4096)),
+        gdown.reshape(lead + (64, 1024)),
+        gsmall.reshape(lead + (16, 256)),
     )
+    chains = [c for g in SCATTER_ORDER for c in g]
+    scratch = [pltpu.VMEM(s, BF) for s in PART_SHAPES] * 2
+    for chain in chains:
+        scratch += [pltpu.VMEM(s, BF) for s in landing_shapes(chain)]
+    scratch += [pltpu.SemaphoreType.DMA((len(chains), N_SCATTER))] * 2
+    scratch += [pltpu.SemaphoreType.DMA((5,))] * 3
+    return pl.pallas_call(
+        scatter_kernel,
+        out_shape=[jax.ShapeDtypeStruct(s, F32) for s in OUT_SHAPES],
+        in_specs=[pl.BlockSpec(memory_space=pl.ANY)] * 5,
+        out_specs=[pl.BlockSpec(memory_space=pltpu.VMEM)] * 4,
+        scratch_shapes=scratch,
+        compiler_params=pltpu.CompilerParams(collective_id=1, has_side_effects=True, vmem_limit_bytes=56 << 20),
+        name="scatter_grads",
+    )(*args)
 
 
 def on_device(
@@ -94,9 +501,9 @@
     score_scale = HEAD ** (-0.5)
     positions = jnp.arange(length, dtype=jnp.int32)
     distance = jnp.maximum(positions[:, None] - positions[None, :], 0)
-    onehot = (
-        buckets[distance][:, :, None] == jnp.arange(BUCKETS, dtype=jnp.int32)[None, None, :]
-    ).astype(jnp.bfloat16)
+    at_distance = (distance[:, :, None] == positions[None, None, :]).astype(jnp.bfloat16)
+    bucket_of = (buckets[:, None] == jnp.arange(BUCKETS, dtype=jnp.int32)[None, :]).astype(jnp.bfloat16)
+    onehot = jnp.dot(at_distance, bucket_of, preferred_element_type=jnp.float32).astype(jnp.bfloat16)
     allowed = (positions[:, None] >= positions[None, :]) & (seg_ids[:, None] == seg_ids[None, :])
 
     def masked_scores(queries, key_rows, rel_bias):
@@ -190,15 +597,8 @@
         grad_bias_table = jnp.einsum(
             "hij,ijb->bh", grad_scores, onehot, preferred_element_type=jnp.float32
         ).reshape(BUCKETS * HEADS)
-        grad_query_w = jnp.einsum(
-            "ld,le->de", input_one, grad_queries, preferred_element_type=jnp.float32
-        )
-        grad_key_w = jnp.einsum(
-            "ld,le->de", input_one, grad_keys, preferred_element_type=jnp.float32
-        )
-        grad_value_w = jnp.einsum(
-            "ld,le->de", input_one, grad_values, preferred_element_type=jnp.float32
-        )
+        grad_all = jnp.concatenate([grad_queries, grad_keys, grad_values], 1)
+        grad_qkv = jnp.einsum("ld,le->de", input_one, grad_all, preferred_element_type=jnp.float32)
         grad_hidden_one = jnp.einsum(
             "le,de->ld", grad_queries, query_w, preferred_element_type=jnp.float32
         )
@@ -211,39 +611,55 @@
         grad_gain_one = jnp.sum(grad_hidden_one * normed_one, 0)
         grad_shift_one = jnp.sum(grad_hidden_one, 0)
         grad_stream = grad_middle + norm_back(grad_hidden_one, normed_one, inverse_one, gain_one)
-        grads = (
-            grad_gain_one,
-            grad_shift_one,
-            grad_query_w,
-            grad_key_w,
-            grad_value_w,
-            grad_out_w,
-            grad_bias_table,
-            grad_gain_two,
-            grad_shift_two,
-            grad_up,
-            grad_down,
-        )
+        small = jnp.concatenate(
+            [
+                grad_gain_one.reshape(64, 16),
+                grad_shift_one.reshape(64, 16),
+                grad_gain_two.reshape(64, 16),
+                grad_shift_two.reshape(64, 16),
+                grad_bias_table.reshape(64, 8),
+            ],
+            1,
+        )
+        small = jnp.pad(small[:, None], ((0, 0), (0, 15), (0, 56)))
+        small = jnp.concatenate([small, small], 2)
+        grads = tuple(g.astype(BF) for g in (grad_qkv, grad_out_w, grad_up, grad_down, small))
         return (grad_stream, grads)
+
+    def shares(layer_at):
+        return jnp.concatenate(
+            [ln1_gain[layer_at], ln1_bias[layer_at], ln2_gain[layer_at], ln2_bias[layer_at], rel_table[layer_at]]
+        )
+
+    small = jnp.stack([shares(0), shares(1)])
+    small = jnp.pad(small, ((0, 14), (0, 56)))
+    fetched = gather(jnp.concatenate([w_query, w_key, w_value, w_out], 2), w_up, w_down, jnp.concatenate([small, small], 1))
+    small_all = fetched[6].reshape(64, 16, 256)[:, :2, :128]
+
+    def weights_of(layer_at):
+        att = fetched[3 * layer_at].reshape(1024, 4096)
+        up = fetched[3 * layer_at + 1].reshape(1024, 4096)
+        down = fetched[3 * layer_at + 2].reshape(4096, 1024)
+        mine = small_all[:, layer_at]
+        return (
+            mine[:, 0:16].reshape(1024),
+            mine[:, 16:32].reshape(1024),
+            att[:, :1024],
+            att[:, 1024:2048],
+            att[:, 2048:3072],
+            att[:, 3072:],
+            mine[:, 64:72].reshape(512),
+            mine[:, 32:48].reshape(1024),
+            mine[:, 48:64].reshape(1024),
+            up,
+            down,
+        )
 
     stream = tokens.astype(jnp.float32)
     saved_all = []
-    fetched_all = []
     layer_acts = []
     for layer_at in range(2):
-        layer_weights = (
-            lax.all_gather(ln1_gain[layer_at], "wide", axis=0, tiled=True),
-            lax.all_gather(ln1_bias[layer_at], "wide", axis=0, tiled=True),
-            lax.all_gather(w_query[layer_at], "wide", axis=0, tiled=True),
-            lax.all_gather(w_key[layer_at], "wide", axis=0, tiled=True),
-            lax.all_gather(w_value[layer_at], "wide", axis=0, tiled=True),
-            lax.all_gather(w_out[layer_at], "wide", axis=0, tiled=True),
-            lax.all_gather(rel_table[layer_at], "wide", axis=0, tiled=True),
-            lax.all_gather(ln2_gain[layer_at], "wide", axis=0, tiled=True),
-            lax.all_gather(ln2_bias[layer_at], "wide", axis=0, tiled=True),
-            lax.all_gather(w_up[layer_at], "wide", axis=0, tiled=True),
-            lax.all_gather(w_down[layer_at], "wide", axis=0, tiled=True),
-        )
+        layer_weights = weights_of(layer_at)
         (
             layer_gain_one,
             layer_shift_one,
@@ -322,28 +738,29 @@
         stream = result
         saved_layer = layer_saved_layer
         saved_all.append(saved_layer)
-        fetched_all.append(layer_weights)
         layer_acts.append(stream.astype(jnp.bfloat16))
     grad_stream = cotangent.astype(jnp.float32)
     reduced = [None, None]
     for layer_at in (1, 0):
-        layer_weights = (
-            lax.all_gather(ln1_gain[layer_at], "wide", axis=0, tiled=True),
-            lax.all_gather(ln1_bias[layer_at], "wide", axis=0, tiled=True),
-            lax.all_gather(w_query[layer_at], "wide", axis=0, tiled=True),
-            lax.all_gather(w_key[layer_at], "wide", axis=0, tiled=True),
-            lax.all_gather(w_value[layer_at], "wide", axis=0, tiled=True),
-            lax.all_gather(w_out[layer_at], "wide", axis=0, tiled=True),
-            lax.all_gather(rel_table[layer_at], "wide", axis=0, tiled=True),
-            lax.all_gather(ln2_gain[layer_at], "wide", axis=0, tiled=True),
-            lax.all_gather(ln2_bias[layer_at], "wide", axis=0, tiled=True),
-            lax.all_gather(w_up[layer_at], "wide", axis=0, tiled=True),
-            lax.all_gather(w_down[layer_at], "wide", axis=0, tiled=True),
-        )
-        grad_stream, grads = layer_backward(grad_stream, saved_all[layer_at], layer_weights)
-        reduced[layer_at] = reduce_grads(grads)
-    stacked = tuple((jnp.stack([reduced[0][index], reduced[1][index]]) for index in range(11)))
-    return (jnp.stack(layer_acts), grad_stream) + stacked
+        grad_stream, grads = layer_backward(grad_stream, saved_all[layer_at], weights_of(layer_at))
+        reduced[layer_at] = scatter(*grads)
+    stacked = [jnp.stack([reduced[0][i], reduced[1][i]]) for i in range(4)]
+    att, up, down, small = stacked
+    return (
+        jnp.stack(layer_acts),
+        grad_stream,
+        small[:, 0, 0:16],
+        small[:, 0, 16:32],
+        att[:, :, :1024],
+        att[:, :, 1024:2048],
+        att[:, :, 2048:3072],
+        att[:, :, 3072:],
+        small[:, 0, 64:72],
+        small[:, 0, 32:48],
+        small[:, 0, 48:64],
+        up,
+        down,
+    )
 
 
 def solution(mesh):

time: 4960 us -> 523 us (0.11)
  waiting for transfers between devices: 3670 us -> 0 us
  blocking collectives: 559 us -> 0 us
  local copies, waits for them, and re-layouts: 466 us -> 41.4 us
  Pallas kernels: 0 us -> 269 us
    reduce_scatter x12 -> x0, waiting for transfers between devices: 3140 us -> none  [the longest x2 618 us: reduce_grads(): lax.psum_scatter(grads[9], 'wide', scatter_dimension=0, tiled=True)]
    unnamed x2 -> x0, blocking collectives: 559 us -> none
    all_gather x12 -> x0, waiting for transfers between devices: 499 us -> none  [the longest x2 110 us: on_device(): lax.all_gather(w_up[layer_at], 'wide', axis=0, tiled=True)]
    gather x2 -> x0, local copies, waits for them, and re-layouts: 408 us -> none  [on_device(): buckets[distance][:, :, None]]
    pallas_call x0 -> x3, Pallas kernels: none -> 269 us  [the longest x2 156 us: scatter(): pl.pallas_call(scatter_kernel, out_shape=[jax.ShapeDtypeStruct(s, F32) fo...]
  transfers between devices with their start and end apart: 26 -> 0, of which waited for: 17 -> 0; matrix products, arithmetic and copies ran while one was open for 13% -> 0% of each run, Pallas kernels for 0% -> 0%
where the time goes in v1:
time: 523 us; the launch traced here: 514 us
  Pallas kernels  269 us (51%)
  matrix products  178 us (34%)
  local copies, waits for them, and re-layouts  41.4 us (8%)
  other arithmetic  24.5 us (5%)
    pallas_call x2, Pallas kernels, scatter(): pl.pallas_call(scatter_kernel, out_shape=[jax.ShapeDtypeStruct(s, F32) fo...  156 us
    pallas_call x1, Pallas kernels, gather(): pl.pallas_call(functools.partial(gather_kernel, n_layers), out_shape=[jax...  112 us
    dot_general x2, local copies, waits for them, and re-layouts, on_device(): jnp.einsum('ijb,bh->hij', onehot, layer_table.reshape(BUCKETS, HEADS), pr...  21.6 us
    dot_general x1, matrix products, on_device(): jnp.dot(at_distance, bucket_of, preferred_element_type=jnp.float32)  17.6 us
    dot_general x2, matrix products, on_device(): jnp.dot(layer_activated, layer_down_w, preferred_element_type=jnp.float32)  11.8 us
    dot_general x2, matrix products, on_device(): jnp.dot(layer_input_two, layer_up_w, preferred_element_type=jnp.float32)  11.8 us
    dot_general x2, matrix products, layer_backward(): jnp.einsum('ld,lf->df', input_two, grad_upward, preferred_element_type=jn...  11.5 us
    dot_general x2, matrix products, layer_backward(): jnp.einsum('lf,ld->fd', activated, down_in, preferred_element_type=jnp.fl...  11.1 us

profile of v1, /device:TPU:0, one launch (start us, length us, event | category | flops | bytes accessed | tf_op | source)
XLA Modules:
  0.0 514.0 jit_solution(3495896554464596714)
XLA Ops:
  9.5 17.6 %fusion.19 = bf16[256,256,32]{1,2,0:T(8,128)(2,1)} fusion(s32[256,256]{1,0:T(8,128)S(1)} %subtract_maximum_fusion, pred[256,32,1]{0,1,2:T(32,128)(4,1)S(1)} %fusion.233), kind=kOutput, calls=%fused_computation.46 | convolution fusion | flops 1092616192 | bytes 4464640 | tf_op jit(solution)/shard_map/dot_general | solution.py:506
  27.1 112.5 %gather_weights.1 = (bf16[4,2,4,2,16,4096]{5,4,3,2,1,0:T(8,128)(2,1)}, bf16[4,2,4,2,16,4096]{5,4,3,2,1,0:T(8,128)(2,1)}, bf16[4,2,4,2,64,1024]{5,4,3,2,1,0:T(8,1...) custom-call(bf16[2,16,4096]{2,1,0:T(8,128)(2,1)} %pad_maximum_fusion, ...), custom_call_target="tpu_custom_call" | custom-call | tf_op jit(solution)/shard_map/gather_weights/pallas_call | solution.py:239
  141.7 2.3 fusion.97
  144.3 2.5 fusion.100
  147.1 2.5 fusion.94
  149.8 5.1 fusion.157
  154.9 16.4 %copy.62 = f32[16,256,256]{1,2,0:T(8,128)} copy(f32[16,256,256]{2,0,1:T(8,128)} %fusion.157) | data formatting | bytes 8388608 | tf_op jit(solution)/shard_map/ijb,bh->hij/dot_general | solution.py:695
  171.3 3.2 fusion.171
  176.4 2.6 fusion.172
  179.4 2.7 fusion.155
  182.1 5.3 %copy.69 = f32[16,256,256]{1,2,0:T(8,128)} copy(f32[16,256,256]{2,0,1:T(8,128)} %fusion.155) | data formatting | bytes 8388608 | tf_op jit(solution)/shard_map/ijb,bh->hij/dot_general | solution.py:695
  187.4 5.8 %fusion.164 = f32[256,4096]{1,0:T(8,128)S(1)} fusion(bf16[1024,4096]{1,0:T(8,128)(2,1)} %bitcast.256, f32[256,1024]{1,0:T(8,128)S(1)} %get-tuple-element.92, f32[1024]{0:T(1024)S(1)} %reshape.417, f32[1024]{0:T(1024)S(1)} %reshape.416, f32[256]{0:T(256)S(1)} %add_rsqrt_fusion.2, f32[256]{0:T(256)S(1)} %broadcast_multiply_fusion.10), kind=kOutput, calls=%fused_computation.256 | convolution fusion | flops 2148794368 | bytes 13641728 | tf_op jit(solution)/shard_map/dot_general | solution.py:719
  193.2 7.7 %fusion.173 = (f32[256]{0:T(256)S(1)}, f32[256,1024]{1,0:T(8,128)S(1)}) fusion(f32[256,1024]{1,0:T(8,128)S(1)} %get-tuple-element.92, bf16[4096,1024]{1,0:T(8,128)(2,1)} %bitcast.260, f32[256,4096]{1,0:T(8,128)S(1)} %fusion.164), kind=kOutput, calls=%fused_computation.261 | convolution fusion | flops 2157444864 | bytes 14681088 | tf_op jit(solution)/shard_map/dot_general | solution.py:721
  201.5 2.5 fusion.112
  204.2 2.5 fusion.109
  206.9 3.4 fusion.174
  212.9 2.3 fusion.106
  215.4 3.2 fusion.122
  218.7 2.6 fusion.175
  221.5 6.0 %fusion.165 = f32[256,4096]{1,0:T(8,128)S(1)} fusion(bf16[1024,4096]{1,0:T(8,128)(2,1)} %bitcast.264, f32[256,1024]{1,0:T(8,128)S(1)} %get-tuple-element.98, f32[1024]{0:T(1024)S(1)} %reshape.421, f32[1024]{0:T(1024)S(1)} %reshape.420, f32[256]{0:T(256)S(1)} %add_rsqrt_fusion, f32[256]{0:T(256)S(1)} %broadcast_multiply_fusion.8), kind=kOutput, calls=%fused_computation.257 | convolution fusion | flops 2148794368 | bytes 13641728 | tf_op jit(solution)/shard_map/dot_general | solution.py:719
  227.5 4.1 fusion.130
  231.6 4.7 fusion.3
  236.3 2.7 multiply_reduce_fusion.2
  239.6 3.4 fusion.115
  244.3 3.9 fusion.88
  255.1 3.3 copy.83
  258.4 4.1 convolution_bitcast_fusion.1
  262.7 2.5 fusion.32
  265.2 2.4 fusion.81
  267.6 2.9 multiply_reduce_fusion.3
  272.0 4.5 fusion.4
  276.6 2.7 multiply_reduce_fusion.4
  282.4 3.2 fusion.103
  286.8 3.9 fusion.91
  290.8 2.1 convolution_convert_fusion.7
  292.8 5.6 %convolution_convert_fusion.2 = bf16[4096,1024]{1,0:T(8,128)(2,1)} fusion(f32[256,1024]{1,0:T(8,128)S(1)} %copy-done.25, f32[256,4096]{1,0:T(8,128)S(1)} %copy-done.60), kind=kOutput, calls=%fused_computation.5 | convolution fusion | flops 2161377280 | bytes 13631488 | tf_op jit(solution)/shard_map/lf,ld->fd/dot_general | solution.py:548
  303.6 3.1 copy.80
  306.8 4.4 convolution_bitcast_fusion.2
  311.3 2.4 fusion.48
  313.7 2.4 fusion.73
  316.1 2.8 fusion.137
  321.8 5.9 %convolution_convert_fusion.4 = bf16[1024,3072]{1,0:T(8,128)(2,1)} fusion(bf16[256,1024]{1,0:T(8,128)(2,1)} %copy-done.45, bf16[256,1024]{0,1:T(8,128)(2,1)S(1)} %bitcast.229, bf16[256,1024]{0,1:T(8,128)(2,1)} %bitcast.232, bf16[256,1024]{0,1:T(8,128)(2,1)S(1)} %bitcast.219), kind=kOutput, calls=%fused_computation.11 | convolution fusion | flops 1618477056 | bytes 8388608 | tf_op jit(solution)/shard_map/ld,le->de/dot_general | solution.py:601
  327.7 5.5 %convolution_convert_fusion = bf16[4096,1024]{1,0:T(8,128)(2,1)} fusion(bf16[256,1024]{1,0:T(8,128)(2,1)S(1)} %copy-done.40, f32[256,4096]{1,0:T(8,128)S(1)} %copy-done.57), kind=kOutput, calls=%fused_computation.3 | convolution fusion | flops 2161115136 | bytes 13107200 | tf_op jit(solution)/shard_map/lf,ld->fd/dot_general | solution.py:548
  333.3 4.8 convolution_convert_fusion.5
  338.1 5.7 %convolution_convert_fusion.3 = bf16[1024,4096]{1,0:T(8,128)(2,1)} fusion(bf16[256,4096]{1,0:T(8,128)(2,1)S(1)} %copy-done.29, f32[256,1024]{1,0:T(8,128)S(1)} %copy-done.7, f32[1024]{0:T(1024)S(1)} %reshape.417, f32[1024]{0:T(1024)S(1)} %reshape.416, f32[256]{0:T(256)S(1)} %add_rsqrt_fusion.2, f32[256]{0:T(256)S(1)} %broadcast_multiply_fusion.10), kind=kOutput, calls=%fused_computation.6 | convolution fusion | flops 2152988672 | bytes 11544576 | tf_op jit(solution)/shard_map/ld,lf->df/dot_general | solution.py:551
  343.8 78.6 %scatter_grads.2 = (f32[16,4096]{1,0:T(8,128)}, f32[16,4096]{1,0:T(8,128)}, f32[64,1024]{1,0:T(8,128)}, f32[16,256]{1,0:T(8,128)}) custom-call(bf16[4,2,4,2,16,3072]{5,4,3,2,1,0:T(8,128)(2,1)} %bitcast.181, bf16[4,2,4,2,16,1024]{5,4,3,2,1,0:T(8,128)(2,1)} %bitcast.179, bf16[4,2,4,2,16,4096]{5,4,3,2,1,0:T(8,128)(2,1)} %bitcast.174, ...), custom_call_target="tpu_custom_call" | custom-call | tf_op jit(solution)/shard_map/scatter_grads/pallas_call | solution.py:471
  422.4 5.8 %convolution_convert_fusion.1 = bf16[1024,4096]{1,0:T(8,128)(2,1)} fusion(bf16[256,4096]{1,0:T(8,128)(2,1)S(1)} %copy-done.27, f32[256,1024]{1,0:T(8,128)S(1)} %get-tuple-element.98, f32[1024]{0:T(1024)S(1)} %reshape.421, f32[1024]{0:T(1024)S(1)} %reshape.420, f32[256]{0:T(256)S(1)} %add_rsqrt_fusion, f32[256]{0:T(256)S(1)} %broadcast_multiply_fusion.8), kind=kOutput, calls=%fused_computation.4 | convolution fusion | flops 2152988672 | bytes 11544576 | tf_op jit(solution)/shard_map/ld,lf->df/dot_general | solution.py:551
  428.2 77.5 %scatter_grads.3 = (f32[16,4096]{1,0:T(8,128)}, f32[16,4096]{1,0:T(8,128)}, f32[64,1024]{1,0:T(8,128)}, f32[16,256]{1,0:T(8,128)}) custom-call(bf16[4,2,4,2,16,3072]{5,4,3,2,1,0:T(8,128)(2,1)} %bitcast.180, bf16[4,2,4,2,16,1024]{5,4,3,2,1,0:T(8,128)(2,1)} %bitcast.178, bf16[4,2,4,2,16,4096]{5,4,3,2,1,0:T(8,128)(2,1)} %bitcast.175, ...), custom_call_target="tpu_custom_call" | custom-call | tf_op jit(solution)/shard_map/scatter_grads/pallas_call | solution.py:471
  (242 shorter events, 48.5 us)
Async XLA Ops:
  9.4 132.3 %copy-start.14 = (bf16[256,1024]{1,0:T(8,128)(2,1)S(1)}, bf16[256,1024]{1,0:T(8,128)(2,1)}, u32[]{:S(2)}) copy-start(bf16[256,1024]{1,0:T(8,128)(2,1)} %param.15) | copy-start | bytes 1572868
  141.3 5.8 %copy-start.54 = (f32[1024]{0:T(1024)}, f32[1024]{0:T(1024)S(1)}, u32[]{:S(2)}) copy-start(f32[1024]{0:T(1024)S(1)} %reshape.415) | copy-start | bytes 12292
  144.3 27.0 %copy-start.16 = (bf16[256,1024]{0,1:T(8,128)(2,1)}, bf16[256,1024]{0,1:T(8,128)(2,1)S(1)}, u32[]{:S(2)}) copy-start(bf16[256,1024]{0,1:T(8,128)(2,1)S(1)} %copy.59) | copy-start | bytes 1572868
  147.1 24.2 %copy-start.18 = (bf16[256,1024]{0,1:T(8,128)(2,1)}, bf16[256,1024]{0,1:T(8,128)(2,1)S(1)}, u32[]{:S(2)}) copy-start(bf16[256,1024]{0,1:T(8,128)(2,1)S(1)} %copy.60) | copy-start | bytes 1572868
  149.8 25.2 %copy-start.32 = (bf16[256,1024]{0,1:T(8,128)(2,1)}, bf16[256,1024]{0,1:T(8,128)(2,1)S(1)}, u32[]{:S(2)}) copy-start(bf16[256,1024]{0,1:T(8,128)(2,1)S(1)} %copy.58) | copy-start | bytes 1572868
  179.1 14.1 %copy-start.5 = (f32[256,1024]{1,0:T(8,128)}, f32[256,1024]{1,0:T(8,128)S(1)}, u32[]{:S(2)}) copy-start(f32[256,1024]{1,0:T(8,128)S(1)} %get-tuple-element.92) | copy-start | bytes 3145732
  193.2 7.7 %copy-start.58 = (f32[256,4096]{1,0:T(8,128)}, f32[256,4096]{1,0:T(8,128)S(1)}, u32[]{:S(2)}) copy-start(f32[256,4096]{1,0:T(8,128)S(1)} %fusion.164) | copy-start | bytes 12582916
  201.0 17.7 %copy-start.8 = (f32[256,1024]{1,0:T(8,128)}, f32[256,1024]{1,0:T(8,128)S(1)}, u32[]{:S(2)}) copy-start(f32[256,1024]{1,0:T(8,128)S(1)} %get-tuple-element.94) | copy-start | bytes 3145732
  201.5 11.4 %copy-start.45 = (bf16[256,1024]{1,0:T(8,128)(2,1)}, bf16[256,1024]{1,0:T(8,128)(2,1)S(1)}, u32[]{:S(2)}) copy-start(bf16[256,1024]{1,0:T(8,128)(2,1)S(1)} %add_convert_fusion.1) | copy-start | bytes 1572868
  204.2 6.1 %copy-start.20 = (bf16[256,1024]{0,1:T(8,128)(2,1)}, bf16[256,1024]{0,1:T(8,128)(2,1)S(1)}, u32[]{:S(2)}) copy-start(bf16[256,1024]{0,1:T(8,128)(2,1)S(1)} %copy.67) | copy-start | bytes 1572868
  218.7 8.8 %slice-start.6 = ((s8[8388608]{0:T(1024)(128)(4,1)}), s8[4194304]{0:T(1024)(128)(4,1)S(1)}, s32[]{:S(2)}) async-start(s8[8388608]{0:T(1024)(128)(4,1)} %bitcast.268), calls=%async_computation.6 | async-start | bytes 8388608
  221.5 6.0 %slice-start.7 = ((s8[8388608]{0:T(1024)(128)(4,1)}), s8[4194304]{0:T(1024)(128)(4,1)S(1)}, s32[]{:S(2)}) async-start(s8[8388608]{0:T(1024)(128)(4,1)} %bitcast.268), calls=%async_computation.7 | async-start | bytes 8388608
  227.5 8.8 %slice-start.4 = ((s8[8388608]{0:T(1024)(128)(4,1)}), s8[4194304]{0:T(1024)(128)(4,1)S(1)}, s32[]{:S(2)}) async-start(s8[8388608]{0:T(1024)(128)(4,1)} %bitcast.265), calls=%async_computation.4 | async-start | bytes 8388608
  231.6 4.7 slice-start.5
  239.5 8.7 %copy-start.12 = (f32[256,1024]{1,0:T(8,128)}, f32[256,1024]{1,0:T(8,128)S(1)}, u32[]{:S(2)}) copy-start(f32[256,1024]{1,0:T(8,128)S(1)} %multiply_add_fusion.4) | copy-start | bytes 3145732
  244.3 6.0 %copy-start.3 = (f32[16,256,256]{1,2,0:T(8,128)S(1)}, f32[16,256,256]{1,2,0:T(8,128)}, u32[]{:S(2)}) copy-start(f32[16,256,256]{1,2,0:T(8,128)} %copy-done.2) | copy-start | bytes 12582916
  244.3 6.0 %copy-start.35 = (bf16[256,1024]{0,1:T(8,128)(2,1)S(1)}, bf16[256,1024]{0,1:T(8,128)(2,1)}, u32[]{:S(2)}) copy-start(bf16[256,1024]{0,1:T(8,128)(2,1)} %copy-done.34) | copy-start | bytes 1572868
  258.4 6.8 %copy-start.36 = (bf16[16,64,256]{2,1,0:T(8,128)(2,1)S(1)}, bf16[16,64,256]{2,1,0:T(8,128)(2,1)}, u32[]{:S(2)}) copy-start(bf16[16,64,256]{2,1,0:T(8,128)(2,1)} %fusion.118) | copy-start | bytes 1572868
  262.7 4.9 copy-start.9
  262.7 4.9 copy-start.41
  262.7 8.3 %slice-start.2 = ((s8[8388608]{0:T(1024)(128)(4,1)}), s8[4194304]{0:T(1024)(128)(4,1)S(1)}, s32[]{:S(2)}) async-start(s8[8388608]{0:T(1024)(128)(4,1)} %bitcast.261), calls=%async_computation.2 | async-start | bytes 8388608
  267.6 4.4 copy-start.59
  270.5 6.0 %slice-start = ((s8[8388608]{0:T(1024)(128)(4,1)}), s8[4194304]{0:T(1024)(128)(4,1)S(1)}, s32[]{:S(2)}) async-start(s8[8388608]{0:T(1024)(128)(4,1)} %bitcast.257), calls=%async_computation | async-start | bytes 8388608
  271.0 9.4 %copy-start.24 = (f32[256,1024]{1,0:T(8,128)}, f32[256,1024]{1,0:T(8,128)S(1)}, u32[]{:S(2)}) copy-start(f32[256,1024]{1,0:T(8,128)S(1)} %get-tuple-element.59) | copy-start | bytes 3145732
  272.0 4.6 copy-start.6
  272.0 4.6 slice-start.1
  280.8 10.0 %copy-start.10 = (f32[256,1024]{1,0:T(8,128)}, f32[256,1024]{1,0:T(8,128)S(1)}, u32[]{:S(2)}) copy-start(f32[256,1024]{1,0:T(8,128)S(1)} %multiply_add_fusion.2) | copy-start | bytes 3145732
  282.4 8.4 %copy-start.31 = (bf16[16,64,256]{2,1,0:T(8,128)(2,1)S(1)}, bf16[16,64,256]{2,1,0:T(8,128)(2,1)}, u32[]{:S(2)}) copy-start(bf16[16,64,256]{2,1,0:T(8,128)(2,1)} %copy-done.30) | copy-start | bytes 1572868
  286.8 6.0 %copy-start.25 = (f32[256,1024]{1,0:T(8,128)S(1)}, f32[256,1024]{1,0:T(8,128)}, u32[]{:S(2)}) copy-start(f32[256,1024]{1,0:T(8,128)} %copy-done.24) | copy-start | bytes 3145732
  286.8 6.0 %copy-start.60 = (f32[256,4096]{1,0:T(8,128)S(1)}, f32[256,4096]{1,0:T(8,128)}, u32[]{:S(2)}) copy-start(f32[256,4096]{1,0:T(8,128)} %copy-done.58) | copy-start | bytes 12582916
  292.8 5.6 %copy-start.1 = (f32[16,256,256]{1,2,0:T(8,128)S(1)}, f32[16,256,256]{1,2,0:T(8,128)}, u32[]{:S(2)}) copy-start(f32[16,256,256]{1,2,0:T(8,128)} %copy-done) | copy-start | bytes 12582916
  292.8 5.6 %copy-start.33 = (bf16[256,1024]{0,1:T(8,128)(2,1)S(1)}, bf16[256,1024]{0,1:T(8,128)(2,1)}, u32[]{:S(2)}) copy-start(bf16[256,1024]{0,1:T(8,128)(2,1)} %copy-done.32) | copy-start | bytes 1572868
  306.8 4.5 copy-start.48
  306.8 7.0 %copy-start.38 = (bf16[16,64,256]{2,1,0:T(8,128)(2,1)S(1)}, bf16[16,64,256]{2,1,0:T(8,128)(2,1)}, u32[]{:S(2)}) copy-start(bf16[16,64,256]{2,1,0:T(8,128)(2,1)} %fusion.120) | copy-start | bytes 1572868
  311.3 4.8 copy-start.15
  311.3 4.8 copy-start.43
  321.8 5.9 %copy-start.40 = (bf16[256,1024]{1,0:T(8,128)(2,1)S(1)}, bf16[256,1024]{1,0:T(8,128)(2,1)}, u32[]{:S(2)}) copy-start(bf16[256,1024]{1,0:T(8,128)(2,1)} %param.18) | copy-start | bytes 1572868
  321.8 5.9 %copy-start.57 = (f32[256,4096]{1,0:T(8,128)S(1)}, f32[256,4096]{1,0:T(8,128)}, u32[]{:S(2)}) copy-start(f32[256,4096]{1,0:T(8,128)} %copy-done.56) | copy-start | bytes 12582916
  327.7 5.5 %copy-start.44 = (bf16[16,64,256]{2,1,0:T(8,128)(2,1)S(1)}, bf16[16,64,256]{2,1,0:T(8,128)(2,1)}, u32[]{:S(2)}) copy-start(bf16[16,64,256]{2,1,0:T(8,128)(2,1)} %fusion.91) | copy-start | bytes 1572868
  327.7 5.5 %copy-start.49 = (bf16[16,64,256]{2,1,0:T(8,128)(2,1)S(1)}, bf16[16,64,256]{2,1,0:T(8,128)(2,1)}, u32[]{:S(2)}) copy-start(bf16[16,64,256]{2,1,0:T(8,128)(2,1)} %fusion.121) | copy-start | bytes 1572868
  327.7 5.5 %copy-start.55 = (f32[1024]{0:T(1024)S(1)}, f32[1024]{0:T(1024)}, u32[]{:S(2)}) copy-start(f32[1024]{0:T(1024)} %copy-done.54) | copy-start | bytes 12292
  333.3 4.8 copy-start.7
  333.3 4.8 copy-start.29
  343.8 78.6 %copy-start.27 = (bf16[256,4096]{1,0:T(8,128)(2,1)S(1)}, bf16[256,4096]{1,0:T(8,128)(2,1)}, u32[]{:S(2)}) copy-start(bf16[256,4096]{1,0:T(8,128)(2,1)} %copy-done.26) | copy-start | bytes 6291460
  428.2 77.5 %copy-start.52 = (f32[16,4096]{1,0:T(8,128)S(1)}, f32[16,4096]{1,0:T(8,128)}, u32[]{:S(2)}) copy-start(f32[16,4096]{1,0:T(8,128)} %get-tuple-element.37) | copy-start | bytes 786436
  428.2 79.2 %copy-start.53 = (f32[16,256]{1,0:T(8,128)S(1)}, f32[16,256]{1,0:T(8,128)}, u32[]{:S(2)}) copy-start(f32[16,256]{1,0:T(8,128)} %get-tuple-element.35) | copy-start | bytes 49156
  428.2 82.0 %copy-start.51 = (f32[16,4096]{1,0:T(8,128)S(1)}, f32[16,4096]{1,0:T(8,128)}, u32[]{:S(2)}) copy-start(f32[16,4096]{1,0:T(8,128)} %get-tuple-element.39) | copy-start | bytes 786436
  428.2 83.8 %copy-start.50 = (f32[64,1024]{1,0:T(8,128)S(1)}, f32[64,1024]{1,0:T(8,128)}, u32[]{:S(2)}) copy-start(f32[64,1024]{1,0:T(8,128)} %get-tuple-element.41) | copy-start | bytes 786436
  (21 other events, 59.3 us)

commit v2 on v1

--- a/solution.py
+++ b/solution.py
@@ -6,10 +6,6 @@
 from jax.experimental import pallas as pl
 from jax.experimental.pallas import tpu as pltpu
 from jax.sharding import PartitionSpec as P
-
-HEADS = 16
-HEAD = 64
-BUCKETS = 32
 
 epsilon = 1e-05
 gelu_coef = 0.7978845608028654
@@ -30,19 +26,6 @@
         scaled
         - jnp.mean(scaled, -1, keepdims=True)
         - normed * jnp.mean(scaled * normed, -1, keepdims=True)
-    )
-
-
-def smooth_gelu(inputs):
-    return (
-        0.5 * inputs * (1.0 + jnp.tanh(gelu_coef * (inputs + 0.044715 * inputs * inputs * inputs)))
-    )
-
-
-def gelu_slope(inputs):
-    tangent = jnp.tanh(gelu_coef * (inputs + 0.044715 * inputs * inputs * inputs))
-    return 0.5 * (1.0 + tangent) + 0.5 * inputs * (1.0 - tangent * tangent) * gelu_coef * (
-        1.0 + 3.0 * 0.044715 * inputs * inputs
     )
 
 
@@ -199,56 +182,23 @@
 N_GATHER = 15
 
 
-def gather_kernel(n_layers, att, up, down, small, *rest):
-    outs, (send, recv, local) = rest[:-3], rest[-3:]
-    at = place()
-    greet(at, PEERS)
-    mine = (att, up, down, small)
+def gather_groups(at, n_layers, mine, fetched, send, recv, local):
     groups = []
     index = 0
     for layer in range(n_layers):
         for group in CHAINS:
             chains = []
             for chain in group:
-                if chain[0] == 3:
-                    if layer > 0:
-                        continue
-                    ref = outs[3 * n_layers]
-                else:
-                    ref = outs[3 * layer + chain[0]]
+                array = chain[0]
+                if array == 3 and layer > 0:
+                    continue
+                ref = fetched[3 * n_layers] if array == 3 else fetched[3 * layer + array]
                 made = Gather(at, ref, chain, send.at[index], recv.at[index])
-                made.place_own(mine[chain[0]] if chain[0] == 3 else mine[chain[0]].at[layer], local.at[index])
+                made.place_own(mine[array] if array == 3 else mine[array].at[layer], local.at[index])
                 chains.append(made)
                 index += 1
             groups.append(chains)
-    for slot in range(7 + len(groups) - 1):
-        for g, chains in reversed(list(enumerate(groups))):
-            k = slot - g
-            if 0 <= k < 7:
-                for chain in chains:
-                    chain.step(k)
-
-
-def gather(att, up, down, small):
-    n_layers = att.shape[0]
-    n_chains = n_layers * 9 + 1
-    shapes = []
-    for _ in range(n_layers):
-        shapes += [(4, 2, 4, 2, 16, 4096), (4, 2, 4, 2, 16, 4096), (4, 2, 4, 2, 64, 1024)]
-    shapes.append((4, 2, 4, 2, 16, 256))
-    return pl.pallas_call(
-        functools.partial(gather_kernel, n_layers),
-        out_shape=[jax.ShapeDtypeStruct(s, BF) for s in shapes],
-        in_specs=[pl.BlockSpec(memory_space=pltpu.VMEM)] * 4,
-        out_specs=[pl.BlockSpec(memory_space=pl.ANY)] * len(shapes),
-        scratch_shapes=[
-            pltpu.SemaphoreType.DMA((n_chains, N_GATHER)),
-            pltpu.SemaphoreType.DMA((n_chains, N_GATHER)),
-            pltpu.SemaphoreType.DMA((n_chains,)),
-        ],
-        compiler_params=pltpu.CompilerParams(collective_id=0, has_side_effects=True),
-        name="gather_weights",
-    )(att, up, down, small)
+    return groups
 
 
 N_SCATTER = 12
@@ -479,6 +429,253 @@
     )(*args)
 
 
+LANES = 128
+GELU = 0.7978845608028654
+EPSILON = 1e-05
+ROWS = 256
+WIDTH = 1024
+HIDDEN = 4096
+HEADS = 16
+HEAD = 64
+BUCKETS = 32
+MASKED = -1e30
+
+
+def dot(a, b, ca=1, cb=0):
+    return lax.dot_general(a, b, (((ca,), (cb,)), ((), ())), preferred_element_type=F32)
+
+
+def iota(shape, dim):
+    return lax.broadcasted_iota(jnp.int32, shape, dim)
+
+
+def param_rows(small, layer):
+    flat = small[...].reshape(1024, 256)[:, :128]
+    chosen = (iota((64, 1024), 1) == iota((64, 1024), 0) * 16 + layer).astype(BF)
+    shares = dot(chosen, flat).astype(BF)
+    owner = iota((64, 1024), 0) == iota((64, 1024), 1) // 16
+    rows = []
+    for k in range(4):
+        spread = (iota((128, 1024), 0) == 16 * k + iota((128, 1024), 1) % 16).astype(BF)
+        rows.append(jnp.sum(jnp.where(owner, dot(shares, spread), 0.0), 0, keepdims=True))
+    return rows, shares
+
+
+def bias_rows(shares, bucket_rows):
+    picked = (iota((16, 128), 1) == 64 + iota((16, 128), 0) % 8).astype(BF)
+    entries = dot(picked, shares, 1, 1)
+    entries = jnp.where(iota((16, 64), 1) % 2 == iota((16, 64), 0) // 8, entries, 0.0).astype(BF)
+    return dot(entries, bucket_rows)
+
+
+def norm_parts(rows):
+    center = jnp.mean(rows, -1, keepdims=True)
+    centered = rows - center
+    inverse = lax.rsqrt(jnp.mean(centered * centered, -1, keepdims=True) + EPSILON)
+    return centered * inverse, inverse
+
+
+def norm_into(dst, src, gain, shift):
+    def body(i, _):
+        at = pl.ds(pl.multiple_of(i * 64, 64), 64)
+        normed, _unused = norm_parts(src[at, :])
+        dst[at, :] = (normed * gain[...] + shift[...]).astype(BF)
+        return 0
+
+    lax.fori_loop(0, ROWS // 64, body, 0)
+
+
+def attention_forward(qkv, probs, mixed, bias, allowed):
+    scale = HEAD ** (-0.5)
+    low = iota((ROWS, LANES), 1) < HEAD
+
+    def pair(i, _):
+        def columns(k):
+            return pl.ds(pl.multiple_of(k * WIDTH + i * LANES, LANES), LANES)
+
+        q, k, v = (qkv[:, columns(j)] for j in range(3))
+        halves = []
+        for side in range(2):
+            head = 2 * i + side
+            mine = jnp.where(low == (side == 0), q, jnp.zeros_like(q))
+            scores = dot(mine, k, 1, 1) * scale
+            first = bias[head]
+            shifted = jnp.concatenate([first] + [pltpu.roll(first, 16 * b, 1) for b in range(1, 16)], 0)
+            scores = jnp.where(allowed[...] > 0, scores + shifted, MASKED)
+            peak = jnp.max(scores, -1, keepdims=True)
+            terms = jnp.exp(scores - peak)
+            rounded = (terms / jnp.sum(terms, -1, keepdims=True)).astype(BF)
+            probs[head] = rounded
+            halves.append(dot(rounded, v))
+        mixed[:, pl.ds(pl.multiple_of(i * LANES, LANES), LANES)] = jnp.where(low, halves[0], halves[1]).astype(BF)
+        return 0
+
+    lax.fori_loop(0, HEADS // 2, pair, 0)
+
+
+def forward_kernel(att, up, down, small, tokens, seg_col, seg_row, bucket_rows, *rest):
+    outs, rest = rest[:16], rest[16:]
+    fetched = outs[:7]
+    o_acts, o_mid0, o_mid1, o_next, o_qkv, o_probs, o_mixed, o_active, o_slope = outs[7:]
+    (w_att, w_up, w_down, w_small, stream, middle, hidden, qkv, probs, mixed, active, slope, rounded,
+     bias, allowed, params, send, recv, local, loads, stores) = rest
+    at = place()
+    greet(at, PEERS)
+    groups = gather_groups(at, 2, (att, up, down, small), fetched, send, recv, local)
+    stored = []
+
+    def store(src, dst):
+        made = pltpu.make_async_copy(src, dst, stores.at[len(stored)])
+        made.start()
+        stored.append(made)
+
+    def load(i, src, dst):
+        made = pltpu.make_async_copy(src, dst, loads.at[i])
+        made.start()
+        return made
+
+    def slot(n):
+        for g, chains in reversed(list(enumerate(groups))):
+            k = n - g
+            if 0 <= k < 7:
+                for chain in chains:
+                    chain.step(k)
+
+    same = (seg_col[...] == seg_row[...]) & (iota((ROWS, ROWS), 0) >= iota((ROWS, ROWS), 1))
+    allowed[...] = same.astype(F32)
+    stream[0] = tokens[...].astype(F32)
+    for n in range(7):
+        slot(n)
+    load(0, fetched[6], w_small).wait()
+    for layer in range(2):
+        load(1, fetched[3 * layer], w_att).wait()
+        rows, shares = param_rows(w_small, layer)
+        for k in range(4):
+            params[layer, pl.ds(k, 1), :] = rows[k]
+        by_offset = bias_rows(shares, bucket_rows[...])
+        for head in range(HEADS):
+            wide = jnp.broadcast_to(by_offset[head : head + 1], (16, ROWS))
+            bias[head] = pltpu.roll(wide, 0, 1, stride=1, stride_axis=0)
+        here, mid = stream.at[layer], middle.at[layer]
+        row = lambda k: params.at[layer, pl.ds(k, 1), :]
+        norm_into(hidden, here, row(0), row(1))
+        wide_qkv, wide_probs, wide_mixed = qkv.at[layer], probs.at[layer], mixed.at[layer]
+        wide_active, wide_slope = active.at[layer], slope.at[layer]
+
+        def project(i, _):
+            cols = pl.ds(pl.multiple_of(i * 512, 512), 512)
+            weights = w_att[:, :, :, :, :, cols].reshape(WIDTH, 512)
+            wide_qkv[:, cols] = dot(hidden[...], weights).astype(BF)
+            return 0
+
+        lax.fori_loop(0, 6, project, 0)
+        attention_forward(wide_qkv, wide_probs, wide_mixed, bias, allowed)
+
+        def out_project(i, _):
+            cols = pl.ds(pl.multiple_of(i * 512, 512), 512)
+            from_cols = pl.ds(pl.multiple_of(3072 + i * 512, 512), 512)
+            weights = w_att[:, :, :, :, :, from_cols].reshape(WIDTH, 512)
+            mid[:, cols] = here[:, cols] + dot(wide_mixed[...], weights)
+            return 0
+
+        lax.fori_loop(0, 2, out_project, 0)
+        norm_into(hidden, mid, row(2), row(3))
+        store(wide_qkv, o_qkv.at[layer])
+        store(wide_probs, o_probs.at[layer])
+        store(wide_mixed, o_mixed.at[layer])
+        store(mid, (o_mid0, o_mid1)[layer])
+        slot(7 + 3 * layer)
+        load(2, fetched[3 * layer + 1], w_up).wait()
+
+        def expand(i, _):
+            cols = pl.ds(pl.multiple_of(i * 512, 512), 512)
+            weights = w_up[:, :, :, :, :, cols].reshape(WIDTH, 512)
+            u = dot(hidden[...], weights)
+            square = u * u
+            tangent = jnp.tanh(GELU * (u + 0.044715 * square * u))
+            wide_active[:, cols] = (0.5 * u * (1.0 + tangent)).astype(BF)
+            wide_slope[:, cols] = (
+                0.5 * (1.0 + tangent)
+                + 0.5 * u * (1.0 - tangent * tangent) * GELU * (1.0 + 3.0 * 0.044715 * square)
+            ).astype(BF)
+            return 0
+
+        lax.fori_loop(0, 8, expand, 0)
+        store(wide_active, o_active.at[layer])
+        store(wide_slope, o_slope.at[layer])
+        slot(8 + 3 * layer)
+        load(3, fetched[3 * layer + 2], w_down).wait()
+        acts = rounded.at[layer]
+
+        def contract(i, _):
+            cols = pl.ds(pl.multiple_of(i * 256, 256), 256)
+            weights = w_down[:, :, :, :, :, cols].reshape(HIDDEN, 256)
+            result = mid[:, cols] + dot(wide_active[...], weights)
+            if layer == 0:
+                stream[1, :, cols] = result
+            acts[:, cols] = result.astype(BF)
+            return 0
+
+        lax.fori_loop(0, 4, contract, 0)
+        store(acts, o_acts.at[layer])
+        if layer == 0:
+            store(stream.at[1], o_next)
+            slot(9)
+    for made in stored:
+        made.wait()
+
+
+def forward(att, up, down, small, tokens, seg_ids, bucket_rows):
+    lead = (4, 2, 4, 2)
+    gathered = [lead + (16, 4096), lead + (16, 4096), lead + (64, 1024)] * 2 + [lead + (16, 256)]
+    saved = [
+        ((2, ROWS, WIDTH), BF),
+        ((ROWS, WIDTH), F32),
+        ((ROWS, WIDTH), F32),
+        ((ROWS, WIDTH), F32),
+        ((2, ROWS, 3 * WIDTH), BF),
+        ((2, HEADS, ROWS, ROWS), BF),
+        ((2, ROWS, WIDTH), BF),
+        ((2, ROWS, HIDDEN), BF),
+        ((2, ROWS, HIDDEN), BF),
+    ]
+    vmem = pl.BlockSpec(memory_space=pltpu.VMEM)
+    hbm = pl.BlockSpec(memory_space=pl.ANY)
+    return pl.pallas_call(
+        forward_kernel,
+        out_shape=[jax.ShapeDtypeStruct(s, BF) for s in gathered] + [jax.ShapeDtypeStruct(s, t) for s, t in saved],
+        in_specs=[vmem] * 8,
+        out_specs=[hbm] * 16,
+        scratch_shapes=[
+            pltpu.VMEM(gathered[0], BF),
+            pltpu.VMEM(gathered[1], BF),
+            pltpu.VMEM(gathered[2], BF),
+            pltpu.VMEM(gathered[6], BF),
+            pltpu.VMEM((2, ROWS, WIDTH), F32),
+            pltpu.VMEM((2, ROWS, WIDTH), F32),
+            pltpu.VMEM((ROWS, WIDTH), BF),
+            pltpu.VMEM((2, ROWS, 3 * WIDTH), BF),
+            pltpu.VMEM((2, HEADS, ROWS, ROWS), BF),
+            pltpu.VMEM((2, ROWS, WIDTH), BF),
+            pltpu.VMEM((2, ROWS, HIDDEN), BF),
+            pltpu.VMEM((2, ROWS, HIDDEN), BF),
+            pltpu.VMEM((2, ROWS, WIDTH), BF),
+            pltpu.VMEM((HEADS, 16, ROWS), F32),
+            pltpu.VMEM((ROWS, ROWS), F32),
+            pltpu.VMEM((2, 8, WIDTH), F32),
+            pltpu.SemaphoreType.DMA((19, N_GATHER)),
+            pltpu.SemaphoreType.DMA((19, N_GATHER)),
+            pltpu.SemaphoreType.DMA((19,)),
+            pltpu.SemaphoreType.DMA((4,)),
+            pltpu.SemaphoreType.DMA((16,)),
+        ],
+        compiler_params=pltpu.CompilerParams(
+            collective_id=0, has_side_effects=True, vmem_limit_bytes=58 << 20
+        ),
+        name="gather_forward",
+    )(att, up, down, small, tokens, seg_ids[:, None], seg_ids[None, :], bucket_rows)
+
+
 def on_device(
     tokens,
     seg_ids,
@@ -496,58 +693,58 @@
     w_up,
     w_down,
 ):
-    length = tokens.shape[0]
-    model_width = tokens.shape[1]
+    length, width = ROWS, WIDTH
     score_scale = HEAD ** (-0.5)
     positions = jnp.arange(length, dtype=jnp.int32)
     distance = jnp.maximum(positions[:, None] - positions[None, :], 0)
     at_distance = (distance[:, :, None] == positions[None, None, :]).astype(jnp.bfloat16)
     bucket_of = (buckets[:, None] == jnp.arange(BUCKETS, dtype=jnp.int32)[None, :]).astype(jnp.bfloat16)
     onehot = jnp.dot(at_distance, bucket_of, preferred_element_type=jnp.float32).astype(jnp.bfloat16)
-    allowed = (positions[:, None] >= positions[None, :]) & (seg_ids[:, None] == seg_ids[None, :])
-
-    def masked_scores(queries, key_rows, rel_bias):
-        raw_scores = (
-            jnp.einsum("ihe,jhe->hij", queries, key_rows, preferred_element_type=jnp.float32)
-            * score_scale
-            + rel_bias
-        )
-        return jnp.where(allowed[None], raw_scores, -1e30)
-
-    def layer_backward(grad_result, saved_layer, layer_weights):
-        (
-            gain_one,
-            shift_one,
-            query_w,
-            key_w,
-            value_w,
-            out_w,
-            table,
-            gain_two,
-            shift_two,
-            up_w,
-            down_w,
-        ) = layer_weights
-        (
-            normed_one,
-            inverse_one,
-            input_one,
-            queries,
-            key_rows,
-            values,
-            rel_bias,
-            log_total,
-            mixed,
-            normed_two,
-            inverse_two,
-            input_two,
-            upward,
-            activated,
-        ) = saved_layer
+
+    small = jnp.stack(
+        [
+            jnp.concatenate([ln1_gain[i], ln1_bias[i], ln2_gain[i], ln2_bias[i], rel_table[i]])
+            for i in range(2)
+        ]
+    )
+    small = jnp.pad(small, ((0, 14), (0, 56)))
+    by_offset = jnp.concatenate([buckets[:1], buckets[:0:-1]])
+    bucket_rows = (by_offset[None, :] == (jnp.arange(64, dtype=jnp.int32) // 2)[:, None]).astype(BF)
+    done = forward(
+        jnp.concatenate([w_query, w_key, w_value, w_out], 2),
+        w_up,
+        w_down,
+        jnp.concatenate([small, small], 1),
+        tokens,
+        seg_ids,
+        bucket_rows,
+    )
+    fetched = done[:7]
+    acts, mid0, mid1, stream1, qkv_all, probs_all, mixed_all, active_all, slope_all = done[7:]
+    middles = (mid0, mid1)
+    streams = (tokens.astype(F32), stream1)
+    small_all = fetched[6].reshape(64, 16, 256)[:, :2, :128]
+
+    def heads_of(value):
+        return value.reshape(length, HEADS, HEAD)
+
+    def layer_backward(grad_result, layer_at):
+        att = fetched[3 * layer_at].reshape(1024, 4096)
+        up_w = fetched[3 * layer_at + 1].reshape(1024, 4096)
+        down_w = fetched[3 * layer_at + 2].reshape(4096, 1024)
+        mine = small_all[:, layer_at]
+        gain_one, shift_one, gain_two, shift_two = (mine[:, 16 * i : 16 * i + 16].reshape(1024) for i in range(4))
+        out_w = att[:, 3072:]
+        normed_one, inverse_one, hidden_one = normalize(streams[layer_at], gain_one, shift_one)
+        normed_two, inverse_two, hidden_two = normalize(middles[layer_at], gain_two, shift_two)
+        input_one, input_two = hidden_one.astype(BF), hidden_two.astype(BF)
+        queries, key_rows, values = (heads_of(qkv_all[layer_at][:, i * width : (i + 1) * width]) for i in range(3))
+        prob_rows = probs_all[layer_at]
+        mixed, activated, slope = mixed_all[layer_at], active_all[layer_at], slope_all[layer_at]
         down_in = grad_result.astype(jnp.bfloat16)
         grad_down = jnp.einsum("lf,ld->fd", activated, down_in, preferred_element_type=jnp.float32)
         grad_active = jnp.einsum("ld,fd->lf", down_in, down_w, preferred_element_type=jnp.float32)
-        grad_upward = (grad_active * gelu_slope(upward)).astype(jnp.bfloat16)
+        grad_upward = (grad_active * slope.astype(F32)).astype(jnp.bfloat16)
         grad_up = jnp.einsum(
             "ld,lf->df", input_two, grad_upward, preferred_element_type=jnp.float32
         )
@@ -561,8 +758,6 @@
         grad_out_w = jnp.einsum("ld,le->de", mixed, branch_in, preferred_element_type=jnp.float32)
         grad_mixed = jnp.einsum("le,de->ld", branch_in, out_w, preferred_element_type=jnp.float32)
         grad_mixed = grad_mixed.astype(jnp.bfloat16).reshape(length, HEADS, HEAD)
-        scores = masked_scores(queries, key_rows, rel_bias)
-        prob_rows = jnp.exp(scores - log_total)
         grad_probs = jnp.einsum(
             "ihe,jhe->hij", grad_mixed, values, preferred_element_type=jnp.float32
         )
@@ -572,9 +767,9 @@
             grad_mixed,
             preferred_element_type=jnp.float32,
         )
-        grad_values = grad_values.astype(jnp.bfloat16).reshape(length, model_width)
+        grad_values = grad_values.astype(jnp.bfloat16).reshape(length, width)
         grad_scores = (
-            prob_rows * (grad_probs - jnp.sum(prob_rows * grad_probs, -1, keepdims=True))
+            prob_rows.astype(F32) * (grad_probs - jnp.sum(prob_rows.astype(F32) * grad_probs, -1, keepdims=True))
         ).astype(jnp.bfloat16)
         grad_queries = (
             (
@@ -584,7 +779,7 @@
                 * score_scale
             )
             .astype(jnp.bfloat16)
-            .reshape(length, model_width)
+            .reshape(length, width)
         )
         grad_keys = (
             (
@@ -592,22 +787,14 @@
                 * score_scale
             )
             .astype(jnp.bfloat16)
-            .reshape(length, model_width)
+            .reshape(length, width)
         )
         grad_bias_table = jnp.einsum(
             "hij,ijb->bh", grad_scores, onehot, preferred_element_type=jnp.float32
         ).reshape(BUCKETS * HEADS)
         grad_all = jnp.concatenate([grad_queries, grad_keys, grad_values], 1)
         grad_qkv = jnp.einsum("ld,le->de", input_one, grad_all, preferred_element_type=jnp.float32)
-        grad_hidden_one = jnp.einsum(
-            "le,de->ld", grad_queries, query_w, preferred_element_type=jnp.float32
-        )
-        grad_hidden_one = grad_hidden_one + jnp.einsum(
-            "le,de->ld", grad_keys, key_w, preferred_element_type=jnp.float32
-        )
-        grad_hidden_one = grad_hidden_one + jnp.einsum(
-            "le,de->ld", grad_values, value_w, preferred_element_type=jnp.float32
-        )
+        grad_hidden_one = jnp.einsum("le,de->ld", grad_all, att[:, :3072], preferred_element_type=jnp.float32)
         grad_gain_one = jnp.sum(grad_hidden_one * normed_one, 0)
         grad_shift_one = jnp.sum(grad_hidden_one, 0)
         grad_stream = grad_middle + norm_back(grad_hidden_one, normed_one, inverse_one, gain_one)
@@ -626,128 +813,15 @@
         grads = tuple(g.astype(BF) for g in (grad_qkv, grad_out_w, grad_up, grad_down, small))
         return (grad_stream, grads)
 
-    def shares(layer_at):
-        return jnp.concatenate(
-            [ln1_gain[layer_at], ln1_bias[layer_at], ln2_gain[layer_at], ln2_bias[layer_at], rel_table[layer_at]]
-        )
-
-    small = jnp.stack([shares(0), shares(1)])
-    small = jnp.pad(small, ((0, 14), (0, 56)))
-    fetched = gather(jnp.concatenate([w_query, w_key, w_value, w_out], 2), w_up, w_down, jnp.concatenate([small, small], 1))
-    small_all = fetched[6].reshape(64, 16, 256)[:, :2, :128]
-
-    def weights_of(layer_at):
-        att = fetched[3 * layer_at].reshape(1024, 4096)
-        up = fetched[3 * layer_at + 1].reshape(1024, 4096)
-        down = fetched[3 * layer_at + 2].reshape(4096, 1024)
-        mine = small_all[:, layer_at]
-        return (
-            mine[:, 0:16].reshape(1024),
-            mine[:, 16:32].reshape(1024),
-            att[:, :1024],
-            att[:, 1024:2048],
-            att[:, 2048:3072],
-            att[:, 3072:],
-            mine[:, 64:72].reshape(512),
-            mine[:, 32:48].reshape(1024),
-            mine[:, 48:64].reshape(1024),
-            up,
-            down,
-        )
-
-    stream = tokens.astype(jnp.float32)
-    saved_all = []
-    layer_acts = []
-    for layer_at in range(2):
-        layer_weights = weights_of(layer_at)
-        (
-            layer_gain_one,
-            layer_shift_one,
-            layer_query_w,
-            layer_key_w,
-            layer_value_w,
-            layer_out_w,
-            layer_table,
-            layer_gain_two,
-            layer_shift_two,
-            layer_up_w,
-            layer_down_w,
-        ) = layer_weights
-        layer_normed_one, layer_inverse_one, hidden_one = normalize(
-            stream, layer_gain_one, layer_shift_one
-        )
-        layer_input_one = hidden_one.astype(jnp.bfloat16)
-        layer_queries = (
-            jnp.dot(layer_input_one, layer_query_w, preferred_element_type=jnp.float32)
-            .astype(jnp.bfloat16)
-            .reshape(length, HEADS, HEAD)
-        )
-        layer_key_rows = (
-            jnp.dot(layer_input_one, layer_key_w, preferred_element_type=jnp.float32)
-            .astype(jnp.bfloat16)
-            .reshape(length, HEADS, HEAD)
-        )
-        layer_values = (
-            jnp.dot(layer_input_one, layer_value_w, preferred_element_type=jnp.float32)
-            .astype(jnp.bfloat16)
-            .reshape(length, HEADS, HEAD)
-        )
-        layer_rel_bias = jnp.einsum(
-            "ijb,bh->hij",
-            onehot,
-            layer_table.reshape(BUCKETS, HEADS),
-            preferred_element_type=jnp.float32,
-        )
-        layer_scores = masked_scores(layer_queries, layer_key_rows, layer_rel_bias)
-        row_peak = jnp.max(layer_scores, -1, keepdims=True)
-        exp_terms = jnp.exp(layer_scores - row_peak)
-        totals = jnp.sum(exp_terms, -1, keepdims=True)
-        layer_prob_rows = exp_terms / totals
-        layer_log_total = row_peak + jnp.log(totals)
-        layer_mixed = jnp.einsum(
-            "hij,jhe->ihe",
-            layer_prob_rows.astype(jnp.bfloat16),
-            layer_values,
-            preferred_element_type=jnp.float32,
-        )
-        layer_mixed = layer_mixed.reshape(length, model_width).astype(jnp.bfloat16)
-        middle = stream + jnp.dot(layer_mixed, layer_out_w, preferred_element_type=jnp.float32)
-        layer_normed_two, layer_inverse_two, hidden_two = normalize(
-            middle, layer_gain_two, layer_shift_two
-        )
-        layer_input_two = hidden_two.astype(jnp.bfloat16)
-        layer_upward = jnp.dot(layer_input_two, layer_up_w, preferred_element_type=jnp.float32)
-        layer_activated = smooth_gelu(layer_upward).astype(jnp.bfloat16)
-        result = middle + jnp.dot(layer_activated, layer_down_w, preferred_element_type=jnp.float32)
-        layer_saved_layer = (
-            layer_normed_one,
-            layer_inverse_one,
-            layer_input_one,
-            layer_queries,
-            layer_key_rows,
-            layer_values,
-            layer_rel_bias,
-            layer_log_total,
-            layer_mixed,
-            layer_normed_two,
-            layer_inverse_two,
-            layer_input_two,
-            layer_upward,
-            layer_activated,
-        )
-        stream = result
-        saved_layer = layer_saved_layer
-        saved_all.append(saved_layer)
-        layer_acts.append(stream.astype(jnp.bfloat16))
     grad_stream = cotangent.astype(jnp.float32)
     reduced = [None, None]
     for layer_at in (1, 0):
-        grad_stream, grads = layer_backward(grad_stream, saved_all[layer_at], weights_of(layer_at))
+        grad_stream, grads = layer_backward(grad_stream, layer_at)
         reduced[layer_at] = scatter(*grads)
     stacked = [jnp.stack([reduced[0][i], reduced[1][i]]) for i in range(4)]
     att, up, down, small = stacked
     return (
-        jnp.stack(layer_acts),
+        acts,
         grad_stream,
         small[:, 0, 0:16],
         small[:, 0, 16:32],

time: 523 us -> 498 us (0.952)
  matrix products: 178 us -> 124 us
  Pallas kernels: 269 us -> 305 us
  local copies, waits for them, and re-layouts: 41.4 us -> 34.2 us
    dot_general x24 -> x2, matrix products: 77.2 us -> 10.3 us  [layer_backward(): jnp.einsum('le,de->ld', grad_all, att[:, :3072], preferred_element_type=j...]
    pallas_call x1, Pallas kernels: 112 us -> 150 us  [forward(): pl.pallas_call(forward_kernel, out_shape=[jax.ShapeDtypeStruct(s, BF) for...]
    dot_general x2 -> x0, local copies, waits for them, and re-layouts: 21.6 us -> none  [on_device(): jnp.einsum('ijb,bh->hij', onehot, layer_table.reshape(BUCKETS, HEADS), pr...]
    slice x3 -> x11, local copies, waits for them, and re-layouts: 1.19 us -> 15.9 us  [the longest x8 12.9 us: layer_backward(): qkv_all[layer_at][:, i * width:(i + 1) * width]]
    dot_general x2, matrix products: 5.39 us -> 13.7 us  [layer_backward(): jnp.einsum('lf,df->ld', grad_upward, up_w, preferred_element_type=jnp.flo...]
    convert_element_type x12 -> x4, local copies, waits for them, and re-layouts: 7.92 us -> 0.3 us  [norm_back(): scaled = grad_hidden * gain.astype(jnp.float32)]
where the time goes in v2:
time: 498 us; the launch traced here: 490 us
  Pallas kernels  305 us (61%)
  matrix products  124 us (25%)
  local copies, waits for them, and re-layouts  34.2 us (7%)
  other arithmetic  24.5 us (5%)
    pallas_call x2, Pallas kernels, scatter(): pl.pallas_call(scatter_kernel, out_shape=[jax.ShapeDtypeStruct(s, F32) fo...  155 us
    pallas_call x1, Pallas kernels, forward(): pl.pallas_call(forward_kernel, out_shape=[jax.ShapeDtypeStruct(s, BF) for...  150 us
    dot_general x1, matrix products, on_device(): jnp.dot(at_distance, bucket_of, preferred_element_type=jnp.float32)  16.9 us
    dot_general x2, matrix products, layer_backward(): jnp.einsum('lf,df->ld', grad_upward, up_w, preferred_element_type=jnp.flo...  13.7 us
    dot_general x2, matrix products, layer_backward(): jnp.einsum('ld,lf->df', input_two, grad_upward, preferred_element_type=jn...  13.2 us
    dot_general x2, matrix products, layer_backward(): jnp.einsum('ld,fd->lf', down_in, down_w, preferred_element_type=jnp.float32)  13.1 us
    slice x8, local copies, waits for them, and re-layouts, layer_backward(): qkv_all[layer_at][:, i * width:(i + 1) * width]  12.9 us
    dot_general x2, matrix products, layer_backward(): jnp.einsum('lf,ld->fd', activated, down_in, preferred_element_type=jnp.fl...  11.2 us

profile of v2, /device:TPU:0, one launch (start us, length us, event | category | flops | bytes accessed | tf_op | source)
XLA Modules:
  0.0 490.1 jit_solution(7949506739402668678)
XLA Ops:
  0.7 1.7 pad_maximum_fusion.10.att
  5.4 1.5 copy.45.seg_col
  10.4 150.0 %gather_forward.1 = (bf16[4,2,4,2,16,4096]{5,4,3,2,1,0:T(8,128)(2,1)}, bf16[4,2,4,2,16,4096]{5,4,3,2,1,0:T(8,128)(2,1)}, bf16[4,2,4,2,64,1024]{5,4,3,2,1,0:T(8,1...) custom-call(bf16[2,16,4096]{2,1,0:T(8,128)(2,1)} %pad_maximum_fusion, ...), custom_call_target="tpu_custom_call" | custom-call | tf_op jit(solution)/shard_map/gather_forward/pallas_call | solution.py:644
  160.5 1.4 reduce_sum.234
  161.8 1.5 multiply_reduce_fusion.8
  164.5 6.4 %fusion.7 = bf16[256,4096]{1,0:T(8,128)(2,1)S(1)} fusion(bf16[4096,1024]{1,0:T(8,128)(2,1)} %bitcast.233, bf16[256,1024]{1,0:T(8,128)(2,1)S(1)} %copy-done.27, bf16[2,256,4096]{2,1,0:T(8,128)(2,1)} %get-tuple-element.40), kind=kOutput, calls=%fused_computation.20 | convolution fusion | flops 2150629376 | bytes 13107200 | tf_op jit(solution)/shard_map/ld,fd->lf/dot_general | solution.py:746
  171.0 6.8 %multiply_reduce_fusion = (bf16[1024]{0:T(1024)(128)(2,1)S(1)}, f32[256]{0:T(256)S(1)}, f32[256]{0:T(256)S(1)}, bf16[1024]{0:T(1024)(128)(2,1)S(1)}, f32[256,1024]{1,0:T(8,128)S(1)}) fusion(f32[256,1024]{1,0:T(8,128)S(1)} %copy-done.2, f32[256]{0:T(256)S(1)} %add_rsqrt_fusion.3, f32[256]{0:T(256)S(1)} %broadcast_multiply_fusion.11, f32[1024]{0:T(1024)S(1)} %reshape.359, ...), kind=kOutput, calls=%fused_computation.81 | convolution fusion | flops 2149840384 | bytes 12595200 | tf_op jit(solution)/shard_map/lf,df->ld/dot_general | solution.py:751
  179.6 3.1 fusion.38
  182.7 2.0 copy.49
  184.7 3.2 fusion.32
  187.9 1.3 slice_bitcast_fusion
  192.6 2.8 fusion.9
  196.7 1.3 copy-done.5
  198.5 2.2 copy.48
  200.7 2.5 fusion.44
  203.3 5.1 %multiply_reduce_fusion.1 = (bf16[1024]{0:T(1024)(128)(2,1)S(1)}, f32[256]{0:T(256)S(1)}, f32[256]{0:T(256)S(1)}, bf16[1024]{0:T(1024)(128)(2,1)S(1)}, f32[256,1024]{1,0:T(8,128)S(1)}) fusion(f32[256,1024]{1,0:T(8,128)S(1)} %copy-done.4, f32[256]{0:T(256)S(1)} %add_rsqrt_fusion.2, f32[256]{0:T(256)S(1)} %broadcast_multiply_fusion.8, ...), kind=kOutput, calls=%fused_computation.82 | convolution fusion | flops 1617688064 | bytes 9973760 | tf_op jit(solution)/shard_map/le,de->ld/dot_general | solution.py:797
  208.5 1.4 multiply_add_fusion.1
  210.4 6.7 %fusion.8 = bf16[256,4096]{1,0:T(8,128)(2,1)S(1)} fusion(bf16[4096,1024]{1,0:T(8,128)(2,1)} %bitcast.229, bf16[2,256,4096]{2,1,0:T(8,128)(2,1)} %get-tuple-element.40, f32[256,1024]{1,0:T(8,128)} %multiply_add_fusion.1), kind=kOutput, calls=%fused_computation.21 | convolution fusion | flops 2150891520 | bytes 13631488 | tf_op jit(solution)/shard_map/ld,fd->lf/dot_general | solution.py:746
  217.1 6.8 %multiply_reduce_fusion.2 = (bf16[1024]{0:T(1024)(128)(2,1)S(1)}, f32[256]{0:T(256)S(1)}, f32[256]{0:T(256)S(1)}, bf16[1024]{0:T(1024)(128)(2,1)S(1)}, f32[256,1024]{1,0:T(8,128)S(1)}) fusion(f32[256,1024]{1,0:T(8,128)S(1)} %copy-done.3, f32[256]{0:T(256)S(1)} %add_rsqrt_fusion.1, f32[256]{0:T(256)S(1)} %broadcast_multiply_fusion.5, ...), kind=kOutput, calls=%fused_computation.85 | convolution fusion | flops 2149840384 | bytes 12595200 | tf_op jit(solution)/shard_map/lf,df->ld/dot_general | solution.py:751
  224.0 1.4 multiply_add_fusion
  225.9 3.5 fusion.41
  229.4 2.0 copy.56
  231.5 3.1 fusion.35
  235.8 2.0 copy.60
  237.9 2.1 copy.57
  239.9 3.1 fusion.11
  246.6 2.0 copy.55
  248.6 2.6 fusion.46
  251.3 5.2 %fusion.66 = (bf16[1024]{0:T(1024)(128)(2,1)S(1)}, f32[256]{0:T(256)S(1)}, f32[256]{0:T(256)S(1)}, bf16[1024]{0:T(1024)(128)(2,1)S(1)}, f32[256,1024]{1,0:T(8,128)S(1)}) fusion(bf16[256,1024]{1,0:T(8,128)(2,1)S(1)} %copy-done.17, f32[256]{0:T(256)S(1)} %add_rsqrt_fusion, f32[256]{0:T(256)S(1)} %broadcast_multiply_fusion.2, f32[1024]{0:T(1024)S(1)} %reshape.363, ...), kind=kOutput, calls=%fused_computation.79 | convolution fusion | flops 1617950208 | bytes 9449472 | tf_op jit(solution)/shard_map/le,de->ld/dot_general | solution.py:797
  256.5 1.4 fusion.63
  258.0 6.2 %convolution_convert_fusion.4 = bf16[1024,3072]{1,0:T(8,128)(2,1)} fusion(bf16[256,1024]{0,1:T(8,128)(2,1)} %bitcast.183, bf16[256,1024]{0,1:T(8,128)(2,1)} %bitcast.186, bf16[256,1024]{0,1:T(8,128)(2,1)} %bitcast.188, f32[256,1024]{1,0:T(8,128)S(1)} %copy-done.4, f32[1024]{0:T(1024)S(1)} %reshape.367, f32[1024]{0:T(1024)S(1)} %reshape.360, ...), kind=kOutput, calls=%fused_computation.11 | convolution fusion | flops 1619787776 | bytes 8923136 | tf_op jit(solution)/shard_map/ld,le->de/dot_general | solution.py:796
  264.2 2.0 convolution_convert_fusion.6
  266.3 7.5 %convolution_convert_fusion.1 = bf16[1024,4096]{1,0:T(8,128)(2,1)} fusion(bf16[256,4096]{1,0:T(8,128)(2,1)} %copy-done.24, f32[256,1024]{1,0:T(8,128)S(1)} %copy-done.2, f32[1024]{0:T(1024)S(1)} %reshape.368, f32[1024]{0:T(1024)S(1)} %reshape.359, f32[256]{0:T(256)S(1)} %add_rsqrt_fusion.3, f32[256]{0:T(256)S(1)} %broadcast_multiply_fusion.11), kind=kOutput, calls=%fused_computation.4 | convolution fusion | flops 2152988672 | bytes 11544576 | tf_op jit(solution)/shard_map/ld,lf->df/dot_general | solution.py:748
  273.8 5.6 %convolution_convert_fusion = bf16[4096,1024]{1,0:T(8,128)(2,1)} fusion(bf16[256,1024]{1,0:T(8,128)(2,1)S(1)} %copy-done.29, bf16[2,256,4096]{2,1,0:T(8,128)(2,1)S(1)} %copy-done.19), kind=kOutput, calls=%fused_computation.3 | convolution fusion | flops 2151677952 | bytes 11010048 | tf_op jit(solution)/shard_map/lf,ld->fd/dot_general | solution.py:745
  279.8 16.9 %fusion.13 = bf16[256,256,32]{1,2,0:T(8,128)(2,1)S(1)} fusion(s32[256,256]{1,0:T(8,128)S(1)} %subtract_maximum_fusion, pred[256,32,1]{0,1,2:T(32,128)(4,1)S(1)} %fusion.143), kind=kOutput, calls=%fused_computation.26 | convolution fusion | flops 1092616192 | bytes 4464640 | tf_op jit(solution)/shard_map/dot_general | solution.py:702
  296.7 2.0 copy-done.49
  298.7 1.5 fusion.57
  301.5 77.1 %scatter_grads.3 = (f32[16,4096]{1,0:T(8,128)}, f32[16,4096]{1,0:T(8,128)}, f32[64,1024]{1,0:T(8,128)}, f32[16,256]{1,0:T(8,128)}) custom-call(bf16[4,2,4,2,16,3072]{5,4,3,2,1,0:T(8,128)(2,1)} %bitcast.173, bf16[4,2,4,2,16,1024]{5,4,3,2,1,0:T(8,128)(2,1)} %bitcast.174, bf16[4,2,4,2,16,4096]{5,4,3,2,1,0:T(8,128)(2,1)} %bitcast.171, ...), custom_call_target="tpu_custom_call" | custom-call | tf_op jit(solution)/shard_map/scatter_grads/pallas_call | solution.py:421
  378.7 4.7 convolution_convert_fusion.5
  383.4 2.1 convolution_convert_fusion.7
  385.6 5.7 %convolution_convert_fusion.3 = bf16[1024,4096]{1,0:T(8,128)(2,1)} fusion(bf16[256,4096]{1,0:T(8,128)(2,1)S(1)} %copy-done.26, f32[256,1024]{1,0:T(8,128)S(1)} %copy-done.3, f32[1024]{0:T(1024)S(1)} %reshape.365, f32[1024]{0:T(1024)S(1)} %reshape.362, f32[256]{0:T(256)S(1)} %add_rsqrt_fusion.1, f32[256]{0:T(256)S(1)} %broadcast_multiply_fusion.5), kind=kOutput, calls=%fused_computation.6 | convolution fusion | flops 2152988672 | bytes 11544576 | tf_op jit(solution)/shard_map/ld,lf->df/dot_general | solution.py:748
  391.4 5.6 %convolution_convert_fusion.2 = bf16[4096,1024]{1,0:T(8,128)(2,1)} fusion(bf16[2,256,4096]{2,1,0:T(8,128)(2,1)S(1)} %copy-done.20, f32[256,1024]{1,0:T(8,128)S(1)} %copy-done.15), kind=kOutput, calls=%fused_computation.5 | convolution fusion | flops 2151940096 | bytes 11534336 | tf_op jit(solution)/shard_map/lf,ld->fd/dot_general | solution.py:745
  397.3 3.6 fusion.54
  402.3 78.3 %scatter_grads.2 = (f32[16,4096]{1,0:T(8,128)}, f32[16,4096]{1,0:T(8,128)}, f32[64,1024]{1,0:T(8,128)}, f32[16,256]{1,0:T(8,128)}) custom-call(bf16[4,2,4,2,16,3072]{5,4,3,2,1,0:T(8,128)(2,1)} %bitcast.176, bf16[4,2,4,2,16,1024]{5,4,3,2,1,0:T(8,128)(2,1)} %bitcast.175, bf16[4,2,4,2,16,4096]{5,4,3,2,1,0:T(8,128)(2,1)} %bitcast.172, ...), custom_call_target="tpu_custom_call" | custom-call | tf_op jit(solution)/shard_map/scatter_grads/pallas_call | solution.py:421
  480.6 1.5 pad_maximum_fusion.13
  482.1 1.7 pad_maximum_fusion.11
  485.1 1.8 pad_maximum_fusion.8
  486.9 1.8 pad_maximum_fusion.9
  (178 shorter events, 26.3 us)
Async XLA Ops:
  0.6 163.9 %copy-start.27 = (bf16[256,1024]{1,0:T(8,128)(2,1)S(1)}, bf16[256,1024]{1,0:T(8,128)(2,1)}, u32[]{:S(2)}) copy-start(bf16[256,1024]{1,0:T(8,128)(2,1)} %param.18) | copy-start | bytes 1572868
  164.5 6.5 %copy-start.2 = (f32[256,1024]{1,0:T(8,128)S(1)}, f32[256,1024]{1,0:T(8,128)}, u32[]{:S(2)}) copy-start(f32[256,1024]{1,0:T(8,128)} %get-tuple-element.38) | copy-start | bytes 3145732
  171.0 6.9 %copy-start.24 = (bf16[256,4096]{1,0:T(8,128)(2,1)}, bf16[256,4096]{1,0:T(8,128)(2,1)S(1)}, u32[]{:S(2)}) copy-start(bf16[256,4096]{1,0:T(8,128)(2,1)S(1)} %fusion.7) | copy-start | bytes 6291460
  171.0 6.9 %copy-start.28 = (bf16[256,1024]{1,0:T(8,128)(2,1)S(1)}, bf16[256,1024]{1,0:T(8,128)(2,1)}, u32[]{:S(2)}) copy-start(bf16[256,1024]{1,0:T(8,128)(2,1)} %param.18) | copy-start | bytes 1572868
  178.3 6.4 %copy-start.9 = (f32[256,1024]{1,0:T(8,128)}, f32[256,1024]{1,0:T(8,128)S(1)}, u32[]{:S(2)}) copy-start(f32[256,1024]{1,0:T(8,128)S(1)} %multiply_add_fusion.2) | copy-start | bytes 3145732
  184.7 3.2 copy-start.23
  189.3 3.4 copy-start.22
  192.6 2.8 copy-start
  195.5 2.6 copy-start.34
  196.7 1.4 copy-start.5
  198.0 5.3 %copy-start.30 = (bf16[16,64,256]{2,1,0:T(8,128)(2,1)S(1)}, bf16[16,64,256]{2,1,0:T(8,128)(2,1)}, u32[]{:S(2)}) copy-start(bf16[16,64,256]{2,1,0:T(8,128)(2,1)} %fusion.32) | copy-start | bytes 1572868
  198.5 4.8 copy-start.31
  203.3 5.2 %copy-start.32 = (bf16[16,64,256]{2,1,0:T(8,128)(2,1)}, bf16[16,64,256]{2,1,0:T(8,128)(2,1)S(1)}, u32[]{:S(2)}) copy-start(bf16[16,64,256]{2,1,0:T(8,128)(2,1)S(1)} %fusion.44) | copy-start | bytes 1572868
  203.3 5.2 %copy-start.10 = (f32[256,1024]{1,0:T(8,128)S(1)}, f32[256,1024]{1,0:T(8,128)}, u32[]{:S(2)}) copy-start(f32[256,1024]{1,0:T(8,128)} %copy-done.9) | copy-start | bytes 3145732
  208.4 1.4 copy-start.3
  217.1 6.9 %copy-start.25 = (bf16[256,4096]{1,0:T(8,128)(2,1)}, bf16[256,4096]{1,0:T(8,128)(2,1)S(1)}, u32[]{:S(2)}) copy-start(bf16[256,4096]{1,0:T(8,128)(2,1)S(1)} %fusion.8) | copy-start | bytes 6291460
  217.1 6.9 %copy-start.14 = (f32[256,1024]{1,0:T(8,128)S(1)}, f32[256,1024]{1,0:T(8,128)}, u32[]{:S(2)}) copy-start(f32[256,1024]{1,0:T(8,128)} %multiply_add_fusion.1) | copy-start | bytes 3145732
  224.0 1.4 copy-start.16
  231.5 3.1 copy-start.21
  239.9 3.1 copy-start.1
  243.1 2.2 copy-start.33
  248.6 2.6 copy-start.17
  248.6 2.6 copy-start.38
  248.6 2.7 copy-start.40
  251.2 5.2 %copy-start.42 = (bf16[16,64,256]{2,1,0:T(8,128)(2,1)}, bf16[16,64,256]{2,1,0:T(8,128)(2,1)S(1)}, u32[]{:S(2)}) copy-start(bf16[16,64,256]{2,1,0:T(8,128)(2,1)S(1)} %fusion.46) | copy-start | bytes 1572868
  251.3 5.2 %copy-start.12 = (f32[256,1024]{1,0:T(8,128)S(1)}, f32[256,1024]{1,0:T(8,128)}, u32[]{:S(2)}) copy-start(f32[256,1024]{1,0:T(8,128)} %multiply_add_fusion) | copy-start | bytes 3145732
  258.0 6.2 %copy-start.11 = (f32[256,1024]{1,0:T(8,128)S(1)}, f32[256,1024]{1,0:T(8,128)}, u32[]{:S(2)}) copy-start(f32[256,1024]{1,0:T(8,128)} %copy-done.9) | copy-start | bytes 3145732
  258.0 6.2 %copy-start.35 = (bf16[2,256,1024]{2,1,0:T(8,128)(2,1)S(1)}, bf16[2,256,1024]{2,1,0:T(8,128)(2,1)}, u32[]{:S(2)}) copy-start(bf16[2,256,1024]{2,1,0:T(8,128)(2,1)} %get-tuple-element.51) | copy-start | bytes 3145732
  266.3 7.5 %copy-start.19 = (bf16[2,256,4096]{2,1,0:T(8,128)(2,1)S(1)}, bf16[2,256,4096]{2,1,0:T(8,128)(2,1)}, u32[]{:S(2)}) copy-start(bf16[2,256,4096]{2,1,0:T(8,128)(2,1)} %get-tuple-element.52) | copy-start | bytes 12582916
  266.3 7.5 %copy-start.29 = (bf16[256,1024]{1,0:T(8,128)(2,1)S(1)}, bf16[256,1024]{1,0:T(8,128)(2,1)}, u32[]{:S(2)}) copy-start(bf16[256,1024]{1,0:T(8,128)(2,1)} %param.18) | copy-start | bytes 1572868
  273.8 6.0 %copy-start.48 = (s32[256]{0:T(256)S(1)}, s32[256]{0:T(256)}, u32[]{:S(2)}) copy-start(s32[256]{0:T(256)} %param.17) | copy-start | bytes 3076
  279.8 18.9 %copy-start.6 = (bf16[16,256,256]{2,1,0:T(8,128)(2,1)S(1)}, bf16[16,256,256]{2,1,0:T(8,128)(2,1)}, u32[]{:S(2)}) copy-start(bf16[16,256,256]{2,1,0:T(8,128)(2,1)} %copy-done.5) | copy-start | bytes 6291460
  296.7 2.0 copy-start.49
  301.5 77.2 %copy-start.18 = (bf16[256,1024]{1,0:T(8,128)(2,1)S(1)}, bf16[256,1024]{1,0:T(8,128)(2,1)}, u32[]{:S(2)}) copy-start(bf16[256,1024]{1,0:T(8,128)(2,1)} %tokens.1) | copy-start | bytes 1572868
  301.5 77.2 %copy-start.39 = (bf16[16,64,256]{2,1,0:T(8,128)(2,1)S(1)}, bf16[16,64,256]{2,1,0:T(8,128)(2,1)}, u32[]{:S(2)}) copy-start(bf16[16,64,256]{2,1,0:T(8,128)(2,1)} %fusion.35) | copy-start | bytes 1572868
  301.5 77.2 %copy-start.41 = (bf16[16,64,256]{2,1,0:T(8,128)(2,1)S(1)}, bf16[16,64,256]{2,1,0:T(8,128)(2,1)}, u32[]{:S(2)}) copy-start(bf16[16,64,256]{2,1,0:T(8,128)(2,1)} %fusion.47) | copy-start | bytes 1572868
  301.5 77.2 %copy-start.43 = (bf16[16,64,256]{2,1,0:T(8,128)(2,1)S(1)}, bf16[16,64,256]{2,1,0:T(8,128)(2,1)}, u32[]{:S(2)}) copy-start(bf16[16,64,256]{2,1,0:T(8,128)(2,1)} %copy-done.42) | copy-start | bytes 1572868
  378.7 4.8 copy-start.13
  378.7 4.7 copy-start.36
  383.4 2.2 copy-start.26
  385.6 5.8 %copy-start.15 = (f32[256,1024]{1,0:T(8,128)S(1)}, f32[256,1024]{1,0:T(8,128)}, u32[]{:S(2)}) copy-start(f32[256,1024]{1,0:T(8,128)} %multiply_add_fusion.1) | copy-start | bytes 3145732
  385.6 5.8 %copy-start.20 = (bf16[2,256,4096]{2,1,0:T(8,128)(2,1)S(1)}, bf16[2,256,4096]{2,1,0:T(8,128)(2,1)}, u32[]{:S(2)}) copy-start(bf16[2,256,4096]{2,1,0:T(8,128)(2,1)} %get-tuple-element.52) | copy-start | bytes 12582916
  391.4 5.9 %copy-start.8 = (bf16[16,256,256]{2,1,0:T(8,128)(2,1)S(1)}, bf16[16,256,256]{2,1,0:T(8,128)(2,1)}, u32[]{:S(2)}) copy-start(bf16[16,256,256]{2,1,0:T(8,128)(2,1)} %copy-done.7) | copy-start | bytes 6291460
  402.3 78.3 %copy-start.47 = (f32[16,256]{1,0:T(8,128)S(1)}, f32[16,256]{1,0:T(8,128)}, u32[]{:S(2)}) copy-start(f32[16,256]{1,0:T(8,128)} %get-tuple-element.54) | copy-start | bytes 49156
  402.3 79.8 %copy-start.46 = (f32[16,4096]{1,0:T(8,128)S(1)}, f32[16,4096]{1,0:T(8,128)}, u32[]{:S(2)}) copy-start(f32[16,4096]{1,0:T(8,128)} %get-tuple-element.56) | copy-start | bytes 786436
  402.3 82.9 %copy-start.45 = (f32[16,4096]{1,0:T(8,128)S(1)}, f32[16,4096]{1,0:T(8,128)}, u32[]{:S(2)}) copy-start(f32[16,4096]{1,0:T(8,128)} %get-tuple-element.58) | copy-start | bytes 786436
  402.3 84.7 %copy-start.44 = (f32[64,1024]{1,0:T(8,128)S(1)}, f32[64,1024]{1,0:T(8,128)}, u32[]{:S(2)}) copy-start(f32[64,1024]{1,0:T(8,128)} %get-tuple-element.60) | copy-start | bytes 786436
  480.6 8.1 %copy-start.37 = (bf16[2,256,1024]{2,1,0:T(8,128)(2,1)S(1)}, bf16[2,256,1024]{2,1,0:T(8,128)(2,1)}, u32[]{:S(2)}) copy-start(bf16[2,256,1024]{2,1,0:T(8,128)(2,1)} %get-tuple-element.138) | copy-start | bytes 3145732
  (2 other events, 2.5 us)

commit v3 on v2

--- a/solution.py
+++ b/solution.py
@@ -1,33 +1,9 @@
-import functools
-
 import jax
 import jax.numpy as jnp
 from jax import lax
 from jax.experimental import pallas as pl
 from jax.experimental.pallas import tpu as pltpu
 from jax.sharding import PartitionSpec as P
-
-epsilon = 1e-05
-gelu_coef = 0.7978845608028654
-
-
-def normalize(stream, gain, shift):
-    center = jnp.mean(stream, -1, keepdims=True)
-    centered = stream - center
-    spread = jnp.mean(centered * centered, -1, keepdims=True)
-    inverse = lax.rsqrt(spread + epsilon)
-    normed = centered * inverse
-    return (normed, inverse, normed * gain.astype(jnp.float32) + shift.astype(jnp.float32))
-
-
-def norm_back(grad_hidden, normed, inverse, gain):
-    scaled = grad_hidden * gain.astype(jnp.float32)
-    return inverse * (
-        scaled
-        - jnp.mean(scaled, -1, keepdims=True)
-        - normed * jnp.mean(scaled * normed, -1, keepdims=True)
-    )
-
 
 MESH = pl.DeviceIdType.MESH
 TILE = 128
@@ -203,8 +179,6 @@
 
 N_SCATTER = 12
 PART_SHAPES = ((4, 2, 4, 16, 4096), (4, 2, 4, 16, 4096), (4, 2, 4, 64, 1024), (4, 2, 4, 16, 256))
-OUT_SHAPES = ((16, 4096), (16, 4096), (64, 1024), (16, 256))
-SCATTER_ORDER = (CHAINS[2], CHAINS[1], CHAINS[0])
 
 
 def landing_shapes(chain):
@@ -339,96 +313,6 @@
     lax.fori_loop(0, n, body, 0)
 
 
-def scatter_kernel(gqkv, go, gup, gdown, gsmall, *rest):
-    outs, rest = rest[:4], rest[4:]
-    parts, lands, rest = rest[:4], rest[4:8], rest[8:]
-    landings, (send, recv, local, across_s, across_r) = rest[:-5], rest[-5:]
-    at = place()
-    c = at["c"]
-    greet(at, PEERS)
-    partner = device(moved(at, "c", 1))
-
-    def half(ref, core):
-        return ref.at[:, :, :, core]
-
-    loads = {}
-    for array, src, cols in (
-        (2, gdown, None),
-        (1, gup, None),
-        (0, gqkv, (0, 3072)),
-        (0, go, (3072, 1024)),
-        (3, gsmall, None),
-    ):
-        i = len(loads)
-        window = (lambda r: r) if cols is None else (lambda r, w=cols: r.at[:, :, :, :, pl.ds(w[0], w[1])])
-        own = pltpu.make_async_copy(half(src, c), window(parts[array]), local.at[i])
-        other = pltpu.make_async_remote_copy(
-            src_ref=half(src, 1 - c),
-            dst_ref=window(lands[array]),
-            send_sem=across_s.at[i],
-            recv_sem=across_r.at[i],
-            device_id=partner,
-            device_id_type=MESH,
-        )
-        own.start()
-        other.start()
-        loads[i] = (own, other)
-    needs = {2: (0,), 1: (1,), 0: (2, 3), 3: (4,)}
-    groups = []
-    index = 0
-    for group in SCATTER_ORDER:
-        chains = []
-        for chain in group:
-            land = landings[6 * index : 6 * index + 6]
-            chains.append(Scatter(at, parts[chain[0]], outs[chain[0]], land, chain, send.at[index], recv.at[index]))
-            index += 1
-        groups.append(chains)
-
-    def enter(chains):
-        for array in sorted({chain.chain[0] for chain in chains}):
-            for i in needs[array]:
-                loads[i][0].wait()
-                loads[i][1].wait_recv()
-            add_to(parts[array], (lands[array],))
-
-    for slot in range(8 + len(groups) - 1):
-        for g, chains in enumerate(groups):
-            k = slot - g
-            if k == 0:
-                enter(chains)
-            elif 0 < k < 8:
-                for chain in chains:
-                    chain.step(k - 1)
-    for i in loads:
-        loads[i][1].wait_send()
-
-
-def scatter(gqkv, go, gup, gdown, gsmall):
-    lead = (4, 2, 4, 2)
-    args = (
-        gqkv.reshape(lead + (16, 3072)),
-        go.reshape(lead + (16, 1024)),
-        gup.reshape(lead + (16, 4096)),
-        gdown.reshape(lead + (64, 1024)),
-        gsmall.reshape(lead + (16, 256)),
-    )
-    chains = [c for g in SCATTER_ORDER for c in g]
-    scratch = [pltpu.VMEM(s, BF) for s in PART_SHAPES] * 2
-    for chain in chains:
-        scratch += [pltpu.VMEM(s, BF) for s in landing_shapes(chain)]
-    scratch += [pltpu.SemaphoreType.DMA((len(chains), N_SCATTER))] * 2
-    scratch += [pltpu.SemaphoreType.DMA((5,))] * 3
-    return pl.pallas_call(
-        scatter_kernel,
-        out_shape=[jax.ShapeDtypeStruct(s, F32) for s in OUT_SHAPES],
-        in_specs=[pl.BlockSpec(memory_space=pl.ANY)] * 5,
-        out_specs=[pl.BlockSpec(memory_space=pltpu.VMEM)] * 4,
-        scratch_shapes=scratch,
-        compiler_params=pltpu.CompilerParams(collective_id=1, has_side_effects=True, vmem_limit_bytes=56 << 20),
-        name="scatter_grads",
-    )(*args)
-
-
 LANES = 128
 GELU = 0.7978845608028654
 EPSILON = 1e-05
@@ -514,9 +398,9 @@
 
 
 def forward_kernel(att, up, down, small, tokens, seg_col, seg_row, bucket_rows, *rest):
-    outs, rest = rest[:16], rest[16:]
+    outs, rest = rest[:17], rest[17:]
     fetched = outs[:7]
-    o_acts, o_mid0, o_mid1, o_next, o_qkv, o_probs, o_mixed, o_active, o_slope = outs[7:]
+    o_acts, o_mid0, o_mid1, o_stream, o_params, o_qkv, o_probs, o_mixed, o_active, o_slope = outs[7:]
     (w_att, w_up, w_down, w_small, stream, middle, hidden, qkv, probs, mixed, active, slope, rounded,
      bias, allowed, params, send, recv, local, loads, stores) = rest
     at = place()
@@ -619,8 +503,9 @@
         lax.fori_loop(0, 4, contract, 0)
         store(acts, o_acts.at[layer])
         if layer == 0:
-            store(stream.at[1], o_next)
             slot(9)
+    store(stream, o_stream)
+    store(params, o_params)
     for made in stored:
         made.wait()
 
@@ -632,7 +517,8 @@
         ((2, ROWS, WIDTH), BF),
         ((ROWS, WIDTH), F32),
         ((ROWS, WIDTH), F32),
-        ((ROWS, WIDTH), F32),
+        ((2, ROWS, WIDTH), F32),
+        ((2, 8, WIDTH), F32),
         ((2, ROWS, 3 * WIDTH), BF),
         ((2, HEADS, ROWS, ROWS), BF),
         ((2, ROWS, WIDTH), BF),
@@ -645,7 +531,7 @@
         forward_kernel,
         out_shape=[jax.ShapeDtypeStruct(s, BF) for s in gathered] + [jax.ShapeDtypeStruct(s, t) for s, t in saved],
         in_specs=[vmem] * 8,
-        out_specs=[hbm] * 16,
+        out_specs=[hbm] * 17,
         scratch_shapes=[
             pltpu.VMEM(gathered[0], BF),
             pltpu.VMEM(gathered[1], BF),
@@ -676,6 +562,460 @@
     )(att, up, down, small, tokens, seg_ids[:, None], seg_ids[None, :], bucket_rows)
 
 
+def split_cores(value, core, shape):
+    both = value.reshape(shape)
+    axis = len(shape) - 3
+    even, odd = (lax.index_in_dim(both, i, axis, keepdims=False) for i in range(2))
+    mine = core == 0
+    return jnp.where(mine, even, odd), jnp.where(mine, odd, even)
+
+
+def norm_back_into(grad, dst, src, gain, sums, base):
+    def body(i, carry):
+        by_gain, by_shift = carry
+        at = pl.ds(pl.multiple_of(i * 32, 32), 32)
+        normed, inverse = norm_parts(src[at, :])
+        value = grad[at, :]
+        scaled = value * gain[...]
+        dst[at, :] = dst[at, :] + inverse * (
+            scaled
+            - jnp.mean(scaled, -1, keepdims=True)
+            - normed * jnp.mean(scaled * normed, -1, keepdims=True)
+        )
+        by_gain = by_gain + jnp.sum(value * normed, 0, keepdims=True)
+        return by_gain, by_shift + jnp.sum(value, 0, keepdims=True)
+
+    zero = jnp.zeros((1, WIDTH), F32)
+    by_gain, by_shift = lax.fori_loop(0, ROWS // 32, body, (zero, zero))
+    sums[pl.ds(base, 1), :] = by_gain
+    sums[pl.ds(base + 1, 1), :] = by_shift
+
+
+def attention_backward(qkv, probs, grad_mixed, first, last):
+    scale = HEAD ** (-0.5)
+    low = iota((ROWS, LANES), 1) < HEAD
+
+    def pair(i, _):
+        def columns(k):
+            return pl.ds(pl.multiple_of(k * WIDTH + i * LANES, LANES), LANES)
+
+        q, k, v = (qkv[:, columns(j)] for j in range(3))
+        grad = grad_mixed[:, pl.ds(pl.multiple_of(i * LANES, LANES), LANES)]
+        grads = []
+        for side in range(2):
+            head = 2 * i + side
+            rounded = probs[head]
+            prob = rounded.astype(F32)
+            mine = jnp.where(low == (side == 0), grad, jnp.zeros_like(grad))
+            grad_probs = dot(mine, v, 1, 1)
+            inner = jnp.sum(prob * grad_probs, -1, keepdims=True)
+            grad_scores = (prob * (grad_probs - inner)).astype(BF)
+            probs[head] = grad_scores
+            grads.append(
+                (dot(grad_scores, k) * scale, dot(grad_scores, q, 0, 0) * scale, dot(rounded, grad, 0, 0))
+            )
+        for j in range(3):
+            qkv[:, columns(j)] = jnp.where(low, grads[0][j], grads[1][j]).astype(BF)
+        return 0
+
+    lax.fori_loop(first, last, pair, 0)
+
+
+def table_grads(grad_scores, bucket_rows):
+    total = jnp.zeros((HEADS, 16, ROWS), F32)
+    for b in range(15, -1, -1):
+        if b < 15:
+            total = pltpu.roll(total, ROWS - 16, 2)
+        total = total + grad_scores[:, pl.ds(16 * b, 16), :].astype(F32)
+    line = iota((HEADS, 16, ROWS), 1)
+    for bit in (1, 2, 4, 8):
+        total = jnp.where((line // bit) % 2 == 1, pltpu.roll(total, ROWS - bit, 2), total)
+    by_offset = jnp.sum(total, 1)
+    high = by_offset.astype(BF)
+    rest = (by_offset - high.astype(F32)).astype(BF)
+    return dot(high, bucket_rows, 1, 1) + dot(rest, bucket_rows, 1, 1)
+
+
+def share_grads(sums, table):
+    owner = iota((64, 1024), 0) == iota((64, 1024), 1) // 16
+    shares = jnp.zeros((64, 128), F32)
+    for k in range(4):
+        spread = (iota((128, 1024), 0) == 16 * k + iota((128, 1024), 1) % 16).astype(BF)
+        mine = jnp.where(owner, sums[pl.ds(k, 1), :], 0.0).astype(BF)
+        shares = shares + dot(mine, spread, 1, 1)
+    picked = (iota((16, 128), 1) == 64 + iota((16, 128), 0) % 8).astype(BF)
+    entries = jnp.where(iota((16, 64), 1) % 2 == iota((16, 64), 0) // 8, table, 0.0).astype(BF)
+    return shares + dot(entries, picked, 0, 0)
+
+
+def backward_kernel(*refs):
+    (cotangent, params, bucket_rows, att1, up1, down1, att0, up0, down0,
+     h_stream, h_mid0, h_mid1, h_qkv, h_probs, h_mixed, h_active, h_slope) = refs[:17]
+    o_input, o_att, o_up, o_down, o_small = refs[17:22]
+    rest = refs[22:]
+    parts, lands, rest = rest[:4], rest[4:7], rest[7:]
+    landings, rest = rest[:60], rest[60:]
+    (stage_down, stage_wide, stage_small, tiles_down, tiles_wide, active, slope, probs, qkv, mixed, grad_mixed,
+     state, stream, hidden, grad_hidden, rounded, sums, small_total,
+     send, recv, across_s, across_r, free, free_land, loads, tile_sems, out_sem) = rest
+    weights = ((att0, up0, down0), (att1, up1, down1))
+    middles = (h_mid0, h_mid1)
+    at = place()
+    core = at["c"]
+    partner = device(moved(at, "c", 1))
+    greet(at, PEERS)
+
+    pending = {}
+
+    def fetch(name, i, src, dst):
+        made = pltpu.make_async_copy(src, dst, loads.at[i])
+        made.start()
+        pending[name] = made
+
+    def ready(name):
+        pending.pop(name).wait()
+
+    def fetch_active(layer):
+        fetch("active", 0, h_active.at[layer], active)
+
+    def fetch_slope(layer):
+        fetch("slope", 1, h_slope.at[layer], slope)
+
+    def fetch_mid(layer):
+        fetch("mid", 2, middles[layer], stream)
+
+    def fetch_stream(layer):
+        fetch("stream", 3, h_stream.at[layer], stream)
+
+    def fetch_probs(layer):
+        fetch("probs", 4, h_probs.at[layer], probs)
+
+    def fetch_qkv(layer):
+        fetch("qkv", 5, h_qkv.at[layer], qkv)
+
+    def fetch_mixed(layer):
+        fetch("mixed", 6, h_mixed.at[layer], mixed)
+
+    def streamed(n, source, buffer, body):
+        def tile(i, slot):
+            return pltpu.make_async_copy(source(i), buffer(slot), tile_sems.at[slot])
+
+        tile(0, 0).start()
+
+        def step(i, _):
+            slot = i % 2
+
+            @pl.when(i + 1 < n)
+            def _():
+                tile(i + 1, 1 - slot).start()
+
+            tile(i, slot).wait()
+            body(i, buffer(slot))
+            return 0
+
+        lax.fori_loop(0, n, step, 0)
+
+    chains_of = {array: [c for c in CHAINS[array] if c[0] == array] for array in range(3)}
+    small_chain = CHAINS[0][3]
+    numbers = {}
+    for array in (2, 1, 0):
+        for chain in chains_of[array]:
+            numbers[chain] = len(numbers)
+    numbers[small_chain] = 9
+    land_of = (lands[1], lands[1], lands[0], lands[2])
+    outs = (o_att, o_up, o_down, o_small)
+
+    class Group:
+        def __init__(self, layer, array):
+            self.layer, self.array = layer, array
+            self.turn = 3 * (1 - layer) + (2 - array) if array < 3 else 6
+            self.pieces = []
+            todo = [small_chain] if array == 3 else chains_of[array]
+            self.chains = []
+            for chain in todo:
+                n = numbers[chain]
+                out = outs[array] if array == 3 else outs[array].at[layer]
+                sems = n if array == 3 else n + 10 * (1 - layer)
+                self.chains.append(
+                    Scatter(at, parts[array], out, landings[6 * n : 6 * n + 6], chain, send.at[sems], recv.at[sems])
+                )
+
+        def admit(self):
+            if self.array < 3 and self.layer == 0:
+                pl.semaphore_wait(free.at[self.array], len(PEERS))
+            if self.array in (0, 1) and (self.layer, self.array) != (1, 1):
+                pl.semaphore_wait(free_land, 1)
+
+        def piece(self, src, dst):
+            n = 4 * self.turn + len(self.pieces)
+            made = pltpu.make_async_remote_copy(
+                src_ref=src,
+                dst_ref=dst,
+                send_sem=across_s.at[n],
+                recv_sem=across_r.at[n],
+                device_id=partner,
+                device_id_type=MESH,
+            )
+            made.start()
+            self.pieces.append(made)
+
+        def enter(self):
+            part, land = parts[self.array], land_of[self.array]
+            for x, made in enumerate(self.pieces):
+                made.wait_recv()
+                if self.array == 3:
+                    add_to(part, (land,))
+                else:
+                    add_to(part.at[x], (land.at[x],))
+            if self.array in (0, 1) and (self.layer, self.array) != (0, 0):
+                pl.semaphore_signal(free_land, inc=1, device_id=partner, device_id_type=MESH)
+            for made in self.pieces[-2:]:
+                made.wait_send()
+
+        def step(self, k):
+            for chain in self.chains:
+                chain.step(k)
+            if k == 6 and self.layer == 1 and self.array < 3:
+                for axis, by in PEERS:
+                    pl.semaphore_signal(
+                        free.at[self.array], inc=1, device_id=device(moved(at, axis, by)), device_id_type=MESH
+                    )
+
+    groups = {(layer, array): Group(layer, array) for layer in (1, 0) for array in (2, 1, 0)}
+    last_small = Group(0, 3)
+
+    def serve(*steps):
+        for layer, array, k in steps:
+            groups[(layer, array)].step(k)
+
+    def down_grads(layer):
+        group = groups[(layer, 2)]
+        group.admit()
+        for x in range(4):
+            slot = x % 2
+            if x >= 2:
+                group.pieces[x - 2].wait_send()
+
+            def body(j, _):
+                low, pairs = j // 2, j % 2
+                columns = pl.ds(pl.multiple_of((4 * x + j) * 256, 256), 256)
+                value = dot(active[:, columns], rounded[...], 0, 0).astype(BF)
+                mine, other = split_cores(value, core, (2, 2, 64, WIDTH))
+                parts[2][x, low, pl.ds(2 * pairs, 2)] = mine
+                stage_down[slot, low, pl.ds(2 * pairs, 2)] = other
+                return 0
+
+            lax.fori_loop(0, 4, body, 0)
+            group.piece(stage_down.at[slot], lands[0].at[x])
+
+    def wide_grads(layer, array, terms):
+        group = groups[(layer, array)]
+        group.admit()
+        part = parts[array]
+        for x in range(4):
+            slot = x % 2
+            if x >= 2:
+                group.pieces[x - 2].wait_send()
+            for start, count, left, right, skip in terms:
+
+                def body(j, _):
+                    to = pl.ds(pl.multiple_of(start + j * 1024, 1024), 1024)
+                    frm = pl.ds(pl.multiple_of(skip + j * 1024, 1024), 1024)
+                    value = dot(left[:, pl.ds(256 * x, 256)], right[:, frm], 0, 0).astype(BF)
+                    mine, other = split_cores(value, core, (2, 4, 2, 16, 1024))
+                    part[x, :, :, :, to] = mine
+                    stage_wide[slot, :, :, :, to] = other
+                    return 0
+
+                lax.fori_loop(0, count, body, 0)
+            group.piece(stage_wide.at[slot], lands[1].at[x])
+
+    def through_rows(layer, array, columns, left, put):
+        start, size = columns
+        source = weights[layer][array]
+
+        def body(x, tile):
+            put(x, dot(left[...], tile[:, pl.ds(0, size)], 1, 1))
+
+        streamed(
+            4,
+            lambda x: source.at[pl.ds(pl.multiple_of(x * 256, 256), 256), pl.ds(start, size)],
+            lambda slot: tiles_wide.at[slot, :, pl.ds(0, size)],
+            body,
+        )
+
+    def put_hidden(x, value):
+        grad_hidden[:, pl.ds(pl.multiple_of(x * 256, 256), 256)] = value
+
+    def put_mixed(x, value):
+        grad_mixed[:, pl.ds(pl.multiple_of(x * 256, 256), 256)] = value.astype(BF)
+
+    fetch_active(1)
+    fetch_slope(1)
+    fetch_mid(1)
+    fetch_probs(1)
+    fetch_qkv(1)
+    fetch_mixed(1)
+    state[...] = cotangent[...].astype(F32)
+    rounded[...] = cotangent[...]
+    for layer in (1, 0):
+        row = lambda k: params.at[layer, pl.ds(k, 1), :]
+        ready("active")
+        down_grads(layer)
+        if layer == 1:
+            fetch_active(0)
+        groups[(layer, 2)].enter()
+        serve((layer, 2, 0))
+        if layer == 0:
+            serve((1, 1, 6), (1, 0, 2))
+        ready("slope")
+        down = weights[layer][2]
+
+        def through_down(i, tile):
+            columns = pl.ds(pl.multiple_of(i * 256, 256), 256)
+            value = dot(rounded[...], tile[...], 1, 1)
+            slope[:, columns] = (value * slope[:, columns].astype(F32)).astype(BF)
+
+        streamed(
+            16,
+            lambda i: down.at[pl.ds(pl.multiple_of(i * 256, 256), 256)],
+            lambda slot: tiles_down.at[slot],
+            through_down,
+        )
+        serve((layer, 2, 1))
+        if layer == 0:
+            serve((1, 0, 3))
+        ready("mid")
+        norm_into(hidden, stream, row(2), row(3))
+        wide_grads(layer, 1, ((0, 4, hidden, slope, 0),))
+        groups[(layer, 1)].enter()
+        serve((layer, 1, 0), (layer, 2, 2))
+        if layer == 0:
+            serve((1, 0, 4))
+        through_rows(layer, 1, (0, HIDDEN), slope, put_hidden)
+        if layer == 1:
+            fetch_slope(0)
+        norm_back_into(grad_hidden, state, stream, row(2), sums, 2)
+        fetch_stream(layer)
+        rounded[...] = state[...].astype(BF)
+        serve((layer, 2, 3), (layer, 1, 1))
+        if layer == 0:
+            serve((1, 0, 5))
+        through_rows(layer, 0, (3 * WIDTH, WIDTH), rounded, put_mixed)
+        ready("qkv")
+        ready("probs")
+        attention_backward(qkv, probs, grad_mixed, 0, 4)
+        serve((layer, 2, 4), (layer, 1, 2))
+        if layer == 0:
+            serve((1, 0, 6))
+        attention_backward(qkv, probs, grad_mixed, 4, 8)
+        serve((layer, 2, 5), (layer, 1, 3))
+        ready("stream")
+        ready("mixed")
+        norm_into(hidden, stream, row(0), row(1))
+        wide_grads(layer, 0, ((0, 3, hidden, qkv, 0), (3 * WIDTH, 1, mixed, rounded, 0)))
+        groups[(layer, 0)].enter()
+        serve((layer, 0, 0), (layer, 2, 6), (layer, 1, 4))
+        table = table_grads(probs, bucket_rows[...])
+        if layer == 1:
+            fetch_probs(0)
+            fetch_mixed(0)
+        through_rows(layer, 0, (0, 3 * WIDTH), qkv, put_hidden)
+        norm_back_into(grad_hidden, state, stream, row(0), sums, 0)
+        if layer == 1:
+            fetch_qkv(0)
+            fetch_mid(0)
+        rounded[...] = state[...].astype(BF)
+        shares = share_grads(sums, table).astype(BF)
+        chosen = (iota((64, 1024), 1) == iota((64, 1024), 0) * 16 + layer).astype(BF)
+        placed = dot(chosen, shares, 0, 0)
+        if layer == 1:
+            small_total[...] = placed
+        else:
+            small_total[...] = small_total[...] + placed
+        serve((layer, 0, 1), (layer, 1, 5))
+    finish = pltpu.make_async_copy(state, o_input, out_sem)
+    finish.start()
+    mine, other = split_cores(small_total[...].astype(BF), core, (4, 2, 4, 2, 16, LANES))
+    for i in range(2):
+        columns = pl.ds(i * LANES, LANES)
+        parts[3][:, :, :, :, columns] = mine
+        stage_small[:, :, :, :, columns] = other
+    last_small.piece(stage_small, lands[2])
+    last_small.enter()
+    last_small.step(0)
+    serve((0, 0, 2), (0, 1, 6))
+    for k in range(1, 3):
+        last_small.step(k)
+    serve((0, 0, 3))
+    last_small.step(3)
+    serve((0, 0, 4))
+    last_small.step(4)
+    serve((0, 0, 5))
+    last_small.step(5)
+    serve((0, 0, 6))
+    last_small.step(6)
+    finish.wait()
+
+
+def backward(cotangent, params, bucket_rows, fetched, saved):
+    wide, tall = (1024, 4096), (4096, 1024)
+    arrays = [fetched[i].reshape(s) for i, s in ((3, wide), (4, wide), (5, tall), (0, wide), (1, wide), (2, tall))]
+    vmem = pl.BlockSpec(memory_space=pltpu.VMEM)
+    hbm = pl.BlockSpec(memory_space=pl.ANY)
+    chains = [c for array in (2, 1, 0) for c in CHAINS[array] if c[0] == array] + [CHAINS[0][3]]
+    scratch = [pltpu.VMEM(s, BF) for s in PART_SHAPES]
+    scratch += [pltpu.VMEM(PART_SHAPES[i], BF) for i in (2, 1, 3)]
+    for chain in chains:
+        scratch += [pltpu.VMEM(s, BF) for s in landing_shapes(chain)]
+    scratch += [
+        pltpu.VMEM((2,) + PART_SHAPES[2][1:], BF),
+        pltpu.VMEM((2,) + PART_SHAPES[1][1:], BF),
+        pltpu.VMEM(PART_SHAPES[3], BF),
+        pltpu.VMEM((2, 256, WIDTH), BF),
+        pltpu.VMEM((2, 256, HIDDEN), BF),
+        pltpu.VMEM((ROWS, HIDDEN), BF),
+        pltpu.VMEM((ROWS, HIDDEN), BF),
+        pltpu.VMEM((HEADS, ROWS, ROWS), BF),
+        pltpu.VMEM((ROWS, 3 * WIDTH), BF),
+        pltpu.VMEM((ROWS, WIDTH), BF),
+        pltpu.VMEM((ROWS, WIDTH), BF),
+        pltpu.VMEM((ROWS, WIDTH), F32),
+        pltpu.VMEM((ROWS, WIDTH), F32),
+        pltpu.VMEM((ROWS, WIDTH), BF),
+        pltpu.VMEM((ROWS, WIDTH), F32),
+        pltpu.VMEM((ROWS, WIDTH), BF),
+        pltpu.VMEM((8, WIDTH), F32),
+        pltpu.VMEM((1024, LANES), F32),
+        pltpu.SemaphoreType.DMA((20, N_SCATTER)),
+        pltpu.SemaphoreType.DMA((20, N_SCATTER)),
+        pltpu.SemaphoreType.DMA((28,)),
+        pltpu.SemaphoreType.DMA((28,)),
+        pltpu.SemaphoreType.REGULAR((3,)),
+        pltpu.SemaphoreType.REGULAR,
+        pltpu.SemaphoreType.DMA((7,)),
+        pltpu.SemaphoreType.DMA((2,)),
+        pltpu.SemaphoreType.DMA,
+    ]
+    return pl.pallas_call(
+        backward_kernel,
+        out_shape=[
+            jax.ShapeDtypeStruct((ROWS, WIDTH), F32),
+            jax.ShapeDtypeStruct((2, 16, 4096), F32),
+            jax.ShapeDtypeStruct((2, 16, 4096), F32),
+            jax.ShapeDtypeStruct((2, 64, 1024), F32),
+            jax.ShapeDtypeStruct((16, 256), F32),
+        ],
+        in_specs=[vmem] * 3 + [hbm] * 14,
+        out_specs=[hbm] + [vmem] * 4,
+        scratch_shapes=scratch,
+        compiler_params=pltpu.CompilerParams(
+            collective_id=1, has_side_effects=True, vmem_limit_bytes=63 << 20
+        ),
+        name="backward_scatter",
+    )(cotangent, params, bucket_rows, *arrays, *saved)
+
+
 def on_device(
     tokens,
     seg_ids,
@@ -693,20 +1033,7 @@
     w_up,
     w_down,
 ):
-    length, width = ROWS, WIDTH
-    score_scale = HEAD ** (-0.5)
-    positions = jnp.arange(length, dtype=jnp.int32)
-    distance = jnp.maximum(positions[:, None] - positions[None, :], 0)
-    at_distance = (distance[:, :, None] == positions[None, None, :]).astype(jnp.bfloat16)
-    bucket_of = (buckets[:, None] == jnp.arange(BUCKETS, dtype=jnp.int32)[None, :]).astype(jnp.bfloat16)
-    onehot = jnp.dot(at_distance, bucket_of, preferred_element_type=jnp.float32).astype(jnp.bfloat16)
-
-    small = jnp.stack(
-        [
-            jnp.concatenate([ln1_gain[i], ln1_bias[i], ln2_gain[i], ln2_bias[i], rel_table[i]])
-            for i in range(2)
-        ]
-    )
+    small = jnp.concatenate([ln1_gain, ln1_bias, ln2_gain, ln2_bias, rel_table], 1)
     small = jnp.pad(small, ((0, 14), (0, 56)))
     by_offset = jnp.concatenate([buckets[:1], buckets[:0:-1]])
     bucket_rows = (by_offset[None, :] == (jnp.arange(64, dtype=jnp.int32) // 2)[:, None]).astype(BF)
@@ -719,119 +1046,21 @@
         seg_ids,
         bucket_rows,
     )
-    fetched = done[:7]
-    acts, mid0, mid1, stream1, qkv_all, probs_all, mixed_all, active_all, slope_all = done[7:]
-    middles = (mid0, mid1)
-    streams = (tokens.astype(F32), stream1)
-    small_all = fetched[6].reshape(64, 16, 256)[:, :2, :128]
-
-    def heads_of(value):
-        return value.reshape(length, HEADS, HEAD)
-
-    def layer_backward(grad_result, layer_at):
-        att = fetched[3 * layer_at].reshape(1024, 4096)
-        up_w = fetched[3 * layer_at + 1].reshape(1024, 4096)
-        down_w = fetched[3 * layer_at + 2].reshape(4096, 1024)
-        mine = small_all[:, layer_at]
-        gain_one, shift_one, gain_two, shift_two = (mine[:, 16 * i : 16 * i + 16].reshape(1024) for i in range(4))
-        out_w = att[:, 3072:]
-        normed_one, inverse_one, hidden_one = normalize(streams[layer_at], gain_one, shift_one)
-        normed_two, inverse_two, hidden_two = normalize(middles[layer_at], gain_two, shift_two)
-        input_one, input_two = hidden_one.astype(BF), hidden_two.astype(BF)
-        queries, key_rows, values = (heads_of(qkv_all[layer_at][:, i * width : (i + 1) * width]) for i in range(3))
-        prob_rows = probs_all[layer_at]
-        mixed, activated, slope = mixed_all[layer_at], active_all[layer_at], slope_all[layer_at]
-        down_in = grad_result.astype(jnp.bfloat16)
-        grad_down = jnp.einsum("lf,ld->fd", activated, down_in, preferred_element_type=jnp.float32)
-        grad_active = jnp.einsum("ld,fd->lf", down_in, down_w, preferred_element_type=jnp.float32)
-        grad_upward = (grad_active * slope.astype(F32)).astype(jnp.bfloat16)
-        grad_up = jnp.einsum(
-            "ld,lf->df", input_two, grad_upward, preferred_element_type=jnp.float32
-        )
-        grad_hidden_two = jnp.einsum(
-            "lf,df->ld", grad_upward, up_w, preferred_element_type=jnp.float32
-        )
-        grad_gain_two = jnp.sum(grad_hidden_two * normed_two, 0)
-        grad_shift_two = jnp.sum(grad_hidden_two, 0)
-        grad_middle = grad_result + norm_back(grad_hidden_two, normed_two, inverse_two, gain_two)
-        branch_in = grad_middle.astype(jnp.bfloat16)
-        grad_out_w = jnp.einsum("ld,le->de", mixed, branch_in, preferred_element_type=jnp.float32)
-        grad_mixed = jnp.einsum("le,de->ld", branch_in, out_w, preferred_element_type=jnp.float32)
-        grad_mixed = grad_mixed.astype(jnp.bfloat16).reshape(length, HEADS, HEAD)
-        grad_probs = jnp.einsum(
-            "ihe,jhe->hij", grad_mixed, values, preferred_element_type=jnp.float32
-        )
-        grad_values = jnp.einsum(
-            "hij,ihe->jhe",
-            prob_rows.astype(jnp.bfloat16),
-            grad_mixed,
-            preferred_element_type=jnp.float32,
-        )
-        grad_values = grad_values.astype(jnp.bfloat16).reshape(length, width)
-        grad_scores = (
-            prob_rows.astype(F32) * (grad_probs - jnp.sum(prob_rows.astype(F32) * grad_probs, -1, keepdims=True))
-        ).astype(jnp.bfloat16)
-        grad_queries = (
-            (
-                jnp.einsum(
-                    "hij,jhe->ihe", grad_scores, key_rows, preferred_element_type=jnp.float32
-                )
-                * score_scale
-            )
-            .astype(jnp.bfloat16)
-            .reshape(length, width)
-        )
-        grad_keys = (
-            (
-                jnp.einsum("hij,ihe->jhe", grad_scores, queries, preferred_element_type=jnp.float32)
-                * score_scale
-            )
-            .astype(jnp.bfloat16)
-            .reshape(length, width)
-        )
-        grad_bias_table = jnp.einsum(
-            "hij,ijb->bh", grad_scores, onehot, preferred_element_type=jnp.float32
-        ).reshape(BUCKETS * HEADS)
-        grad_all = jnp.concatenate([grad_queries, grad_keys, grad_values], 1)
-        grad_qkv = jnp.einsum("ld,le->de", input_one, grad_all, preferred_element_type=jnp.float32)
-        grad_hidden_one = jnp.einsum("le,de->ld", grad_all, att[:, :3072], preferred_element_type=jnp.float32)
-        grad_gain_one = jnp.sum(grad_hidden_one * normed_one, 0)
-        grad_shift_one = jnp.sum(grad_hidden_one, 0)
-        grad_stream = grad_middle + norm_back(grad_hidden_one, normed_one, inverse_one, gain_one)
-        small = jnp.concatenate(
-            [
-                grad_gain_one.reshape(64, 16),
-                grad_shift_one.reshape(64, 16),
-                grad_gain_two.reshape(64, 16),
-                grad_shift_two.reshape(64, 16),
-                grad_bias_table.reshape(64, 8),
-            ],
-            1,
-        )
-        small = jnp.pad(small[:, None], ((0, 0), (0, 15), (0, 56)))
-        small = jnp.concatenate([small, small], 2)
-        grads = tuple(g.astype(BF) for g in (grad_qkv, grad_out_w, grad_up, grad_down, small))
-        return (grad_stream, grads)
-
-    grad_stream = cotangent.astype(jnp.float32)
-    reduced = [None, None]
-    for layer_at in (1, 0):
-        grad_stream, grads = layer_backward(grad_stream, layer_at)
-        reduced[layer_at] = scatter(*grads)
-    stacked = [jnp.stack([reduced[0][i], reduced[1][i]]) for i in range(4)]
-    att, up, down, small = stacked
+    acts, mid0, mid1, stream, params = done[7:12]
+    saved = (stream, mid0, mid1) + tuple(done[12:])
+    grad_input, att, up, down, small = backward(cotangent, params, bucket_rows, done[:6], saved)
     return (
         acts,
-        grad_stream,
-        small[:, 0, 0:16],
-        small[:, 0, 16:32],
+        grad_input,
+        small[:2, 0:16],
+        small[:2, 16:32],
         att[:, :, :1024],
         att[:, :, 1024:2048],
         att[:, :, 2048:3072],
         att[:, :, 3072:],
-        small[:, 0, 64:72],
-        small[:, 0, 32:48],
-        small[:, 0, 48:64],
+        small[:2, 64:72],
+        small[:2, 32:48],
+        small[:2, 48:64],
         up,
         down,
     )

time: 498 us -> 380 us (0.76); the launches traced: 490 us -> 379 us
  matrix products: 124 us -> 0 us
  Pallas kernels: 305 us -> 357 us
  other arithmetic: 24.5 us -> 3.67 us
  local copies, waits for them, and re-layouts: 34.2 us -> 17.4 us
    dot_general x27 -> x0, matrix products: 124 us -> none  [the longest x1 16.9 us: on_device(): jnp.dot(at_distance, bucket_of, preferred_element_type=jnp.float32)]
    pallas_call x2 -> x1, Pallas kernels: 155 us -> 206 us  [backward(): pl.pallas_call(backward_kernel, out_shape=[jax.ShapeDtypeStruct((ROWS, WI...]
    slice x9 -> x3, local copies, waits for them, and re-layouts: 14 us -> 4.68 us  [the longest x1 1.89 us: on_device(): att[:, :, 3072:]]
    another operation x5 -> x0, other arithmetic: 6.79 us -> none  [the longest x4 6.78 us: on_device(): stacked = [jnp.stack([reduced[0][i], reduced[1][i]]) for i in range(4)]]
where the time goes in v3:
time: 380 us; the launch traced here: 379 us
  Pallas kernels  357 us (94%)
  local copies, waits for them, and re-layouts  17.4 us (5%)
    pallas_call x1, Pallas kernels, backward(): pl.pallas_call(backward_kernel, out_shape=[jax.ShapeDtypeStruct((ROWS, WI...  206 us
    pallas_call x1, Pallas kernels, forward(): pl.pallas_call(forward_kernel, out_shape=[jax.ShapeDtypeStruct(s, BF) for...  151 us
    unnamed x6, local copies, waits for them, and re-layouts  8.49 us

profile of v3, /device:TPU:0, one launch (start us, length us, event | category | flops | bytes accessed | tf_op | source)
XLA Modules:
  0.0 378.7 jit_solution(11436534040988590349)
XLA Ops:
  0.6 1.2 slice.33
  1.8 0.8 concatenate.13
  2.6 0.8 slice.34
  3.4 0.1 reverse
  3.5 0.1 slice.44
  3.6 0.7 pad_add_fusion
  4.3 0.6 pad_maximum_fusion.1.small
  4.9 0.7 compare_convert_fusion.bucket_rows.refs_2_
  5.6 1.5 copy.28.seg_col
  7.1 1.7 pad_maximum_fusion.att
  8.7 150.7 %gather_forward.1 = (bf16[4,2,4,2,16,4096]{5,4,3,2,1,0:T(8,128)(2,1)}, bf16[4,2,4,2,16,4096]{5,4,3,2,1,0:T(8,128)(2,1)}, bf16[4,2,4,2,64,1024]{5,4,3,2,1,0:T(8,1...) custom-call(bf16[2,16,4096]{2,1,0:T(8,128)(2,1)} %pad_maximum_fusion, ...), custom_call_target="tpu_custom_call" | custom-call | tf_op jit(solution)/shard_map/gather_forward/pallas_call | solution.py:530
  159.4 206.2 %backward_scatter.1 = (f32[256,1024]{1,0:T(8,128)}, f32[2,16,4096]{2,1,0:T(8,128)}, f32[2,16,4096]{2,1,0:T(8,128)}, f32[2,64,1024]{2,1,0:T(8,128)}, f32[16,256]{1,0:T(8,128)}) custom-call(bf16[256,1024]{1,0:T(8,128)(2,1)} %refs_0_.1, f32[2,8,1024]{2,1,0:T(8,128)} %get-tuple-element.35.refs_1_, bf16[64,256]{1,0:T(8,128)(2,1)} %compare_convert_fusion.bucket_rows.refs_2_, ...), custom_call_target="tpu_custom_call" | custom-call | tf_op jit(solution)/shard_map/backward_scatter/pallas_call | solution.py:1000
  365.7 1.3 slice.41
  367.0 1.5 fusion.1
  368.5 1.9 fusion
  370.4 2.3 copy.33
  372.6 2.3 copy.34
  374.9 1.9 copy.35
  376.8 1.9 copy.36
  (2 shorter events, 0.0 us)

commit v4 on v3

--- a/solution.py
+++ b/solution.py
@@ -313,6 +313,36 @@
     lax.fori_loop(0, n, body, 0)
 
 
+FORWARD_SERVED = (
+    (0, 1, 2, 3, 0, 1, 2, 3, 0, 1, 2, 3, 0, 4, 1, 5, 2, 3, 0, 4, 1, 5, 2, 3, 0, 4, 0, 1,),
+    (1, 5,),
+    (2,),
+    (3, 4,),
+    (2, 5, 3,),
+    (),
+    (),
+    (),
+    (4,),
+    (),
+    (),
+    (),
+    (),
+    (5,),
+    (4,),
+    (5, 4,),
+    (),
+    (5,),
+    (),
+    (),
+    (),
+    (),
+    (),
+    (),
+    (),
+    (),
+)
+
+
 LANES = 128
 GELU = 0.7978845608028654
 EPSILON = 1e-05
@@ -369,7 +399,7 @@
     lax.fori_loop(0, ROWS // 64, body, 0)
 
 
-def attention_forward(qkv, probs, mixed, bias, allowed):
+def attention_forward(qkv, probs, mixed, bias, allowed, start, stop):
     scale = HEAD ** (-0.5)
     low = iota((ROWS, LANES), 1) < HEAD
 
@@ -394,7 +424,7 @@
         mixed[:, pl.ds(pl.multiple_of(i * LANES, LANES), LANES)] = jnp.where(low, halves[0], halves[1]).astype(BF)
         return 0
 
-    lax.fori_loop(0, HEADS // 2, pair, 0)
+    lax.fori_loop(start, stop, pair, 0)
 
 
 def forward_kernel(att, up, down, small, tokens, seg_col, seg_row, bucket_rows, *rest):
@@ -406,33 +436,54 @@
     at = place()
     greet(at, PEERS)
     groups = gather_groups(at, 2, (att, up, down, small), fetched, send, recv, local)
+    buffers = (w_att, w_up, w_down)
+    served = [0] * 6
+    arrived, used, waiting = set(), set(), {}
     stored = []
+    points = [0]
 
     def store(src, dst):
         made = pltpu.make_async_copy(src, dst, stores.at[len(stored)])
         made.start()
         stored.append(made)
 
-    def load(i, src, dst):
-        made = pltpu.make_async_copy(src, dst, loads.at[i])
-        made.start()
-        return made
-
-    def slot(n):
-        for g, chains in reversed(list(enumerate(groups))):
-            k = n - g
-            if 0 <= k < 7:
-                for chain in chains:
-                    chain.step(k)
+    def load(g):
+        if g in arrived and g not in waiting and (g < 3 or g - 3 in used):
+            waiting[g] = pltpu.make_async_copy(fetched[g], buffers[g % 3], loads.at[g])
+            waiting[g].start()
+
+    def serve(g):
+        for chain in groups[g]:
+            chain.step(served[g])
+        served[g] += 1
+        if served[g] == 7:
+            arrived.add(g)
+            load(g)
+            if g == 0:
+                waiting[6] = pltpu.make_async_copy(fetched[6], w_small, loads.at[6])
+                waiting[6].start()
+
+    def point():
+        for g in FORWARD_SERVED[points[0]]:
+            serve(g)
+        points[0] += 1
+
+    def need(g):
+        point()
+        waiting[g].wait()
+
+    def done(g):
+        used.add(g)
+        if g < 3:
+            load(g + 3)
 
     same = (seg_col[...] == seg_row[...]) & (iota((ROWS, ROWS), 0) >= iota((ROWS, ROWS), 1))
     allowed[...] = same.astype(F32)
     stream[0] = tokens[...].astype(F32)
-    for n in range(7):
-        slot(n)
-    load(0, fetched[6], w_small).wait()
     for layer in range(2):
-        load(1, fetched[3 * layer], w_att).wait()
+        need(3 * layer)
+        if layer == 0:
+            waiting[6].wait()
         rows, shares = param_rows(w_small, layer)
         for k in range(4):
             params[layer, pl.ds(k, 1), :] = rows[k]
@@ -452,8 +503,11 @@
             wide_qkv[:, cols] = dot(hidden[...], weights).astype(BF)
             return 0
 
+        point()
         lax.fori_loop(0, 6, project, 0)
-        attention_forward(wide_qkv, wide_probs, wide_mixed, bias, allowed)
+        for n in range(4):
+            point()
+            attention_forward(wide_qkv, wide_probs, wide_mixed, bias, allowed, 2 * n, 2 * n + 2)
 
         def out_project(i, _):
             cols = pl.ds(pl.multiple_of(i * 512, 512), 512)
@@ -462,14 +516,15 @@
             mid[:, cols] = here[:, cols] + dot(wide_mixed[...], weights)
             return 0
 
+        point()
         lax.fori_loop(0, 2, out_project, 0)
+        done(3 * layer)
         norm_into(hidden, mid, row(2), row(3))
         store(wide_qkv, o_qkv.at[layer])
         store(wide_probs, o_probs.at[layer])
         store(wide_mixed, o_mixed.at[layer])
         store(mid, (o_mid0, o_mid1)[layer])
-        slot(7 + 3 * layer)
-        load(2, fetched[3 * layer + 1], w_up).wait()
+        need(3 * layer + 1)
 
         def expand(i, _):
             cols = pl.ds(pl.multiple_of(i * 512, 512), 512)
@@ -484,11 +539,14 @@
             ).astype(BF)
             return 0
 
-        lax.fori_loop(0, 8, expand, 0)
+        for n in range(4):
+            if n > 0:
+                point()
+            lax.fori_loop(2 * n, 2 * n + 2, expand, 0)
+        done(3 * layer + 1)
         store(wide_active, o_active.at[layer])
         store(wide_slope, o_slope.at[layer])
-        slot(8 + 3 * layer)
-        load(3, fetched[3 * layer + 2], w_down).wait()
+        need(3 * layer + 2)
         acts = rounded.at[layer]
 
         def contract(i, _):
@@ -500,10 +558,11 @@
             acts[:, cols] = result.astype(BF)
             return 0
 
-        lax.fori_loop(0, 4, contract, 0)
+        lax.fori_loop(0, 2, contract, 0)
+        point()
+        lax.fori_loop(2, 4, contract, 0)
+        done(3 * layer + 2)
         store(acts, o_acts.at[layer])
-        if layer == 0:
-            slot(9)
     store(stream, o_stream)
     store(params, o_params)
     for made in stored:
@@ -552,7 +611,7 @@
             pltpu.SemaphoreType.DMA((19, N_GATHER)),
             pltpu.SemaphoreType.DMA((19, N_GATHER)),
             pltpu.SemaphoreType.DMA((19,)),
-            pltpu.SemaphoreType.DMA((4,)),
+            pltpu.SemaphoreType.DMA((7,)),
             pltpu.SemaphoreType.DMA((16,)),
         ],
         compiler_params=pltpu.CompilerParams(
@@ -560,6 +619,65 @@
         ),
         name="gather_forward",
     )(att, up, down, small, tokens, seg_ids[:, None], seg_ids[None, :], bucket_rows)
+
+
+SERVED = (
+    (),
+    (),
+    (),
+    (0,),
+    (0, 0,),
+    (0, 0,),
+    (),
+    (),
+    (),
+    (0, 1, 1,),
+    (1, 1, 1,),
+    (),
+    (),
+    (0,),
+    (),
+    (0, 1,),
+    (),
+    (0,),
+    (),
+    (),
+    (),
+    (2,),
+    (0, 1, 2, 2,),
+    (0, 1, 2, 2,),
+    (),
+    (1,),
+    (),
+    (2, 1,),
+    (),
+    (3,),
+    (3,),
+    (3, 3, 3,),
+    (1, 2,),
+    (),
+    (2, 3,),
+    (4,),
+    (4,),
+    (2, 4, 4, 4,),
+    (),
+    (2, 3,),
+    (),
+    (2, 3, 4,),
+    (),
+    (3,),
+    (),
+    (),
+    (),
+    (4, 3, 5, 5,),
+    (5, 4, 3,),
+    (5, 5,),
+    (4,),
+    (),
+    (4, 5,),
+    (),
+    (4, 6, 6, 5, 6, 5, 6, 5, 6, 5, 6, 5, 6, 6,),
+)
 
 
 def split_cores(value, core, shape):
@@ -696,25 +814,6 @@
     def fetch_mixed(layer):
         fetch("mixed", 6, h_mixed.at[layer], mixed)
 
-    def streamed(n, source, buffer, body):
-        def tile(i, slot):
-            return pltpu.make_async_copy(source(i), buffer(slot), tile_sems.at[slot])
-
-        tile(0, 0).start()
-
-        def step(i, _):
-            slot = i % 2
-
-            @pl.when(i + 1 < n)
-            def _():
-                tile(i + 1, 1 - slot).start()
-
-            tile(i, slot).wait()
-            body(i, buffer(slot))
-            return 0
-
-        lax.fori_loop(0, n, step, 0)
-
     chains_of = {array: [c for c in CHAINS[array] if c[0] == array] for array in range(3)}
     small_chain = CHAINS[0][3]
     numbers = {}
@@ -730,6 +829,7 @@
             self.layer, self.array = layer, array
             self.turn = 3 * (1 - layer) + (2 - array) if array < 3 else 6
             self.pieces = []
+            self.served = 0
             todo = [small_chain] if array == 3 else chains_of[array]
             self.chains = []
             for chain in todo:
@@ -759,20 +859,26 @@
             made.start()
             self.pieces.append(made)
 
-        def enter(self):
+        def add_piece(self, x):
             part, land = parts[self.array], land_of[self.array]
-            for x, made in enumerate(self.pieces):
-                made.wait_recv()
-                if self.array == 3:
-                    add_to(part, (land,))
-                else:
-                    add_to(part.at[x], (land.at[x],))
-            if self.array in (0, 1) and (self.layer, self.array) != (0, 0):
-                pl.semaphore_signal(free_land, inc=1, device_id=partner, device_id_type=MESH)
-            for made in self.pieces[-2:]:
-                made.wait_send()
-
-        def step(self, k):
+            self.pieces[x].wait_recv()
+            if self.array == 3:
+                add_to(part, (land,))
+            else:
+                add_to(part.at[x], (land.at[x],))
+            if x == len(self.pieces) - 1:
+                if self.array in (0, 1) and (self.layer, self.array) != (0, 0):
+                    pl.semaphore_signal(free_land, inc=1, device_id=partner, device_id_type=MESH)
+                for made in self.pieces[-2:]:
+                    made.wait_send()
+
+        def serve(self):
+            pieces = 1 if self.array == 3 else 4
+            k = self.served - pieces
+            self.served += 1
+            if k < 0:
+                self.add_piece(k + pieces)
+                return
             for chain in self.chains:
                 chain.step(k)
             if k == 6 and self.layer == 1 and self.array < 3:
@@ -781,15 +887,44 @@
                         free.at[self.array], inc=1, device_id=device(moved(at, axis, by)), device_id_type=MESH
                     )
 
-    groups = {(layer, array): Group(layer, array) for layer in (1, 0) for array in (2, 1, 0)}
-    last_small = Group(0, 3)
-
-    def serve(*steps):
-        for layer, array, k in steps:
-            groups[(layer, array)].step(k)
+    order = [(layer, array) for layer in (1, 0) for array in (2, 1, 0)] + [(0, 3)]
+    groups = [Group(layer, array) for layer, array in order]
+    by_name = dict(zip(order, groups))
+    points = [0]
+
+    def point():
+        for g in SERVED[points[0]] if points[0] < len(SERVED) else ():
+            groups[g].serve()
+        points[0] += 1
+
+    loaded = {}
+
+    def tile_down(layer, i):
+        rows = pl.ds(i * 512, 512)
+        made = pltpu.make_async_copy(weights[layer][2].at[rows], tiles_down.at[i % 4], tile_sems.at[i % 4])
+        made.start()
+        loaded["down", i] = made
+
+    def tile_wide(layer, array, x, slot, start, size, at_column, sem):
+        made = pltpu.make_async_copy(
+            weights[layer][array].at[pl.ds(x * 256, 256), pl.ds(start, size)],
+            tiles_wide.at[slot, :, pl.ds(at_column, size)],
+            tile_sems.at[sem],
+        )
+        made.start()
+        return made
+
+    def tile_up(layer, x):
+        loaded["up", x] = tile_wide(layer, 1, x, x % 2, 0, HIDDEN, 0, 4 + x % 2)
+
+    def tile_out(layer, x):
+        loaded["out", x] = tile_wide(layer, 0, x, 0, 3 * WIDTH, WIDTH, x * WIDTH, 6 + x)
+
+    def tile_qkv(layer, x):
+        loaded["qkv", x] = tile_wide(layer, 0, x, 1 - x % 2, 0, 3 * WIDTH, 0, 5 - x % 2)
 
     def down_grads(layer):
-        group = groups[(layer, 2)]
+        group = by_name[layer, 2]
         group.admit()
         for x in range(4):
             slot = x % 2
@@ -807,9 +942,10 @@
 
             lax.fori_loop(0, 4, body, 0)
             group.piece(stage_down.at[slot], lands[0].at[x])
+            point()
 
     def wide_grads(layer, array, terms):
-        group = groups[(layer, array)]
+        group = by_name[layer, array]
         group.admit()
         part = parts[array]
         for x in range(4):
@@ -829,29 +965,14 @@
 
                 lax.fori_loop(0, count, body, 0)
             group.piece(stage_wide.at[slot], lands[1].at[x])
-
-    def through_rows(layer, array, columns, left, put):
-        start, size = columns
-        source = weights[layer][array]
-
-        def body(x, tile):
-            put(x, dot(left[...], tile[:, pl.ds(0, size)], 1, 1))
-
-        streamed(
-            4,
-            lambda x: source.at[pl.ds(pl.multiple_of(x * 256, 256), 256), pl.ds(start, size)],
-            lambda slot: tiles_wide.at[slot, :, pl.ds(0, size)],
-            body,
-        )
-
-    def put_hidden(x, value):
-        grad_hidden[:, pl.ds(pl.multiple_of(x * 256, 256), 256)] = value
-
-    def put_mixed(x, value):
-        grad_mixed[:, pl.ds(pl.multiple_of(x * 256, 256), 256)] = value.astype(BF)
-
+            point()
+
+    for i in range(4):
+        tile_down(1, i)
     fetch_active(1)
     fetch_slope(1)
+    for x in range(2):
+        tile_up(1, x)
     fetch_mid(1)
     fetch_probs(1)
     fetch_qkv(1)
@@ -864,97 +985,93 @@
         down_grads(layer)
         if layer == 1:
             fetch_active(0)
-        groups[(layer, 2)].enter()
-        serve((layer, 2, 0))
-        if layer == 0:
-            serve((1, 1, 6), (1, 0, 2))
         ready("slope")
-        down = weights[layer][2]
-
-        def through_down(i, tile):
-            columns = pl.ds(pl.multiple_of(i * 256, 256), 256)
-            value = dot(rounded[...], tile[...], 1, 1)
-            slope[:, columns] = (value * slope[:, columns].astype(F32)).astype(BF)
-
-        streamed(
-            16,
-            lambda i: down.at[pl.ds(pl.multiple_of(i * 256, 256), 256)],
-            lambda slot: tiles_down.at[slot],
-            through_down,
-        )
-        serve((layer, 2, 1))
-        if layer == 0:
-            serve((1, 0, 3))
+        for half in range(2):
+            for j in range(4):
+                i = 4 * half + j
+                loaded.pop(("down", i)).wait()
+                columns = pl.ds(i * 512, 512)
+                value = dot(rounded[...], tiles_down[j], 1, 1)
+                slope[:, columns] = (value * slope[:, columns].astype(F32)).astype(BF)
+                if half == 0:
+                    tile_down(layer, i + 4)
+                elif layer == 1:
+                    tile_down(0, j)
+            point()
         ready("mid")
         norm_into(hidden, stream, row(2), row(3))
         wide_grads(layer, 1, ((0, 4, hidden, slope, 0),))
-        groups[(layer, 1)].enter()
-        serve((layer, 1, 0), (layer, 2, 2))
-        if layer == 0:
-            serve((1, 0, 4))
-        through_rows(layer, 1, (0, HIDDEN), slope, put_hidden)
+        for x in range(4):
+            loaded.pop(("up", x)).wait()
+            grad_hidden[:, pl.ds(x * 256, 256)] = dot(slope[...], tiles_wide[x % 2], 1, 1)
+            if x < 2:
+                tile_up(layer, x + 2)
+            elif x == 2:
+                for n in range(4):
+                    tile_out(layer, n)
+            else:
+                tile_qkv(layer, 0)
+            if x % 2 == 1:
+                point()
         if layer == 1:
             fetch_slope(0)
         norm_back_into(grad_hidden, state, stream, row(2), sums, 2)
         fetch_stream(layer)
         rounded[...] = state[...].astype(BF)
-        serve((layer, 2, 3), (layer, 1, 1))
-        if layer == 0:
-            serve((1, 0, 5))
-        through_rows(layer, 0, (3 * WIDTH, WIDTH), rounded, put_mixed)
+        point()
+        for x in range(4):
+            loaded.pop(("out", x)).wait()
+            value = dot(rounded[...], tiles_wide[0, :, pl.ds(x * WIDTH, WIDTH)], 1, 1)
+            grad_mixed[:, pl.ds(x * 256, 256)] = value.astype(BF)
+        tile_qkv(layer, 1)
         ready("qkv")
         ready("probs")
-        attention_backward(qkv, probs, grad_mixed, 0, 4)
-        serve((layer, 2, 4), (layer, 1, 2))
-        if layer == 0:
-            serve((1, 0, 6))
-        attention_backward(qkv, probs, grad_mixed, 4, 8)
-        serve((layer, 2, 5), (layer, 1, 3))
+        point()
+        for n in range(4):
+            attention_backward(qkv, probs, grad_mixed, 2 * n, 2 * n + 2)
+            point()
         ready("stream")
         ready("mixed")
         norm_into(hidden, stream, row(0), row(1))
         wide_grads(layer, 0, ((0, 3, hidden, qkv, 0), (3 * WIDTH, 1, mixed, rounded, 0)))
-        groups[(layer, 0)].enter()
-        serve((layer, 0, 0), (layer, 2, 6), (layer, 1, 4))
         table = table_grads(probs, bucket_rows[...])
         if layer == 1:
             fetch_probs(0)
             fetch_mixed(0)
-        through_rows(layer, 0, (0, 3 * WIDTH), qkv, put_hidden)
+        point()
+        for x in range(4):
+            loaded.pop(("qkv", x)).wait()
+            grad_hidden[:, pl.ds(x * 256, 256)] = dot(qkv[...], tiles_wide[1 - x % 2, :, pl.ds(0, 3 * WIDTH)], 1, 1)
+            if x < 2:
+                tile_qkv(layer, x + 2)
+            elif layer == 1:
+                tile_up(0, 3 - x)
+            if x % 2 == 1:
+                point()
         norm_back_into(grad_hidden, state, stream, row(0), sums, 0)
         if layer == 1:
             fetch_qkv(0)
             fetch_mid(0)
         rounded[...] = state[...].astype(BF)
+        point()
         shares = share_grads(sums, table).astype(BF)
         chosen = (iota((64, 1024), 1) == iota((64, 1024), 0) * 16 + layer).astype(BF)
         placed = dot(chosen, shares, 0, 0)
         if layer == 1:
             small_total[...] = placed
         else:
-            small_total[...] = small_total[...] + placed
-        serve((layer, 0, 1), (layer, 1, 5))
-    finish = pltpu.make_async_copy(state, o_input, out_sem)
-    finish.start()
-    mine, other = split_cores(small_total[...].astype(BF), core, (4, 2, 4, 2, 16, LANES))
-    for i in range(2):
-        columns = pl.ds(i * LANES, LANES)
-        parts[3][:, :, :, :, columns] = mine
-        stage_small[:, :, :, :, columns] = other
-    last_small.piece(stage_small, lands[2])
-    last_small.enter()
-    last_small.step(0)
-    serve((0, 0, 2), (0, 1, 6))
-    for k in range(1, 3):
-        last_small.step(k)
-    serve((0, 0, 3))
-    last_small.step(3)
-    serve((0, 0, 4))
-    last_small.step(4)
-    serve((0, 0, 5))
-    last_small.step(5)
-    serve((0, 0, 6))
-    last_small.step(6)
+            finish = pltpu.make_async_copy(state, o_input, out_sem)
+            finish.start()
+            total = (small_total[...] + placed).astype(BF)
+            mine, other = split_cores(total, core, (4, 2, 4, 2, 16, LANES))
+            for i in range(2):
+                columns = pl.ds(i * LANES, LANES)
+                parts[3][:, :, :, :, columns] = mine
+                stage_small[:, :, :, :, columns] = other
+            by_name[0, 3].piece(stage_small, lands[2])
+        point()
+    while points[0] < len(SERVED):
+        point()
     finish.wait()
 
 
@@ -972,7 +1089,7 @@
         pltpu.VMEM((2,) + PART_SHAPES[2][1:], BF),
         pltpu.VMEM((2,) + PART_SHAPES[1][1:], BF),
         pltpu.VMEM(PART_SHAPES[3], BF),
-        pltpu.VMEM((2, 256, WIDTH), BF),
+        pltpu.VMEM((4, 512, WIDTH), BF),
         pltpu.VMEM((2, 256, HIDDEN), BF),
         pltpu.VMEM((ROWS, HIDDEN), BF),
         pltpu.VMEM((ROWS, HIDDEN), BF),
@@ -994,7 +1111,7 @@
         pltpu.SemaphoreType.REGULAR((3,)),
         pltpu.SemaphoreType.REGULAR,
         pltpu.SemaphoreType.DMA((7,)),
-        pltpu.SemaphoreType.DMA((2,)),
+        pltpu.SemaphoreType.DMA((10,)),
         pltpu.SemaphoreType.DMA,
     ]
     return pl.pallas_call(

time: 380 us -> 323 us (0.85)
  Pallas kernels: 357 us -> 297 us
    pallas_call x1, Pallas kernels: 206 us -> 167 us  [backward(): pl.pallas_call(backward_kernel, out_shape=[jax.ShapeDtypeStruct((ROWS, WI...]
    pallas_call x1, Pallas kernels: 151 us -> 130 us  [forward(): pl.pallas_call(forward_kernel, out_shape=[jax.ShapeDtypeStruct(s, BF) for...]
where the time goes in v4:
time: 323 us; the launch traced here: 319 us
  Pallas kernels  297 us (92%)
  local copies, waits for them, and re-layouts  17.4 us (5%)
  other arithmetic  3.67 us (1%)
    pallas_call x1, Pallas kernels, backward(): pl.pallas_call(backward_kernel, out_shape=[jax.ShapeDtypeStruct((ROWS, WI...  167 us
    pallas_call x1, Pallas kernels, forward(): pl.pallas_call(forward_kernel, out_shape=[jax.ShapeDtypeStruct(s, BF) for...  130 us
    unnamed x6, local copies, waits for them, and re-layouts  8.49 us

profile of v4, /device:TPU:0, one launch (start us, length us, event | category | flops | bytes accessed | tf_op | source)
XLA Modules:
  0.0 319.2 jit_solution(17195114872260850740)
XLA Ops:
  0.6 1.2 slice.33
  1.8 0.8 concatenate.13
  2.6 0.8 slice.34
  3.4 0.1 reverse
  3.5 0.1 slice.44
  3.6 0.7 pad_add_fusion
  4.3 0.6 pad_maximum_fusion.1.small
  4.9 0.7 compare_convert_fusion.bucket_rows.refs_2_
  5.6 1.5 copy.28.seg_col
  7.1 1.7 pad_maximum_fusion.att
  8.7 130.3 %gather_forward.1 = (bf16[4,2,4,2,16,4096]{5,4,3,2,1,0:T(8,128)(2,1)}, bf16[4,2,4,2,16,4096]{5,4,3,2,1,0:T(8,128)(2,1)}, bf16[4,2,4,2,64,1024]{5,4,3,2,1,0:T(8,1...) custom-call(bf16[2,16,4096]{2,1,0:T(8,128)(2,1)} %pad_maximum_fusion, ...), custom_call_target="tpu_custom_call" | custom-call | tf_op jit(solution)/shard_map/gather_forward/pallas_call | solution.py:589
  139.0 167.0 %backward_scatter.1 = (f32[256,1024]{1,0:T(8,128)}, f32[2,16,4096]{2,1,0:T(8,128)}, f32[2,16,4096]{2,1,0:T(8,128)}, f32[2,64,1024]{2,1,0:T(8,128)}, f32[16,256]{1,0:T(8,128)}) custom-call(bf16[256,1024]{1,0:T(8,128)(2,1)} %refs_0_.1, f32[2,8,1024]{2,1,0:T(8,128)} %get-tuple-element.35.refs_1_, bf16[64,256]{1,0:T(8,128)(2,1)} %compare_convert_fusion.bucket_rows.refs_2_, ...), custom_call_target="tpu_custom_call" | custom-call | tf_op jit(solution)/shard_map/backward_scatter/pallas_call | solution.py:1117
  306.0 1.3 slice.41
  307.3 1.5 fusion.1
  308.8 1.9 fusion
  310.7 2.3 copy.33
  312.9 2.3 copy.34
  315.2 1.9 copy.35
  317.1 1.9 copy.36
  (2 shorter events, 0.0 us)
